TPU v7x, 32 devices: a whole 2x2x4 slice. The times are simulated.
32 devices in a mesh: dp: 8 (over z, x), mp: 4 (over y, core).
Axes of the slice: x: 2, y: 2, z: 4, core: 2. Of those that a mesh axis runs over, the one named last changes fastest.
Arguments:
- inputs: bfloat16 [32, 1024, 512], P('dp', None, 'mp'), may hold values from -6 to 6
- cotangent: bfloat16 [32, 1024, 512], P('dp', None, 'mp'), may hold values from -6 to 6
- lengths: int32 [32], P('dp'), may hold values from 256 to 1024, as said below
- conv_master: float32 [9, 512, 512], P(None, 'dp', 'mp'), may hold values from -0.09375 to 0.09375
- hidden_master: float32 [512, 2048], P('dp', 'mp'), may hold values from -0.25 to 0.25
- output_master: float32 [2048, 512], P('mp', 'dp'), may hold values from -0.125 to 0.125
- conv_first: float32 [9, 512, 512], P(None, 'dp', 'mp'), may hold values from -0.00030517578 to 0.00030517578
- hidden_first: float32 [512, 2048], P('dp', 'mp'), may hold values from -0.00030517578 to 0.00030517578
- output_first: float32 [2048, 512], P('mp', 'dp'), may hold values from -0.00030517578 to 0.00030517578
- conv_second: float32 [9, 512, 512], P(None, 'dp', 'mp'), may hold values from 2.2413645e-10 to 8.965458e-10
- hidden_second: float32 [512, 2048], P('dp', 'mp'), may hold values from 2.2413645e-10 to 8.965458e-10
- output_second: float32 [2048, 512], P('mp', 'dp'), may hold values from 2.2413645e-10 to 8.965458e-10
- vectors: float32 [6, 512], replicated, may hold values from -0.6 to 6.5, as said below
- vector_first: float32 [6, 512], replicated, may hold values from -0.00024414062 to 0.00024414062
- vector_second: float32 [6, 512], replicated, may hold values from 1.1206822e-10 to 4.482729e-10
- hidden_bias: float32 [2048], P('mp'), may hold values from -3 to 3
- bias_first: float32 [2048], P('mp'), may hold values from -0.00010681152 to 0.00010681152
- bias_second: float32 [2048], P('mp'), may hold values from 2.2413644e-11 to 8.9654575e-11
Outputs:
- block_output: bfloat16 [32, 1024, 512], P('dp', None, 'mp')
- input_grad: float32 [32, 1024, 512], P('dp', None, 'mp')
- grad_norm: float32 [], replicated
- conv_weight_new: float32 [9, 512, 512], P(None, 'dp', 'mp')
- conv_first_new: float32 [9, 512, 512], P(None, 'dp', 'mp')
- conv_second_new: float32 [9, 512, 512], P(None, 'dp', 'mp')
- hidden_weight_new: float32 [512, 2048], P('dp', 'mp')
- hidden_first_new: float32 [512, 2048], P('dp', 'mp')
- hidden_second_new: float32 [512, 2048], P('dp', 'mp')
- output_weight_new: float32 [2048, 512], P('mp', 'dp')
- output_first_new: float32 [2048, 512], P('mp', 'dp')
- output_second_new: float32 [2048, 512], P('mp', 'dp')
- vectors_new: float32 [6, 512], replicated
- vector_first_new: float32 [6, 512], replicated
- vector_second_new: float32 [6, 512], replicated
- hidden_bias_new: float32 [2048], P('mp')
- bias_first_new: float32 [2048], P('mp')
- bias_second_new: float32 [2048], P('mp')
Inputs may be any that keep to these rules, and one draw needn't show every extreme that they name: `lengths`: each window's valid length is 256, 512 or 1024; the first window has 256 and the last 1024. `vectors`: gains are positive.
All inputs are finite; a program needn't handle non-finite values.
Results may differ from a plain program's by a relative error of at most 0.0095.
Values may be sent and summed in bfloat16 or wider, within the bound.
No kernel may reach another device: no remote copies, remote signals or barrier semaphores. Data moves between devices by JAX's collectives and lax.ppermute only.
A program may use at most 192 MiB of HBM per device.

v0:
```python
import jax
import jax.numpy as jnp
from jax import lax
from jax.sharding import PartitionSpec as P

KERNEL = 9
DILATION = 8
STEP = 10


NORM_EPS = 1e-05
BETA_ONE = 0.9
BETA_TWO = 0.999
ADAM_EPS = 1e-08
MATRIX_RATE = 0.03
VECTOR_RATE = 0.3
WEIGHT_DECAY = 0.01
CLIP_NORM = 1.0


def gelu_value(values):
    return jax.nn.gelu(values, approximate=False)


def gelu_slope(values):
    return (
        0.5 * (1.0 + jax.scipy.special.erf(values * 0.7071067811865476))
        + values * jnp.exp(-0.5 * values * values) * 0.3989422804014327
    )


def norm_parts(values):
    centre = values - jnp.mean(values, axis=-1, keepdims=True)
    inverse = lax.rsqrt(jnp.mean(centre * centre, axis=-1, keepdims=True) + NORM_EPS)
    return (centre * inverse, inverse)


def adam_step(weight, first_mom, second, gradient, clip_scale, step_rate, decay_rate):
    clipped = gradient * clip_scale
    first_new = BETA_ONE * first_mom + (1.0 - BETA_ONE) * clipped
    second_new = BETA_TWO * second + (1.0 - BETA_TWO) * clipped * clipped
    update_dir = (
        first_new
        / (1.0 - BETA_ONE**STEP)
        / (jnp.sqrt(second_new / (1.0 - BETA_TWO**STEP)) + ADAM_EPS)
    )
    return (weight - step_rate * (update_dir + decay_rate * weight), first_new, second_new)


def square_sum(values):
    return jnp.sum(values * values)


def make_mask(lengths, seq_length):
    positions = jnp.arange(seq_length, dtype=jnp.int32)
    return (positions[None, :] < lengths[:, None]).astype(jnp.float32)[:, :, None]


def per_device(
    inputs,
    cotangent,
    lengths,
    conv_master,
    hidden_master,
    output_master,
    conv_first,
    hidden_first,
    output_first,
    conv_second,
    hidden_second,
    output_second,
    vectors,
    vector_first,
    vector_second,
    hidden_bias,
    bias_first,
    bias_second,
):
    full_width = vectors.shape[1]
    own_width = inputs.shape[2]
    hidden_width = hidden_bias.shape[0]
    model_index = lax.axis_index("mp")
    window_count = inputs.shape[0]
    seq_length = inputs.shape[1]
    reach = DILATION * (KERNEL // 2)

    def own_columns(values):
        return lax.dynamic_slice_in_dim(values, model_index * own_width, own_width, values.ndim - 1)

    conv_weight, hidden_weight, output_weight = (
        lax.all_gather(conv_master.astype(jnp.bfloat16), "dp", axis=1, tiled=True),
        lax.all_gather(hidden_master.astype(jnp.bfloat16), "dp", axis=0, tiled=True),
        lax.all_gather(output_master.astype(jnp.bfloat16), "dp", axis=1, tiled=True),
    )
    row_mask = make_mask(lengths, seq_length)
    gain_one = vectors[0]
    shift_one = vectors[1]
    conv_bias = vectors[2]
    gain_two = vectors[3]
    shift_two = vectors[4]
    out_bias = vectors[5]
    upstream = cotangent.astype(jnp.float32)
    mix_grad = (row_mask * upstream).astype(jnp.bfloat16)
    whole_in_low, whole_mix_grad = (
        lax.all_gather(inputs, "mp", axis=2, tiled=True),
        lax.all_gather(mix_grad, "mp", axis=2, tiled=True),
    )
    whole_in = whole_in_low.astype(jnp.float32)
    scaled_one, inverse_one = norm_parts(whole_in)
    normed = (row_mask * (scaled_one * gain_one + shift_one)).astype(jnp.bfloat16)
    padded = jnp.pad(normed, ((0, 0), (reach, reach), (0, 0)))
    conv_out = jnp.zeros((window_count, seq_length, own_width), jnp.float32) + own_columns(
        conv_bias
    )
    for tap_index in range(KERNEL):
        window = lax.slice_in_dim(
            padded, tap_index * DILATION, tap_index * DILATION + seq_length, axis=1
        )
        conv_out = conv_out + jnp.einsum(
            "wpi,io->wpo", window, conv_weight[tap_index], preferred_element_type=jnp.float32
        )
    residual = inputs.astype(jnp.float32) + row_mask * gelu_value(conv_out)
    whole_res = lax.all_gather(residual, "mp", axis=2, tiled=True)
    scaled_two, inverse_two = norm_parts(whole_res)
    second = (scaled_two * gain_two + shift_two).astype(jnp.bfloat16)
    hidden = (
        jnp.einsum("wpi,if->wpf", second, hidden_weight, preferred_element_type=jnp.float32)
        + hidden_bias
    )
    active = gelu_value(hidden).astype(jnp.bfloat16)
    partial_mix = jnp.einsum(
        "wpf,fo->wpo", active, output_weight, preferred_element_type=jnp.float32
    )
    mixed_out = lax.psum_scatter(partial_mix, "mp", scatter_dimension=2, tiled=True)
    block_output = (residual + row_mask * (mixed_out + own_columns(out_bias))).astype(jnp.bfloat16)
    out_bias_grad = jnp.sum(mix_grad.astype(jnp.float32), axis=(0, 1))
    output_grad = jnp.einsum(
        "wpf,wpo->fo", active, whole_mix_grad, preferred_element_type=jnp.float32
    )
    active_grad = jnp.einsum(
        "wpo,fo->wpf", whole_mix_grad, output_weight, preferred_element_type=jnp.float32
    )
    hidden_grad = (active_grad * gelu_slope(hidden)).astype(jnp.bfloat16)
    hidden_bias_grad = jnp.sum(hidden_grad.astype(jnp.float32), axis=(0, 1))
    hidden_w_grad = jnp.einsum(
        "wpi,wpf->if", second, hidden_grad, preferred_element_type=jnp.float32
    )
    second_part = jnp.einsum(
        "wpf,if->wpi", hidden_grad, hidden_weight, preferred_element_type=jnp.float32
    )
    second_grad = lax.psum_scatter(second_part, "mp", scatter_dimension=2, tiled=True)
    own_scaled_two = own_columns(scaled_two)
    gain_two_grad = jnp.sum(second_grad * own_scaled_two, axis=(0, 1))
    shift_two_grad = jnp.sum(second_grad, axis=(0, 1))
    scaled_grad_two = second_grad * own_columns(gain_two)
    plain_two, cross_two = (
        lax.psum(
            jnp.sum(scaled_grad_two, axis=-1, keepdims=True).astype(jnp.bfloat16), "mp"
        ).astype(jnp.float32),
        lax.psum(
            jnp.sum(scaled_grad_two * own_scaled_two, axis=-1, keepdims=True).astype(jnp.bfloat16),
            "mp",
        ).astype(jnp.float32),
    )
    resid_grad = upstream + inverse_two * (
        scaled_grad_two - plain_two / full_width - own_scaled_two * cross_two / full_width
    )
    conv_grad = (row_mask * resid_grad * gelu_slope(conv_out)).astype(jnp.bfloat16)
    conv_bias_grad = jnp.sum(conv_grad.astype(jnp.float32), axis=(0, 1))
    padded_grad = jnp.pad(conv_grad, ((0, 0), (reach, reach), (0, 0)))
    normed_part = jnp.zeros((window_count, seq_length, full_width), jnp.float32)
    tap_grads = []
    for tap_index in range(KERNEL):
        window = lax.slice_in_dim(
            padded, tap_index * DILATION, tap_index * DILATION + seq_length, axis=1
        )
        tap_grads.append(
            jnp.einsum("wpi,wpo->io", window, conv_grad, preferred_element_type=jnp.float32)
        )
        back_start = 2 * reach - tap_index * DILATION
        shifted = lax.slice_in_dim(padded_grad, back_start, back_start + seq_length, axis=1)
        normed_part = normed_part + jnp.einsum(
            "wpo,io->wpi", shifted, conv_weight[tap_index], preferred_element_type=jnp.float32
        )
    conv_w_grad = jnp.stack(tap_grads)
    normed_grad = lax.psum_scatter(
        normed_part.astype(jnp.bfloat16), "mp", scatter_dimension=2, tiled=True
    ).astype(jnp.float32)
    first_grad = row_mask * normed_grad
    own_scaled_one = own_columns(scaled_one)
    gain_one_grad = jnp.sum(first_grad * own_scaled_one, axis=(0, 1))
    shift_one_grad = jnp.sum(first_grad, axis=(0, 1))
    scaled_grad_one = first_grad * own_columns(gain_one)
    plain_one, cross_one = (
        lax.psum(
            jnp.sum(scaled_grad_one, axis=-1, keepdims=True).astype(jnp.bfloat16), "mp"
        ).astype(jnp.float32),
        lax.psum(
            jnp.sum(scaled_grad_one * own_scaled_one, axis=-1, keepdims=True).astype(jnp.bfloat16),
            "mp",
        ).astype(jnp.float32),
    )
    input_grad = resid_grad + inverse_one * (
        scaled_grad_one - plain_one / full_width - own_scaled_one * cross_one / full_width
    )
    vector_part = jnp.stack(
        [
            gain_one_grad,
            shift_one_grad,
            conv_bias_grad,
            gain_two_grad,
            shift_two_grad,
            out_bias_grad,
        ]
    )
    vector_padded = lax.dynamic_update_slice_in_dim(
        jnp.zeros((6, full_width), jnp.float32), vector_part, model_index * own_width, 1
    )
    conv_share, hidden_share, output_share = (
        lax.psum_scatter(conv_w_grad, "dp", scatter_dimension=1, tiled=True),
        lax.psum_scatter(hidden_w_grad, "dp", scatter_dimension=0, tiled=True),
        lax.psum_scatter(output_grad, "dp", scatter_dimension=1, tiled=True),
    )
    big_squares = square_sum(conv_share) + square_sum(hidden_share) + square_sum(output_share)
    bias_padded = lax.dynamic_update_slice_in_dim(
        jnp.zeros((hidden_width * lax.axis_size("mp"),), jnp.float32),
        hidden_bias_grad,
        model_index * hidden_width,
        0,
    )
    vector_sum, bias_sum, squares_all = lax.psum(
        (vector_padded, bias_padded, big_squares), ("dp", "mp")
    )
    total_sq = squares_all + square_sum(vector_sum) + square_sum(bias_sum)
    bias_share = lax.dynamic_slice_in_dim(bias_sum, model_index * hidden_width, hidden_width, 0)
    grad_norm = jnp.sqrt(total_sq)
    clip_scale = jnp.minimum(1.0, CLIP_NORM / (grad_norm + 1e-06))
    conv_new = adam_step(
        conv_master, conv_first, conv_second, conv_share, clip_scale, MATRIX_RATE, WEIGHT_DECAY
    )
    hidden_new = adam_step(
        hidden_master,
        hidden_first,
        hidden_second,
        hidden_share,
        clip_scale,
        MATRIX_RATE,
        WEIGHT_DECAY,
    )
    output_new = adam_step(
        output_master,
        output_first,
        output_second,
        output_share,
        clip_scale,
        MATRIX_RATE,
        WEIGHT_DECAY,
    )
    vector_new = adam_step(
        vectors, vector_first, vector_second, vector_sum, clip_scale, VECTOR_RATE, 0.0
    )
    bias_new = adam_step(
        hidden_bias, bias_first, bias_second, bias_share, clip_scale, VECTOR_RATE, 0.0
    )
    return (
        block_output,
        input_grad,
        grad_norm,
        conv_new[0],
        conv_new[1],
        conv_new[2],
        hidden_new[0],
        hidden_new[1],
        hidden_new[2],
        output_new[0],
        output_new[1],
        output_new[2],
        vector_new[0],
        vector_new[1],
        vector_new[2],
        bias_new[0],
        bias_new[1],
        bias_new[2],
    )


def solution(mesh):
    placed = (
        P("dp", None, "mp"),
        P("dp", None, "mp"),
        P("dp"),
        P(None, "dp", "mp"),
        P("dp", "mp"),
        P("mp", "dp"),
        P(None, "dp", "mp"),
        P("dp", "mp"),
        P("mp", "dp"),
        P(None, "dp", "mp"),
        P("dp", "mp"),
        P("mp", "dp"),
        P(),
        P(),
        P(),
        P("mp"),
        P("mp"),
        P("mp"),
    )
    return jax.shard_map(
        per_device,
        mesh=mesh,
        in_specs=placed,
        out_specs=(
            P("dp", None, "mp"),
            P("dp", None, "mp"),
            P(),
            P(None, "dp", "mp"),
            P(None, "dp", "mp"),
            P(None, "dp", "mp"),
            P("dp", "mp"),
            P("dp", "mp"),
            P("dp", "mp"),
            P("mp", "dp"),
            P("mp", "dp"),
            P("mp", "dp"),
            P(),
            P(),
            P(),
            P("mp"),
            P("mp"),
            P("mp"),
        ),
        check_vma=False,
    )
```

profile of v0, /device:TPU:0, one launch (start us, length us, event | category | flops | bytes accessed | tf_op | source)
XLA Modules:
  0.0 646.8 jit_solution(6764629995446909580)
XLA Ops:
  12.0 35.4 %all-gather.5.cloned.1.call-done = bf16[4,1024,512]{2,1,0:T(8,128)(2,1)} async-done(((bf16[4,1024,128]{2,1,0:T(8,128)(2,1)}), bf16[4,1024,512]{2,1,0:T(8,128)(2,1)}) %all-gather.5.cloned.1.call-update) | async-done | bytes 4194320 | tf_op jit(solution)/shard_map/all_gather | solution.py:105
  53.0 5.4 fusion
  58.4 32.8 %all-gather.7.cloned.1.call-done = bf16[9,512,128]{2,1,0:T(8,128)(2,1)} async-done(((bf16[9,64,128]{2,1,0:T(8,128)(2,1)}), bf16[9,512,128]{2,1,0:T(8,128)(2,1)}) %all-gather.7.cloned.1.call-update) | async-done | bytes 1179664 | tf_op jit(solution)/shard_map/all_gather | solution.py:91
  106.7 10.0 %convert_reduce_fusion.2 = (f32[128]{0:T(128)S(1)}, bf16[4,1024,128]{2,1,0:T(8,128)(2,1)}, f32[4,1024,128]{2,1,0:T(8,128)}, f32[4,1024,128]{2,1,0:T(8,128)}) fusion(bf16[4,1024,128]{2,1,0:T(8,128)(2,1)S(1)} %copy-done.8, f32[4,1024]{1,0:T(4,128)S(1)} %fusion.160, bf16[4,1024,128]{2,1,0:T(8,128)(2,1)S(1)} %copy-done.14, f32[4,1024,128]{2,1,0:T(8,128)} %fusion.20, ...), kind=kOutput, calls=%fused_computation.87 | convolution fusion | flops 579338112 | bytes 28460032 | tf_op jit(solution)/shard_map/wpi,io->wpo/dot_general | solution.py:119
  117.4 31.3 %all_gather.22 = bf16[512,512]{0,1:T(8,128)(2,1)S(1)} all-gather(bf16[512,64]{0,1:T(8,128)(2,1)S(1)} %convert_element_type.137), channel_id=1, replica_groups=mesh['dp'=8,'mp'=4] {'dp'}, dimensions={1}, use_global_device_ids=true | all-gather | bytes 589824 | tf_op jit(solution)/shard_map/all_gather | solution.py:93
  148.7 31.3 %all_gather.21 = bf16[512,512]{1,0:T(8,128)(2,1)S(1)} all-gather(bf16[64,512]{1,0:T(8,128)(2,1)S(1)} %convert_element_type.135), channel_id=1, replica_groups=mesh['dp'=8,'mp'=4] {'dp'}, dimensions={0}, use_global_device_ids=true | all-gather | bytes 589824 | tf_op jit(solution)/shard_map/all_gather | solution.py:92
  184.3 4.9 multiply_reduce_fusion
  195.5 7.4 %fusion.72 = (u8[1024,512]{1,0:T(8,128)(4,1)S(1)}, u8[1024,512]{1,0:T(8,128)(4,1)S(1)}, f32[4,1024,512]{2,1,0:T(8,128)}) fusion(f32[512]{0:T(512)S(1)} %copy-done.21, bf16[512,512]{1,0:T(8,128)(2,1)S(1)} %all_gather.21, f32[4,1024,512]{2,1,0:T(8,128)S(1)} %subtract_multiply_fusion, f32[512]{0:T(512)S(1)} %bitcast.165, f32[512]{0:T(512)S(1)} %bitcast.167), kind=kOutput, calls=%fused_computation.116 | convolution fusion | flops 2182086656 | bytes 18356224 | tf_op jit(solution)/shard_map/wpi,if->wpf/dot_general | solution.py:127
  202.9 9.1 %all-gather.11.cloned.1.call-done = bf16[4,1024,512]{2,1,0:T(8,128)(2,1)} async-done(((bf16[4,1024,128]{2,1,0:T(8,128)(2,1)}), bf16[4,1024,512]{2,1,0:T(8,128)(2,1)}) %all-gather.11.cloned.1.call-update) | async-done | bytes 4194320 | tf_op jit(solution)/shard_map/all_gather | solution.py:106
  212.1 8.2 %convert_reduce_fusion.1 = (f32[512]{0:T(512)S(1)}, bf16[4,1024,512]{2,1,0:T(8,128)(2,1)S(1)}) fusion(f32[4,1024,512]{2,1,0:T(8,128)} %get-tuple-element.66, f32[512]{0:T(512)S(1)} %copy-done.21, bf16[4,1024,512]{2,1,0:T(8,128)(2,1)} %all-gather.11.cloned.1.call-done, bf16[512,512]{0,1:T(8,128)(2,1)S(1)} %all_gather.22), kind=kOutput, calls=%fused_computation.21 | convolution fusion | flops 2174746112 | bytes 17305600 | tf_op jit(solution)/shard_map/wpo,fo->wpf/dot_general | solution.py:140
  222.2 5.8 fusion.143
  228.1 21.1 %fusion.5 = bf16[4,1024,512]{2,1,0:T(8,128)(2,1)S(1)} fusion(f32[4,1024,512]{2,1,0:T(8,128)} %get-tuple-element.66, f32[512]{0:T(512)S(1)} %copy-done.21, u8[1024,512]{1,0:T(8,128)(4,1)S(1)} %get-tuple-element.23, u8[1024,512]{1,0:T(8,128)(4,1)S(1)} %get-tuple-element.22), kind=kLoop, calls=%fused_computation.9 | loop fusion | flops 148897792 | bytes 13633536 | tf_op jit(solution)/shard_map/convert_element_type | solution.py:130
  254.6 7.9 %convolution_bitcast_fusion.1 = f32[512,512]{1,0:T(8,128)} fusion(bf16[4,1024,512]{2,1,0:T(8,128)(2,1)} %copy-done.6, f32[4,1024,512]{2,1,0:T(8,128)} %copy-done.1, f32[512]{0:T(512)S(1)} %bitcast.166, f32[512]{0:T(512)S(1)} %bitcast.168), kind=kOutput, calls=%fused_computation.119 | convolution fusion | flops 2153775104 | bytes 13635584 | tf_op jit(solution)/shard_map/wpi,wpf->if/dot_general | solution.py:145
  262.6 37.3 %reduce-scatter.11.cloned.1.call-done = f32[4,1024,128]{2,1,0:T(8,128)} async-done(((f32[4,1024,512]{2,1,0:T(8,128)}), f32[4,1024,128]{2,1,0:T(8,128)}) %reduce-scatter.11.cloned.1.call-update) | async-done | bytes 2097168 | tf_op jit(solution)/shard_map/reduce_scatter | solution.py:151
  303.5 10.2 %all-reduce.4 = (bf16[4,1024]{1,0:T(4,128)(2,1)S(1)}, bf16[4,1024,1]{1,0,2:T(4,128)(2,1)S(1)}) all-reduce(bf16[4,1024]{1,0:T(4,128)(2,1)S(1)} %get-tuple-element.19, bf16[4,1024,1]{1,0,2:T(4,128)(2,1)S(1)} %bitcast.164), channel_id=1, replica_groups=mesh['dp'=8,'mp'=4] {'mp'}, use_global_device_ids=true, to_apply=%region_9.10 | all-reduce | flops 8192 | bytes 32768 | tf_op jit(solution)/shard_map/psum | solution.py:160
  313.7 6.6 %convert_reduce_fusion.3 = (f32[128]{0:T(128)S(1)}, bf16[4,1024,128]{2,1,0:T(8,128)(2,1)S(1)}) fusion(f32[4,1024,128]{2,1,0:T(8,128)} %get-tuple-element.65, f32[4,1024]{1,0:T(4,128)S(1)} %mul.518, f32[4,1024,512]{2,1,0:T(8,128)} %copy-done.1, s32[]{:T(128)S(6)} %select_n.4, f32[4,1024]{1,0:T(4,128)S(1)} %multiply_bitcast_fusion.1, ...), kind=kLoop, calls=%fused_computation.89 | loop fusion | flops 11009920 | bytes 8455172 | tf_op jit(solution)/shard_map/reduce_sum | solution.py:169
  338.6 5.5 fusion.134
  344.1 4.5 fusion.132
  348.5 4.5 fusion.130
  357.4 4.5 fusion.126
  361.9 4.5 fusion.136
  370.9 4.5 fusion.157
  375.3 24.3 %add_convert_fusion = bf16[4,1024,512]{2,1,0:T(8,128)(2,1)} fusion(f32[4,1024,512]{2,1,0:T(8,128)} %fusion.126, f32[4,1024,512]{2,1,0:T(8,128)} %fusion.128, f32[4,1024,512]{2,1,0:T(8,128)} %fusion.130, f32[4,1024,512]{2,1,0:T(8,128)} %fusion.157, f32[4,1024,512]{2,1,0:T(8,128)} %fusion.132, f32[4,1024,512]{2,1,0:T(8,128)} %fusion.134, ...), kind=kOutput, calls=%fused_computation.22 | convolution fusion | flops 555745280 | bytes 72482816 | tf_op jit(solution)/shard_map/wpo,io->wpi/dot_general | solution.py:182
  399.6 8.1 %copy.69 = bf16[4,1024,512]{1,0,2:T(4,128)(2,1)} copy(bf16[4,1024,512]{2,1,0:T(8,128)(2,1)} %add_convert_fusion) | data formatting | bytes 8388608
  407.7 6.5 %copy.71 = bf16[64,8,4,1024]{3,1,2,0:T(8,128)(2,1)} copy(bf16[64,8,4,1024]{3,2,1,0:T(4,128)(2,1)} %bitcast.161) | data formatting | bytes 8388608
  415.2 7.8 %fusion.141 = f32[4,1024,512]{2,1,0:T(8,128)} fusion(bf16[4,1024,512]{2,1,0:T(8,128)(2,1)} %copy-done.7, bf16[512,512]{0,1:T(8,128)(2,1)S(1)} %copy-done.10), kind=kOutput, calls=%fused_computation.155 | convolution fusion | flops 2147483648 | bytes 13107200 | tf_op jit(solution)/shard_map/wpf,fo->wpo/dot_general | solution.py:131
  425.4 8.0 %reduce-scatter.15.cloned.1.call-done = f32[64,512]{1,0:T(8,128)} async-done(((f32[512,512]{1,0:T(8,128)}), f32[64,512]{1,0:T(8,128)}) %reduce-scatter.15.cloned.1.call-update) | async-done | bytes 131088 | tf_op jit(solution)/shard_map/reduce_scatter | solution.py:221
  434.9 71.4 %reduce-scatter.13.cloned.1.call-done = f32[9,64,128]{2,1,0:T(8,128)} async-done(((f32[9,512,128]{2,1,0:T(8,128)}), f32[9,64,128]{2,1,0:T(8,128)}) %reduce-scatter.13.cloned.1.call-update) | async-done | bytes 294928 | tf_op jit(solution)/shard_map/reduce_scatter | solution.py:220
  510.0 42.7 %reduce-scatter.19.cloned.1.call-done = bf16[128,4096]{1,0:T(8,128)(2,1)} async-done(((bf16[512,4096]{1,0:T(8,128)(2,1)}), bf16[128,4096]{1,0:T(8,128)(2,1)}) %reduce-scatter.19.cloned.1.call-update) | async-done | bytes 1048592
  562.3 40.2 %all-reduce.2 = (f32[]{:T(128)}, f32[6,512]{1,0:T(8,128)S(1)}, f32[2048]{0:T(1024)}) all-reduce(f32[]{:T(128)S(6)} %add.311, f32[6,512]{1,0:T(8,128)S(1)} %constant_dynamic-update-slice_fusion, f32[2048]{0:T(1024)} %copy-done.20), channel_id=1, replica_groups=mesh['dp'=8,'mp'=4] {'dp','mp'}, use_global_device_ids=true, to_apply=%region_21.22 | all-reduce | flops 5121 | bytes 40968 | tf_op jit(solution)/shard_map/psum | solution.py:231
  606.5 13.2 %all-reduce.3 = (bf16[4,1024]{1,0:T(4,128)(2,1)S(1)}, bf16[4,1024,1]{1,0,2:T(4,128)(2,1)}) all-reduce(bf16[4,1024]{1,0:T(4,128)(2,1)} %get-tuple-element.21, bf16[4,1024,1]{1,0,2:T(4,128)(2,1)} %bitcast.163), channel_id=1, replica_groups=mesh['dp'=8,'mp'=4] {'mp'}, use_global_device_ids=true, to_apply=%region_14.15 | all-reduce | flops 8192 | bytes 32768 | tf_op jit(solution)/shard_map/psum | solution.py:198
  629.2 9.2 %multiply_add_fusion = (f32[4,1024,128]{2,1,0:T(8,128)}, bf16[4,1024,128]{2,1,0:T(8,128)(2,1)}) fusion(bf16[4,1024,128]{2,1,0:T(8,128)(2,1)S(1)} %copy.70, f32[4,1024,512]{2,1,0:T(8,128)} %get-tuple-element.54, s32[]{:T(128)S(6)} %select_n.4, f32[4,1024]{1,0:T(4,128)S(1)} %mul.539, f32[4,1024]{1,0:T(4,128)S(1)} %multiply_bitcast_fusion, f32[128]{0:T(128)} %copy-done.24, ...), kind=kLoop, calls=%fused_computation.91 | loop fusion | flops 11010048 | bytes 15844868 | tf_op jit(solution)/shard_map/add | solution.py:203
  (135 shorter events, 102.9 us)
Async XLA Ops:
  7.2 40.1 %all-gather.5.cloned.1.call-start = ((), (), s32[]{:S(2)}) async-start(), calls=%async_computation.6 | async-start | bytes 5242880 | tf_op jit(solution)/shard_map/all_gather | solution.py:105
  7.9 83.3 %all-gather.7.cloned.1.call-start = ((), (), s32[]{:S(2)}) async-start(), calls=%async_computation.7 | async-start | bytes 1327104 | tf_op jit(solution)/shard_map/all_gather | solution.py:91
  9.6 170.4 %all-gather.9.cloned.1.call-start = ((), (), s32[]{:S(2)}) async-start(), calls=%async_computation.8 | async-start | bytes 10485760 | tf_op jit(solution)/shard_map/all_gather | solution.py:123
  11.2 41.2 %copy-start.22 = (f32[1,512]{1,0:T(1,128)}, f32[1,512]{1,0:T(1,128)S(1)}, u32[]{:S(2)}) copy-start(f32[1,512]{1,0:T(1,128)S(1)} %get-tuple-element.63) | copy-start | bytes 6148
  47.3 3.4 copy-start.4
  91.2 3.6 copy-start.2
  91.2 3.8 copy-start.11
  106.7 10.6 %copy-start.16 = (f32[64,512]{1,0:T(8,128)S(1)}, f32[64,512]{1,0:T(8,128)}, u32[]{:S(2)}) copy-start(f32[64,512]{1,0:T(8,128)} %param.22) | copy-start | bytes 393220
  106.7 10.7 %copy-start.15 = (f32[512,64]{0,1:T(8,128)S(1)}, f32[512,64]{0,1:T(8,128)}, u32[]{:S(2)}) copy-start(f32[512,64]{0,1:T(8,128)} %param.23) | copy-start | bytes 393220
  116.7 95.4 %all-gather.11.cloned.1.call-start = ((), (), s32[]{:S(2)}) async-start(), calls=%async_computation.10 | async-start | bytes 5242880 | tf_op jit(solution)/shard_map/all_gather | solution.py:106
  117.3 182.6 %reduce-scatter.11.cloned.1.call-start = ((), (), s32[]{:S(2)}) async-start(), calls=%async_computation.11 | async-start | bytes 10485760 | tf_op jit(solution)/shard_map/reduce_scatter | solution.py:151
  148.7 63.4 %copy-start.9 = (bf16[512,512]{0,1:T(8,128)(2,1)}, bf16[512,512]{0,1:T(8,128)(2,1)S(1)}, u32[]{:S(2)}) copy-start(bf16[512,512]{0,1:T(8,128)(2,1)S(1)} %all_gather.22) | copy-start | bytes 1572868
  184.2 6.6 %copy-start = (f32[4,1024,512]{2,1,0:T(8,128)S(1)}, f32[4,1024,512]{2,1,0:T(8,128)}, u32[]{:S(2)}) copy-start(f32[4,1024,512]{2,1,0:T(8,128)} %all-gather.9.cloned.1.call-done) | copy-start | bytes 25165828
  190.9 4.6 copy-start.21
  192.3 3.2 copy-start.1
  220.3 1.9 copy-start.6
  228.0 195.8 %reduce-scatter.17.cloned.1.call-start = ((), (), s32[]{:S(2)}) async-start(), calls=%async_computation.14 | async-start | bytes 1179648 | tf_op jit(solution)/shard_map/reduce_scatter | solution.py:222
  228.1 23.1 %copy-start.25 = (bf16[4,1024,512]{2,1,0:T(8,128)(2,1)S(1)}, bf16[4,1024,512]{2,1,0:T(8,128)(2,1)}, u32[]{:S(2)}) copy-start(bf16[4,1024,512]{2,1,0:T(8,128)(2,1)} %all-gather.11.cloned.1.call-done) | copy-start | bytes 12582916
  249.2 2.0 copy-start.7
  254.6 178.8 %reduce-scatter.15.cloned.1.call-start = ((), (), s32[]{:S(2)}) async-start(), calls=%async_computation.13 | async-start | bytes 1179648 | tf_op jit(solution)/shard_map/reduce_scatter | solution.py:221
  254.6 59.0 %copy-start.23 = (f32[128]{0:T(128)}, f32[128]{0:T(128)S(1)}, u32[]{:S(2)}) copy-start(f32[128]{0:T(128)S(1)} %fusion.164) | copy-start | bytes 1540
  262.6 243.8 %reduce-scatter.13.cloned.1.call-start = ((), (), s32[]{:S(2)}) async-start(), calls=%async_computation.12 | async-start | bytes 2654208 | tf_op jit(solution)/shard_map/reduce_scatter | solution.py:220
  299.9 13.8 %copy-start.5 = (f32[4,1024,128]{2,1,0:T(8,128)S(1)}, f32[4,1024,128]{2,1,0:T(8,128)}, u32[]{:S(2)}) copy-start(f32[4,1024,128]{2,1,0:T(8,128)} %reduce-scatter.11.cloned.1.call-done) | copy-start | bytes 6291460
  313.7 6.6 %copy-start.3 = (bf16[4,1024,512]{2,1,0:T(8,128)(2,1)S(1)}, bf16[4,1024,512]{2,1,0:T(8,128)(2,1)}, u32[]{:S(2)}) copy-start(bf16[4,1024,512]{2,1,0:T(8,128)(2,1)} %get-tuple-element.55) | copy-start | bytes 12582916
  338.3 214.4 %reduce-scatter.19.cloned.1.call-start = ((), (), s32[]{:S(2)}) async-start(), calls=%async_computation.15 | async-start | bytes 5242880
  338.6 5.5 copy-start.12
  414.2 215.0 %reduce-scatter.9.cloned.1.call-start = ((), (), s32[]{:S(2)}) async-start(), calls=%async_computation.9 | async-start | bytes 10485760 | tf_op jit(solution)/shard_map/reduce_scatter | solution.py:134
  423.7 137.3 %copy-start.24 = (f32[128]{0:T(128)}, f32[128]{0:T(128)S(1)}, u32[]{:S(2)}) copy-start(f32[128]{0:T(128)S(1)} %fusion.165) | copy-start | bytes 1540
  423.9 128.8 %copy-start.20 = (f32[2048]{0:T(1024)}, f32[2048]{0:T(1024)S(1)}, u32[]{:S(2)}) copy-start(f32[2048]{0:T(1024)S(1)} %dynamic_update_slice.7) | copy-start | bytes 24580
  555.3 71.6 %copy-start.13 = (f32[9,64,128]{2,1,0:T(8,128)S(1)}, f32[9,64,128]{2,1,0:T(8,128)}, u32[]{:S(2)}) copy-start(f32[9,64,128]{2,1,0:T(8,128)} %param.21) | copy-start | bytes 884740
  557.3 71.9 %copy-start.18 = (f32[4,1024]{1,0:T(4,128)S(1)}, f32[4,1024]{1,0:T(4,128)}, u32[]{:S(2)}) copy-start(f32[4,1024]{1,0:T(4,128)} %copy-done.17) | copy-start | bytes 49156
  602.5 17.1 %copy-start.19 = (f32[6,512]{1,0:T(8,128)}, f32[6,512]{1,0:T(8,128)S(1)}, u32[]{:S(2)}) copy-start(f32[6,512]{1,0:T(8,128)S(1)} %get-tuple-element.29) | copy-start | bytes 36868
  (4 other events, 4.4 us)
Sparse Core Ops, SparseCore 0:
  9.6 37.7 all-gather.4
  50.1 41.0 all-gather.6
  116.8 58.1 all-gather.8
  177.0 35.0 all-gather.10
  228.2 71.6 reduce-scatter.10
  303.5 63.3 reduce-scatter.16
  370.9 62.4 reduce-scatter.14
  437.3 69.0 reduce-scatter.12
  509.1 43.5 reduce-scatter.18
  555.1 72.6 reduce-scatter.8
where the time goes:
time: 657 us; the launch traced here: 647 us
  waiting for transfers between devices  238 us (36%)
  matrix products  144 us (22%)
  blocking collectives  126 us (19%)
  other arithmetic  83.3 us (13%)
  local copies, waits for them, and re-layouts  34.2 us (5%)
  between operations  20.1 us (3%)
    reduce_scatter x1, waiting for transfers between devices, per_device(): lax.psum_scatter(conv_w_grad, 'dp', scatter_dimension=1, tiled=True)  71.4 us
    dot_general x9, matrix products, per_device(): jnp.einsum('wpo,io->wpi', shifted, conv_weight[tap_index], preferred_elem...  61 us
    unnamed x11, waiting for transfers between devices  44 us
    psum x1, blocking collectives, per_device(): lax.psum((vector_padded, bias_padded, big_squares), ('dp', 'mp'))  40.2 us
    reduce_scatter x1, waiting for transfers between devices, per_device(): lax.psum_scatter(second_part, 'mp', scatter_dimension=2, tiled=True)  37.3 us
    all_gather x1, waiting for transfers between devices, per_device(): lax.all_gather(inputs, 'mp', axis=2, tiled=True)  35.4 us
    all_gather x1, waiting for transfers between devices, per_device(): lax.all_gather(conv_master.astype(jnp.bfloat16), 'dp', axis=1, tiled=True)  32.8 us
    all_gather x1, blocking collectives, per_device(): lax.all_gather(hidden_master.astype(jnp.bfloat16), 'dp', axis=0, tiled=True)  31.3 us
  transfers between devices with their start and end apart: 10, of which 7 were waited for; matrix products, arithmetic and copies ran while one was open for 31% of the time, Pallas kernels for 0%

commit v1 on v0

v1 whole, which is shorter than its diff:
```python
import functools

import jax
import jax.numpy as jnp
from jax import lax
from jax.experimental import pallas as pl
from jax.experimental.pallas import tpu as pltpu
from jax.sharding import PartitionSpec as P

KERNEL = 9
DILATION = 8
REACH = DILATION * (KERNEL // 2)
STEP = 10
ROWS = 256

NORM_EPS = 1e-05
BETA_ONE = 0.9
BETA_TWO = 0.999
ADAM_EPS = 1e-08
MATRIX_RATE = 0.03
VECTOR_RATE = 0.3
WEIGHT_DECAY = 0.01
CLIP_NORM = 1.0

f32 = jnp.float32
bf16 = jnp.bfloat16
NN = (((1,), (0,)), ((), ()))
NT = (((1,), (1,)), ((), ()))


def dot(a, b, dims=NN):
    return lax.dot_general(a, b, dims, preferred_element_type=f32)


def phi_of(v):
    return 0.5 * (1.0 + lax.erf(v * 0.7071067811865476))


def slope_of(v, phi):
    return phi + v * jnp.exp(-0.5 * v * v) * 0.3989422804014327


def norm_parts(v):
    centre = v - jnp.mean(v, axis=-1, keepdims=True)
    inverse = lax.rsqrt(jnp.mean(centre * centre, axis=-1, keepdims=True) + NORM_EPS)
    return centre * inverse, inverse


def norm_back(e, s, inverse):
    return inverse * (
        e - jnp.mean(e, axis=-1, keepdims=True) - s * jnp.mean(e * s, axis=-1, keepdims=True)
    )


def mult(v, n):
    return pl.multiple_of(v, n)


def dest_slot(place, d, m):
    dp, mp = place[0], place[1]
    fx = (dp & 1) ^ (d & 1)
    fy = (mp >> 1) ^ (m >> 1)
    dz = (dp >> 1) ^ (d >> 1)
    dc = (mp & 1) ^ (m & 1)
    flip = m & 1
    a = jnp.where(flip == 0, fx, fy)
    b = jnp.where(flip == 0, fy, fx)
    return dc, b, a, dz


def source_of(place, dc, b, a, dz):
    dp, mp = place[0], place[1]
    flip = (mp & 1) ^ dc
    fx = jnp.where(flip == 0, a, b)
    fy = jnp.where(flip == 0, b, a)
    d = ((dp >> 1) ^ dz) * 2 + ((dp & 1) ^ fx)
    m = ((mp >> 1) ^ fy) * 2 + ((mp & 1) ^ dc)
    return d, m


SLOTS = tuple((dc, b, a) for dc in (0, 1) for b, a in ((0, 0), (0, 1), (1, 0), (1, 1)))


def conv_forward(place, x0, x1, x2, x3, vec, *rest):
    pieces, (w_out, x_out, na_out, conv_out, nf, nab) = rest[:8], rest[8:]
    taps, di, own = pieces[0].shape[1:]
    full = vec.shape[1]
    length = place[2]
    blocks = place[3]

    def place_z(z, _):
        for (dc, b, a), piece in zip(SLOTS, pieces):
            d, m = source_of(place, dc, b, a, z)
            col = mult(m * own, own)
            for t in range(taps):
                row = mult(t * full + d * di, di)
                w_out[pl.ds(row, di), pl.ds(col, own)] = piece[z, t]
        return 0

    lax.fori_loop(0, pieces[0].shape[0], place_z, 0)
    for k, xk in enumerate((x0, x1, x2, x3)):
        x_out[:, pl.ds(mult((place[1] ^ k) * own, own), own)] = xk[...]

    nf[...] = jnp.zeros_like(nf)
    na_out[...] = jnp.zeros_like(na_out)
    conv_out[...] = jnp.zeros_like(conv_out)
    gain = vec[0:1, :]
    shift = vec[1:2, :]

    def norm_step(i, _):
        rows = pl.ds(mult(i * 128, 128), 128)
        scaled, _ = norm_parts(x_out[rows, :].astype(f32))
        nf[pl.ds(mult(i * 128 + REACH, 8), 128), :] = scaled * gain + shift
        return 0

    lax.fori_loop(0, blocks * (ROWS // 128), norm_step, 0)
    padded = nab.shape[1]

    def shift_step(i, _):
        row = mult(i * 64, 64)
        nab[0, pl.ds(row, 64), :] = nf[pl.ds(row, 64), :].astype(bf16)
        nab[1, pl.ds(row, 64), :] = nf[pl.ds(mult(row + 8, 8), 64), :].astype(bf16)
        return 0

    lax.fori_loop(0, padded // 64, shift_step, 0)

    def conv_step(i, _):
        row = mult(i * ROWS, ROWS)
        na_out[pl.ds(row, ROWS), :] = nab[0, pl.ds(mult(row + REACH, 32), ROWS), :]
        window = jnp.concatenate(
            [
                nab[t & 1, pl.ds(mult(row + DILATION * (t - (t & 1)), 16), ROWS), :]
                for t in range(KERNEL)
            ],
            axis=1,
        )
        conv_out[pl.ds(row, ROWS), :] = dot(window, w_out[...]) + vec[2:3, :]
        return 0

    lax.fori_loop(0, blocks, conv_step, 0)


def ffn(place, x_full, conv_out, c0, c1, c2, c3, vec, hbias, *rest):
    pieces = rest[:8]
    block_out, resid_out, cg_out, rsb, vgrad, hbgrad = rest[8:14]
    wh, wo, cot, act, hg, sec, mg = rest[14:]
    seq, full = x_full.shape
    hidden = wh.shape[1]
    di, part = pieces[0].shape[2:]
    own = c0.shape[1]
    blocks = place[3]

    def place_z(z, _):
        for (dc, b, a), piece in zip(SLOTS, pieces):
            d, m = source_of(place, dc, b, a, z)
            row = mult(d * di, di)
            col = mult(m * part, part)
            wh[pl.ds(row, di), pl.ds(col, part)] = piece[z, 0]
            wo[pl.ds(row, di), pl.ds(col, part)] = piece[z, 1]
        return 0

    lax.fori_loop(0, pieces[0].shape[0], place_z, 0)
    for k, ck in enumerate((c0, c1, c2, c3)):
        cot[:, pl.ds(mult((place[1] ^ k) * own, own), own)] = ck[...]
    vgrad[...] = jnp.zeros_like(vgrad)
    hbgrad[...] = jnp.zeros_like(hbgrad)

    def out_store(rows, values):
        for m in range(full // own):
            block_out[place[1] ^ m, rows, :] = values[:, m * own : (m + 1) * own]

    def row_step(i, _):
        rows = pl.ds(mult(i * ROWS, ROWS), ROWS)
        conv = conv_out[rows, :]
        residual = x_full[rows, :].astype(f32) + conv * phi_of(conv)
        s, inverse = norm_parts(residual)
        second = (s * vec[3:4, :] + vec[4:5, :]).astype(bf16)
        sec[rows, :] = second
        grad = cot[rows, :]
        mg[rows, :] = grad
        for j in range(hidden // 512):
            cols = slice(j * 512, (j + 1) * 512)
            h = dot(second, wh[:, cols]) + hbias[0:1, cols]
            phi = phi_of(h)
            act[rows, cols] = (h * phi).astype(bf16)
            hidden_grad = (dot(grad, wo[:, cols]) * slope_of(h, phi)).astype(bf16)
            hg[rows, cols] = hidden_grad
            hbgrad[0:1, cols] += jnp.sum(hidden_grad.astype(f32), axis=0, keepdims=True)
        mixed = dot(act[rows, :], wo[...], NT)
        out_store(rows, (residual + (mixed + vec[5:6, :])).astype(bf16))
        second_grad = dot(hg[rows, :], wh[...], NT)
        up = grad.astype(f32)
        vgrad[3:4, :] += jnp.sum(second_grad * s, axis=0, keepdims=True)
        vgrad[4:5, :] += jnp.sum(second_grad, axis=0, keepdims=True)
        vgrad[5:6, :] += jnp.sum(up, axis=0, keepdims=True)
        resid_grad = up + norm_back(second_grad * vec[3:4, :], s, inverse)
        resid_out[rows, :] = resid_grad
        conv = conv_out[rows, :]
        conv_grad = (resid_grad * slope_of(conv, phi_of(conv))).astype(bf16)
        cg_out[rows, :] = conv_grad
        vgrad[2:3, :] += jnp.sum(conv_grad.astype(f32), axis=0, keepdims=True)
        return 0

    def idle_step(i, _):
        rows = pl.ds(mult(i * ROWS, ROWS), ROWS)
        out_store(rows, x_full[rows, :])
        resid_out[rows, :] = cot[rows, :].astype(f32)
        for ref in (cg_out, sec, mg):
            ref[rows, :] = jnp.zeros((ROWS, full), bf16)
        for ref in (act, hg):
            ref[rows, :] = jnp.zeros((ROWS, hidden), bf16)
        return 0

    lax.fori_loop(0, blocks, row_step, 0)
    lax.fori_loop(blocks, seq // ROWS, idle_step, 0)

    sec_t = sec[...].T
    mg_t = mg[...].T
    for m in range(hidden // part):
        cols = slice(m * part, (m + 1) * part)
        for w, (left, right) in enumerate(((sec_t, hg), (mg_t, act))):
            value = dot(left, right[:, cols]).astype(bf16)
            for d in range(full // di):
                dc, b, a, dz = dest_slot(place, d, m)
                rsb[dc, b, a, dz, w] = value[d * di : (d + 1) * di, :]


def conv_backward(place, x_full, na, cg, resid, w, vec, *rest):
    in_grad, rsb, vgrad, cf, cab = rest
    seq, full = x_full.shape
    taps, di, own = rsb.shape[4:]
    blocks = place[3]
    vgrad[...] = jnp.zeros_like(vgrad)
    cf[...] = jnp.zeros_like(cf)

    def widen(i, _):
        row = mult(i * 128, 128)
        cf[pl.ds(mult(row + REACH, 8), 128), :] = cg[pl.ds(row, 128), :].astype(f32)
        return 0

    lax.fori_loop(0, seq // 128, widen, 0)

    def shift_step(i, _):
        row = mult(i * 64, 64)
        cab[0, pl.ds(row, 64), :] = cf[pl.ds(row, 64), :].astype(bf16)
        cab[1, pl.ds(row, 64), :] = cf[pl.ds(mult(row + 8, 8), 64), :].astype(bf16)
        return 0

    lax.fori_loop(0, cab.shape[1] // 64, shift_step, 0)

    def in_store(rows, values):
        values = values.astype(bf16)
        for m in range(full // own):
            in_grad[place[1] ^ m, rows, :] = values[:, m * own : (m + 1) * own]

    def row_step(i, _):
        row = mult(i * ROWS, ROWS)
        rows = pl.ds(row, ROWS)
        total = jnp.zeros((ROWS, full), f32)
        for t in range(KERNEL):
            u = KERNEL - 1 - t
            shifted = cab[u & 1, pl.ds(mult(row + DILATION * (u - (u & 1)), 16), ROWS), :]
            total = total + dot(shifted, w[t * full : (t + 1) * full, :], NT)
        s, inverse = norm_parts(x_full[rows, :].astype(f32))
        vgrad[0:1, :] += jnp.sum(total * s, axis=0, keepdims=True)
        vgrad[1:2, :] += jnp.sum(total, axis=0, keepdims=True)
        in_store(rows, resid[rows, :] + norm_back(total * vec[0:1, :], s, inverse))
        return 0

    def idle_step(i, _):
        rows = pl.ds(mult(i * ROWS, ROWS), ROWS)
        in_store(rows, resid[rows, :])
        return 0

    lax.fori_loop(0, blocks, row_step, 0)
    lax.fori_loop(blocks, seq // ROWS, idle_step, 0)

    na_t = na[...].T

    def tap_step(t, _):
        u = KERNEL - 1 - t
        odd = u & 1
        shifted = cab[odd, pl.ds(mult((u - odd) * DILATION, 16), seq), :]
        value = dot(na_t, shifted).astype(bf16)
        for d in range(full // di):
            for m in range(full // own):
                dc, b, a, dz = dest_slot(place, d, m)
                rsb[dc, b, a, dz, t] = value[d * di : (d + 1) * di, m * own : (m + 1) * own]
        return 0

    lax.fori_loop(0, KERNEL, tap_step, 0)


def call(kernel, place, args, outs, scratch, flops, mib):
    spec = pl.BlockSpec(memory_space=pltpu.VMEM)
    moved = sum(a.size * a.dtype.itemsize for a in (*args, *outs))
    return pl.pallas_call(
        kernel,
        out_shape=outs,
        in_specs=[pl.BlockSpec(memory_space=pltpu.SMEM)] + [spec] * len(args),
        out_specs=[spec] * len(outs),
        scratch_shapes=scratch,
        compiler_params=pltpu.CompilerParams(vmem_limit_bytes=mib * 2**20),
        cost_estimate=pl.CostEstimate(flops=flops, bytes_accessed=moved, transcendentals=0),
    )(place, *args)


def adam_step(weight, first_mom, second, gradient, clip_scale, step_rate, decay_rate):
    clipped = gradient * clip_scale
    first_new = BETA_ONE * first_mom + (1.0 - BETA_ONE) * clipped
    second_new = BETA_TWO * second + (1.0 - BETA_TWO) * clipped * clipped
    update_dir = (
        first_new
        / (1.0 - BETA_ONE**STEP)
        / (jnp.sqrt(second_new / (1.0 - BETA_TWO**STEP)) + ADAM_EPS)
    )
    return (weight - step_rate * (update_dir + decay_rate * weight), first_new, second_new)


def square_sum(values):
    return jnp.sum(values * values)


def per_device(
    ndp,
    nmp,
    inputs,
    cotangent,
    lengths,
    conv_master,
    hidden_master,
    output_master,
    conv_first,
    hidden_first,
    output_first,
    conv_second,
    hidden_second,
    output_second,
    vectors,
    vector_first,
    vector_second,
    hidden_bias,
    bias_first,
    bias_second,
):
    axes = ("dp", "mp")
    nz = ndp // 2
    seq, own = inputs.shape[1:]
    full = vectors.shape[1]
    part = hidden_bias.shape[0]
    hidden = part * nmp
    di = full // ndp
    dp, mp = lax.axis_index("dp"), lax.axis_index("mp")

    def perm(move):
        pairs = []
        for i in range(ndp * nmp):
            d, m = divmod(i, nmp)
            z, x, y, c = move(d >> 1, d & 1, m >> 1, m & 1)
            pairs.append((i, (z * 2 + x) * nmp + y * 2 + c))
        return pairs

    across_z = [perm(lambda z, x, y, c, k=k: (z ^ k, x, y, c)) for k in range(nz)]
    step_a = perm(lambda z, x, y, c: (z, x ^ 1, y, c) if c == 0 else (z, x, y ^ 1, c))
    step_b = perm(lambda z, x, y, c: (z, x, y ^ 1, c) if c == 0 else (z, x ^ 1, y, c))
    step_c = perm(lambda z, x, y, c: (z, x, y, c ^ 1))
    within = [[(i, i ^ k) for i in range(nmp)] for k in range(nmp)]

    def send(values, pairs):
        return lax.ppermute(values, axes, pairs)

    def gather(shard):
        flat = jnp.stack([shard] + [send(shard, across_z[k]) for k in range(1, nz)])
        part_a, part_b = send(flat, step_a), send(flat, step_b)
        mine = [flat, part_a, part_b, send(part_a, step_b)]
        return mine + [send(t, step_c) for t in mine]

    def scatter(parts):
        parts = parts[0].astype(f32) + send(parts[1], step_c).astype(f32)
        parts = parts[0] + send(parts[1].astype(bf16), step_b).astype(f32)
        parts = parts[0] + send(parts[1].astype(bf16), step_a).astype(f32)
        low = parts.astype(bf16)
        total = parts[0]
        for k in range(1, nz):
            total = total + send(low[k], across_z[k]).astype(f32)
        return total

    def to_windows(values):
        blocks = [lax.dynamic_index_in_dim(values, mp ^ k, 0, False) for k in range(nmp)]
        return [blocks[0]] + [lax.ppermute(blocks[k], "mp", within[k]) for k in range(1, nmp)]

    def to_columns(values):
        pieces = [values[0]] + [lax.ppermute(values[k], "mp", within[k]) for k in range(1, nmp)]
        for bit in range(nmp.bit_length() - 1):
            odd = ((mp >> bit) & 1) == 1
            pieces = [jnp.where(odd, pieces[k ^ (1 << bit)], pieces[k]) for k in range(nmp)]
        return jnp.stack(pieces)

    def all_sum(values):
        for pairs in (step_c, step_a, step_b):
            values = values + send(values, pairs)
        step = 1
        while step < nz:
            values = values + send(values, across_z[step])
            step *= 2
        return values

    length = lax.dynamic_index_in_dim(lengths, mp, 0, False)
    place = jnp.stack([dp, mp, length, length // ROWS]).astype(jnp.int32)
    x_parts = to_windows(inputs)
    conv_parts = gather(conv_master.astype(bf16))
    c_parts = to_windows(cotangent)
    ffn_parts = gather(jnp.stack([hidden_master.astype(bf16), output_master.astype(bf16).T]))
    vec = jnp.concatenate([vectors, jnp.zeros((2, full), f32)])
    bias_parts = [hidden_bias] + [lax.ppermute(hidden_bias, "mp", within[k]) for k in range(1, nmp)]
    bias_all = to_columns_local(bias_parts, mp, nmp).reshape(1, hidden)

    S = jax.ShapeDtypeStruct
    padded = seq + 2 * REACH
    w_full, x_full, normed, conv_out = call(
        conv_forward,
        place,
        (*x_parts, vec, *conv_parts),
        (
            S((KERNEL * full, full), bf16),
            S((seq, full), bf16),
            S((seq, full), bf16),
            S((seq, full), f32),
        ),
        [pltpu.VMEM((padded + 8, full), f32), pltpu.VMEM((2, padded, full), bf16)],
        2 * seq * KERNEL * full * full,
        40,
    )
    block_rel, resid_grad, conv_grad, ffn_send, vgrad_two, bias_grad = call(
        ffn,
        place,
        (x_full, conv_out, *c_parts, vec, bias_all, *ffn_parts),
        (
            S((nmp, seq, own), bf16),
            S((seq, full), f32),
            S((seq, full), bf16),
            S((2, 2, 2, nz, 2, di, part), bf16),
            S((8, full), f32),
            S((1, hidden), f32),
        ),
        [
            pltpu.VMEM((full, hidden), bf16),
            pltpu.VMEM((full, hidden), bf16),
            pltpu.VMEM((seq, full), bf16),
            pltpu.VMEM((seq, hidden), bf16),
            pltpu.VMEM((seq, hidden), bf16),
            pltpu.VMEM((seq, full), bf16),
            pltpu.VMEM((seq, full), bf16),
        ],
        12 * seq * hidden * full,
        56,
    )
    in_rel, conv_send, vgrad_one = call(
        conv_backward,
        place,
        (x_full, normed, conv_grad, resid_grad, w_full, vec),
        (
            S((nmp, seq, own), bf16),
            S((2, 2, 2, nz, KERNEL, di, own), bf16),
            S((8, full), f32),
        ),
        [pltpu.VMEM((padded + 8, full), f32), pltpu.VMEM((2, padded, full), bf16)],
        4 * seq * KERNEL * full * full,
        48,
    )
    block_output = to_columns(block_rel)
    ffn_share = scatter(ffn_send)
    conv_share = scatter(conv_send)
    input_grad = to_columns(in_rel).astype(f32)

    small = all_sum(
        jnp.concatenate([(vgrad_one + vgrad_two)[:6], bias_grad.reshape(hidden // full, full)])
    )
    vector_sum, bias_sum = small[:6], small[6:].reshape(hidden)
    hidden_share, output_share = ffn_share[0], ffn_share[1].T
    squares = square_sum(conv_share) + square_sum(ffn_share)
    squares_all = all_sum(jnp.broadcast_to(squares, (8, 128)))[0, 0]
    grad_norm = jnp.sqrt(squares_all + square_sum(small))
    clip_scale = jnp.minimum(1.0, CLIP_NORM / (grad_norm + 1e-06))
    bias_share = lax.dynamic_slice_in_dim(bias_sum, mp * part, part, 0)
    matrices = (
        (conv_master, conv_first, conv_second, conv_share),
        (hidden_master, hidden_first, hidden_second, hidden_share),
        (output_master, output_first, output_second, output_share),
    )
    small_ones = (
        (vectors, vector_first, vector_second, vector_sum),
        (hidden_bias, bias_first, bias_second, bias_share),
    )
    updated = [adam_step(*m, clip_scale, MATRIX_RATE, WEIGHT_DECAY) for m in matrices]
    updated += [adam_step(*m, clip_scale, VECTOR_RATE, 0.0) for m in small_ones]
    return (block_output, input_grad, grad_norm, *(leaf for new in updated for leaf in new))


def to_columns_local(pieces, mp, nmp):
    for bit in range(nmp.bit_length() - 1):
        odd = ((mp >> bit) & 1) == 1
        pieces = [jnp.where(odd, pieces[k ^ (1 << bit)], pieces[k]) for k in range(nmp)]
    return jnp.stack(pieces)


def solution(mesh):
    rows = P("dp", None, "mp")
    conv = P(None, "dp", "mp")
    hid = P("dp", "mp")
    out = P("mp", "dp")
    return jax.shard_map(
        functools.partial(per_device, mesh.shape["dp"], mesh.shape["mp"]),
        mesh=mesh,
        in_specs=(rows, rows, P("dp"), *(conv, hid, out) * 3, *(P(),) * 3, *(P("mp"),) * 3),
        out_specs=(
            rows,
            rows,
            P(),
            *(conv,) * 3,
            *(hid,) * 3,
            *(out,) * 3,
            *(P(),) * 3,
            *(P("mp"),) * 3,
        ),
        check_vma=False,
    )
```

time: 657 us -> 270 us (0.41); the launches traced: 647 us -> 269 us
  matrix products: 144 us -> 0 us
  waiting for transfers between devices: 238 us -> 104 us
  blocking collectives: 126 us -> 0 us
  starting transfers between devices: 0.62 us -> 68.8 us
  other arithmetic: 83.3 us -> 28.5 us
  Pallas kernels: 0 us -> 38 us
  between operations: 20.1 us -> 7.62 us
  local copies, waits for them, and re-layouts: 34.2 us -> 22.1 us
    dot_general x33 -> x0, matrix products: 144 us -> none  [the longest x9 61 us: per_device(): jnp.einsum('wpo,io->wpi', shifted, conv_weight[tap_index], preferred_elem...]
    reduce_scatter x5 -> x0, waiting for transfers between devices: 117 us -> none  [the longest x1 71.4 us: per_device(): lax.psum_scatter(conv_w_grad, 'dp', scatter_dimension=1, tiled=True)]
    ppermute x0 -> x57, waiting for transfers between devices: none -> 104 us  [the longest x42 67.1 us: send(): return lax.ppermute(values, axes, pairs)]
    all_gather x4 -> x0, waiting for transfers between devices: 77.3 us -> none  [the longest x1 35.4 us: per_device(): lax.all_gather(inputs, 'mp', axis=2, tiled=True)]
    ppermute x0 -> x57, starting transfers between devices: none -> 68.8 us  [the longest x42 57.7 us: send(): return lax.ppermute(values, axes, pairs)]
    psum x3 -> x0, blocking collectives: 63.5 us -> none  [the longest x1 40.2 us: per_device(): lax.psum((vector_padded, bias_padded, big_squares), ('dp', 'mp'))]
    all_gather x2 -> x0, blocking collectives: 62.7 us -> none  [the longest x1 31.3 us: per_device(): lax.all_gather(hidden_master.astype(jnp.bfloat16), 'dp', axis=0, tiled=True)]
    unnamed x11 -> x0, waiting for transfers between devices: 44 us -> none
  transfers between devices with their start and end apart: 10 -> 57, of which waited for: 7 -> 23; matrix products, arithmetic and copies ran while one was open for 31% -> 12% of each run, Pallas kernels for 0% -> 8%
where the time goes in v1:
time: 270 us; the launch traced here: 269 us
  waiting for transfers between devices  104 us (39%)
  starting transfers between devices  68.8 us (25%)
  Pallas kernels  38 us (14%)
  other arithmetic  28.5 us (11%)
  local copies, waits for them, and re-layouts  22.1 us (8%)
  between operations  7.62 us (3%)
    ppermute x42, waiting for transfers between devices, send(): return lax.ppermute(values, axes, pairs)  67.1 us
    ppermute x42, starting transfers between devices, send(): return lax.ppermute(values, axes, pairs)  57.7 us
    pallas_call x3, Pallas kernels, call(): pl.pallas_call(kernel, out_shape=outs, in_specs=[pl.BlockSpec(memory_spac...  38 us
    ppermute x6, waiting for transfers between devices, to_windows(): lax.ppermute(blocks[k], 'mp', within[k])  28 us
    unnamed x93, local copies, waits for them, and re-layouts  9.25 us
    add x2, other arithmetic, scatter(): parts = parts[0].astype(f32) + send(parts[1], step_c).astype(f32)  5.93 us
    squeeze x2, local copies, waits for them, and re-layouts, scatter(): parts = parts[0].astype(f32) + send(parts[1], step_c).astype(f32)  5.71 us
  transfers between devices with their start and end apart: 57, of which 23 were waited for; matrix products, arithmetic and copies ran while one was open for 12% of the time, Pallas kernels for 8%

profile of v1, /device:TPU:0, one launch (start us, length us, event | category | flops | bytes accessed | tf_op | source)
XLA Modules:
  0.0 268.6 jit_solution(16829879073301121016)
XLA Ops:
  1.8 4.1 %collective-permute-start.4 = (bf16[9,64,128]{2,1,0:T(8,128)(2,1)S(1)}, bf16[9,64,128]{2,1,0:T(8,128)(2,1)S(1)}, u32[]{:S(2)}, u32[]{:S(2)}) collective-permute-start(bf16[9,64,128]{2,1,0:T(8,128)(2,1)S(1)} %convert_element_type.82), channel_id=1, source_target_pairs={{0,16},{1,17},{2,18},{3,19},{4,20},{5,21},{6,22},{7,23},{8,24},{9,... | collective-permute-start | bytes 442376 | tf_op jit(solution)/shard_map/ppermute | solution.py:370
  10.3 6.6 %collective-permute-done.4 = bf16[9,64,128]{2,1,0:T(8,128)(2,1)S(1)} collective-permute-done((bf16[9,64,128]{2,1,0:T(8,128)(2,1)S(1)}, bf16[9,64,128]{2,1,0:T(8,128)(2,1)S(1)}, u32[]{:S(2)}, u32[]{:S(2)}) %collective-permute-start.4) | collective-permute-done | bytes 147488 | tf_op jit(solution)/shard_map/ppermute | solution.py:370
  19.8 2.5 collective-permute-start.19
  22.3 1.9 collective-permute-start.20
  29.2 2.3 collective-permute-done.17
  36.8 3.8 %collective-permute-done.21 = bf16[2,64,512]{2,1,0:T(8,128)(2,1)S(1)} collective-permute-done((bf16[2,64,512]{2,1,0:T(8,128)(2,1)}, bf16[2,64,512]{2,1,0:T(8,128)(2,1)S(1)}, u32[]{:S(2)}, u32[]{:S(2)}) %collective-permute-start.21) | collective-permute-done | bytes 131104 | tf_op jit(solution)/shard_map/ppermute | solution.py:370
  42.2 1.8 pad_maximum_fusion.2.rest_0_
  50.9 26.7 %collective-permute-done.14.c2 = bf16[1024,128]{1,0:T(8,128)(2,1)} collective-permute-done((bf16[1024,128]{1,0:T(8,128)(2,1)S(1)}, bf16[1024,128]{1,0:T(8,128)(2,1)}, u32[]{:S(2)}, u32[]{:S(2)}) %collective-permute-start.14) | collective-permute-done | bytes 262176 | tf_op jit(solution)/shard_map/ppermute | solution.py:390
  85.1 2.7 %collective-permute-done.24.rest_3_ = bf16[4,2,64,512]{3,2,1,0:T(8,128)(2,1)} collective-permute-done((bf16[4,2,64,512]{3,2,1,0:T(8,128)(2,1)}, bf16[4,2,64,512]{3,2,1,0:T(8,128)(2,1)}, u32[]{:S(2)}, u32[]{:S(2)}) %collective-permute-start.24) | collective-permute-done | bytes 524320 | tf_op jit(solution)/shard_map/ppermute | solution.py:370
  92.4 7.5 %shard_map.313 = (bf16[4608,512]{1,0:T(8,128)(2,1)}, bf16[1024,512]{1,0:T(8,128)(2,1)S(1)}, bf16[1024,512]{1,0:T(8,128)(2,1)S(1)}, f32[1024,512]{1,0:T(8,128)S(1)}) custom-call(s32[4]{0:T(128)S(1)} %pad_add_fusion.place, bf16[1024,128]{1,0:T(8,128)(2,1)S(1)} %get-tuple-element.89.x0, bf16[1024,128]{1,0:T(8,128)(2,1)S(1)} %collective-permute-done.x1, ...), custom_call_target="tpu_custom_call" | custom-call | flops 4831838208 | bytes 14696448 | tf_op jit(solution)/shard_map/pallas_call | solution.py:297
  103.0 16.1 %shard_map.314 = (bf16[4,1024,128]{2,1,0:T(8,128)(2,1)}, f32[1024,512]{1,0:T(8,128)}, bf16[1024,512]{1,0:T(8,128)(2,1)}, bf16[2,2,2,4,2,64,512]{6,5,4,3,2,1,0:T(...) custom-call(s32[4]{0:T(128)} %copy-done.2, bf16[1024,512]{1,0:T(8,128)(2,1)} %copy-done.9, f32[1024,512]{1,0:T(8,128)} %copy-done.8, ...), custom_call_target="tpu_custom_call" | custom-call | flops 12884901888 | bytes 16826368 | tf_op jit(solution)/shard_map/pallas_call | solution.py:297
  119.2 3.3 %slice_bitcast_fusion.3 = bf16[2,2,4,2,64,512]{5,4,3,2,1,0:T(8,128)(2,1)} fusion(bf16[2,2,2,4,2,64,512]{6,5,4,3,2,1,0:T(8,128)(2,1)} %get-tuple-element.40), kind=kLoop, calls=%fused_computation.9 | loop fusion | bytes 4194304 | tf_op jit(solution)/shard_map/squeeze | solution.py:379
  122.5 14.3 %shard_map.315 = (bf16[4,1024,128]{2,1,0:T(8,128)(2,1)S(1)}, bf16[2,2,2,4,9,64,128]{6,5,4,3,2,1,0:T(8,128)(2,1)}, f32[8,512]{1,0:T(8,128)S(1)}) custom-call(s32[4]{0:T(128)S(1)} %copy-done.3, bf16[1024,512]{1,0:T(8,128)(2,1)S(1)} %copy-done.10, bf16[1024,512]{1,0:T(8,128)(2,1)S(1)} %get-tuple-element.34.na, bf16[1024,512]{1,0:T(8,128)(2,1)S(1)} %copy-done.11, ...), custom_call_target="tpu_custom_call" | custom-call | flops 9663676416 | bytes 15761408 | tf_op jit(solution)/shard_map/pallas_call | solution.py:297
  136.8 2.4 slice_bitcast_fusion.1
  141.2 3.2 %convert_add_fusion.1 = f32[2,2,4,2,64,512]{5,4,3,2,1,0:T(8,128)S(1)} fusion(bf16[2,2,4,2,64,512]{5,4,3,2,1,0:T(8,128)(2,1)} %collective-permute-done.41, bf16[2,2,2,4,2,64,512]{6,5,4,3,2,1,0:T(8,128)(2,1)} %get-tuple-element.40), kind=kLoop, calls=%fused_computation.1 | loop fusion | flops 3145728 | bytes 8388608 | tf_op jit(solution)/shard_map/add | solution.py:379
  145.6 7.1 %collective-permute-start.42 = (bf16[2,4,2,64,512]{4,3,2,1,0:T(8,128)(2,1)}, bf16[2,4,2,64,512]{4,3,2,1,0:T(8,128)(2,1)}, u32[]{:S(2)}, u32[]{:S(2)}) collective-permute-start(bf16[2,4,2,64,512]{4,3,2,1,0:T(8,128)(2,1)} %fusion.4), channel_id=1, source_target_pairs={{0,2},{1,5},{2,0},{3,7},{4,6},{5,1},{6,4},{7,3},{8,10},{9,13},{10,... | collective-permute-start | bytes 3145736 | tf_op jit(solution)/shard_map/ppermute | solution.py:370
  152.8 2.7 %convert_add_fusion = f32[2,2,4,9,64,128]{5,4,3,2,1,0:T(8,128)S(1)} fusion(bf16[2,2,4,9,64,128]{5,4,3,2,1,0:T(8,128)(2,1)} %collective-permute-done.35, bf16[2,2,2,4,9,64,128]{6,5,4,3,2,1,0:T(8,128)(2,1)S(1)} %copy-done.15), kind=kLoop, calls=%fused_computation | loop fusion | flops 3538944 | bytes 9437184 | tf_op jit(solution)/shard_map/add | solution.py:379
  155.5 2.2 copy-done.12
  159.2 4.3 %collective-permute-done.53 = f32[10,512]{1,0:T(8,128)S(1)} collective-permute-done((f32[10,512]{1,0:T(8,128)S(1)}, f32[10,512]{1,0:T(8,128)S(1)}, u32[]{:S(2)}, u32[]{:S(2)}) %collective-permute-start.53) | collective-permute-done | bytes 20512 | tf_op jit(solution)/shard_map/ppermute | solution.py:370
  166.5 18.2 %collective-permute-done.54 = f32[10,512]{1,0:T(8,128)S(1)} collective-permute-done((f32[10,512]{1,0:T(8,128)S(1)}, f32[10,512]{1,0:T(8,128)S(1)}, u32[]{:S(2)}, u32[]{:S(2)}) %collective-permute-start.54) | collective-permute-done | bytes 20512 | tf_op jit(solution)/shard_map/ppermute | solution.py:370
  184.7 2.0 slice_bitcast_fusion.11
  186.7 1.9 collective-permute-done.55
  188.6 17.1 %collective-permute-start.56 = (f32[10,512]{1,0:T(8,128)S(1)}, f32[10,512]{1,0:T(8,128)S(1)}, u32[]{:S(2)}, u32[]{:S(2)}) collective-permute-start(f32[10,512]{1,0:T(8,128)S(1)} %add.204), channel_id=1, source_target_pairs={{0,16},{1,17},{2,18},{3,19},{4,20},{5,21},{6,22},{7,23},{8,24},{9,... | collective-permute-start | bytes 61448 | tf_op jit(solution)/shard_map/ppermute | solution.py:370
  205.8 2.2 fusion.1
  208.8 2.1 collective-permute-start.37
  211.4 5.8 %collective-permute-done.43 = bf16[4,2,64,512]{3,2,1,0:T(8,128)(2,1)S(1)} collective-permute-done((bf16[4,2,64,512]{3,2,1,0:T(8,128)(2,1)S(1)}, bf16[4,2,64,512]{3,2,1,0:T(8,128)(2,1)S(1)}, u32[]{:S(2)}, u32[]{:S(2)}) %collective-permute-start.43) | collective-permute-done | bytes 524320 | tf_op jit(solution)/shard_map/ppermute | solution.py:370
  218.7 4.9 %collective-permute-done.37 = bf16[4,9,64,128]{3,2,1,0:T(8,128)(2,1)S(1)} collective-permute-done((bf16[4,9,64,128]{3,2,1,0:T(8,128)(2,1)S(1)}, bf16[4,9,64,128]{3,2,1,0:T(8,128)(2,1)S(1)}, u32[]{:S(2)}, u32[]{:S(2)}) %collective-permute-start.37) | collective-permute-done | bytes 589856 | tf_op jit(solution)/shard_map/ppermute | solution.py:370
  226.0 5.8 %collective-permute-done.45 = bf16[2,64,512]{2,1,0:T(8,128)(2,1)S(1)} collective-permute-done((bf16[2,64,512]{2,1,0:T(8,128)(2,1)S(1)}, bf16[2,64,512]{2,1,0:T(8,128)(2,1)S(1)}, u32[]{:S(2)}, u32[]{:S(2)}) %collective-permute-start.45) | collective-permute-done | bytes 131104 | tf_op jit(solution)/shard_map/ppermute | solution.py:370
  233.6 6.2 %collective-permute-done.39 = bf16[9,64,128]{2,1,0:T(8,128)(2,1)S(1)} collective-permute-done((bf16[9,64,128]{2,1,0:T(8,128)(2,1)S(1)}, bf16[9,64,128]{2,1,0:T(8,128)(2,1)S(1)}, u32[]{:S(2)}, u32[]{:S(2)}) %collective-permute-start.39) | collective-permute-done | bytes 147488 | tf_op jit(solution)/shard_map/ppermute | solution.py:370
  243.0 1.8 collective-permute-start.30
  249.1 3.2 %collective-permute-done.30 = bf16[1024,128]{1,0:T(8,128)(2,1)S(1)} collective-permute-done((bf16[1024,128]{1,0:T(8,128)(2,1)S(1)}, bf16[1024,128]{1,0:T(8,128)(2,1)S(1)}, u32[]{:S(2)}, u32[]{:S(2)}) %collective-permute-start.30) | collective-permute-done | bytes 262176 | tf_op jit(solution)/shard_map/ppermute | solution.py:393
  257.0 2.5 collective-permute-start.51
  (236 shorter events, 71.7 us)
Async XLA Ops:
  1.8 15.1 %collective-permute-start.4 = (bf16[9,64,128]{2,1,0:T(8,128)(2,1)S(1)}, bf16[9,64,128]{2,1,0:T(8,128)(2,1)S(1)}, u32[]{:S(2)}, u32[]{:S(2)}) collective-permute-start(bf16[9,64,128]{2,1,0:T(8,128)(2,1)S(1)} %convert_element_type.82), channel_id=1, source_target_pairs={{0,16},{1,17},{2,18},{3,19},{4,20},{5,21},{6,22},{7,23},{8,24},{9,... | collective-permute-start | bytes 442376 | tf_op jit(solution)/shard_map/ppermute | solution.py:370
  5.9 11.0 %collective-permute-start.5 = (bf16[9,64,128]{2,1,0:T(8,128)(2,1)S(1)}, bf16[9,64,128]{2,1,0:T(8,128)(2,1)S(1)}, u32[]{:S(2)}, u32[]{:S(2)}) collective-permute-start(bf16[9,64,128]{2,1,0:T(8,128)(2,1)S(1)} %convert_element_type.82), channel_id=1, source_target_pairs={{0,24},{1,25},{2,26},{3,27},{4,28},{5,29},{6,30},{7,31},{8,16},{9,... | collective-permute-start | bytes 442376 | tf_op jit(solution)/shard_map/ppermute | solution.py:370
  7.2 10.2 %collective-permute-start.3 = (bf16[9,64,128]{2,1,0:T(8,128)(2,1)S(1)}, bf16[9,64,128]{2,1,0:T(8,128)(2,1)S(1)}, u32[]{:S(2)}, u32[]{:S(2)}) collective-permute-start(bf16[9,64,128]{2,1,0:T(8,128)(2,1)S(1)} %convert_element_type.82), channel_id=1, source_target_pairs={{0,8},{1,9},{2,10},{3,11},{4,12},{5,13},{6,14},{7,15},{8,0},{9,1},... | collective-permute-start | bytes 442376 | tf_op jit(solution)/shard_map/ppermute | solution.py:370
  17.5 27.9 %collective-permute-start.6 = (bf16[4,9,64,128]{3,2,1,0:T(8,128)(2,1)S(1)}, bf16[4,9,64,128]{3,2,1,0:T(8,128)(2,1)S(1)}, u32[]{:S(2)}, u32[]{:S(2)}) collective-permute-start(bf16[4,9,64,128]{3,2,1,0:T(8,128)(2,1)S(1)} %pad_maximum_fusion.1.rest_0_), channel_id=1, source_target_pairs={{0,4},{1,3},{2,6},{3,1},{4,0},{5,7},{6,2},{7,5},{8,12},{9,11},{10,... | collective-permute-start | bytes 1769480 | tf_op jit(solution)/shard_map/ppermute | solution.py:370
  19.8 14.5 %collective-permute-start.19 = (bf16[2,64,512]{2,1,0:T(8,128)(2,1)}, bf16[2,64,512]{2,1,0:T(8,128)(2,1)}, u32[]{:S(2)}, u32[]{:S(2)}) collective-permute-start(bf16[2,64,512]{2,1,0:T(8,128)(2,1)} %get-tuple-element.98), channel_id=1, source_target_pairs={{0,8},{1,9},{2,10},{3,11},{4,12},{5,13},{6,14},{7,15},{8,0},{9,1},... | collective-permute-start | bytes 393224 | tf_op jit(solution)/shard_map/ppermute | solution.py:370
  22.3 13.6 %collective-permute-start.20 = (bf16[2,64,512]{2,1,0:T(8,128)(2,1)}, bf16[2,64,512]{2,1,0:T(8,128)(2,1)}, u32[]{:S(2)}, u32[]{:S(2)}) collective-permute-start(bf16[2,64,512]{2,1,0:T(8,128)(2,1)} %get-tuple-element.98), channel_id=1, source_target_pairs={{0,16},{1,17},{2,18},{3,19},{4,20},{5,21},{6,22},{7,23},{8,24},{9,... | collective-permute-start | bytes 393224 | tf_op jit(solution)/shard_map/ppermute | solution.py:370
  24.3 16.3 %collective-permute-start = (bf16[1024,128]{1,0:T(8,128)(2,1)S(1)}, bf16[1024,128]{1,0:T(8,128)(2,1)S(1)}, u32[]{:S(2)}, u32[]{:S(2)}) collective-permute-start(bf16[1024,128]{1,0:T(8,128)(2,1)S(1)} %get-tuple-element.88), channel_id=1, source_target_pairs={{0,1},{1,0},{2,3},{3,2},{4,5},{5,4},{6,7},{7,6},{8,9},{9,8},{10,11... | collective-permute-start | bytes 786440 | tf_op jit(solution)/shard_map/ppermute | solution.py:390
  35.9 12.3 %collective-permute-start.2 = (bf16[1024,128]{1,0:T(8,128)(2,1)S(1)}, bf16[1024,128]{1,0:T(8,128)(2,1)S(1)}, u32[]{:S(2)}, u32[]{:S(2)}) collective-permute-start(bf16[1024,128]{1,0:T(8,128)(2,1)S(1)} %get-tuple-element.87), channel_id=1, source_target_pairs={{0,3},{1,2},{2,1},{3,0},{4,7},{5,6},{6,5},{7,4},{8,11},{9,10},{10,... | collective-permute-start | bytes 786440 | tf_op jit(solution)/shard_map/ppermute | solution.py:390
  40.6 37.6 %collective-permute-start.7 = (bf16[4,9,64,128]{3,2,1,0:T(8,128)(2,1)S(1)}, bf16[4,9,64,128]{3,2,1,0:T(8,128)(2,1)S(1)}, u32[]{:S(2)}, u32[]{:S(2)}) collective-permute-start(bf16[4,9,64,128]{3,2,1,0:T(8,128)(2,1)S(1)} %pad_maximum_fusion.1.rest_0_), channel_id=1, source_target_pairs={{0,2},{1,5},{2,0},{3,7},{4,6},{5,1},{6,4},{7,3},{8,10},{9,13},{10,... | collective-permute-start | bytes 1769480 | tf_op jit(solution)/shard_map/ppermute | solution.py:370
  44.7 32.9 %collective-permute-start.22 = (bf16[4,2,64,512]{3,2,1,0:T(8,128)(2,1)}, bf16[4,2,64,512]{3,2,1,0:T(8,128)(2,1)}, u32[]{:S(2)}, u32[]{:S(2)}) collective-permute-start(bf16[4,2,64,512]{3,2,1,0:T(8,128)(2,1)} %pad_maximum_fusion.2.rest_0_), channel_id=1, source_target_pairs={{0,4},{1,3},{2,6},{3,1},{4,0},{5,7},{6,2},{7,5},{8,12},{9,11},{10,... | collective-permute-start | bytes 1572872 | tf_op jit(solution)/shard_map/ppermute | solution.py:370
  45.4 34.4 %collective-permute-start.8 = (bf16[4,9,64,128]{3,2,1,0:T(8,128)(2,1)S(1)}, bf16[4,9,64,128]{3,2,1,0:T(8,128)(2,1)S(1)}, u32[]{:S(2)}, u32[]{:S(2)}) collective-permute-start(bf16[4,9,64,128]{3,2,1,0:T(8,128)(2,1)S(1)} %collective-permute-done.6.rest_1_), channel_id=1, source_target_pairs={{0,2},{1,5},{2,0},{3,7},{4,6},{5,1},{6,4},{7,3},{8,10},{9,13},{10,... | collective-permute-start | bytes 1769480 | tf_op jit(solution)/shard_map/ppermute | solution.py:370
  48.9 29.4 %collective-permute-start.23 = (bf16[4,2,64,512]{3,2,1,0:T(8,128)(2,1)}, bf16[4,2,64,512]{3,2,1,0:T(8,128)(2,1)S(1)}, u32[]{:S(2)}, u32[]{:S(2)}) collective-permute-start(bf16[4,2,64,512]{3,2,1,0:T(8,128)(2,1)} %pad_maximum_fusion.2.rest_0_), channel_id=1, source_target_pairs={{0,2},{1,5},{2,0},{3,7},{4,6},{5,1},{6,4},{7,3},{8,10},{9,13},{10,... | collective-permute-start | bytes 1572872 | tf_op jit(solution)/shard_map/ppermute | solution.py:370
  49.2 28.5 %collective-permute-start.14 = (bf16[1024,128]{1,0:T(8,128)(2,1)S(1)}, bf16[1024,128]{1,0:T(8,128)(2,1)}, u32[]{:S(2)}, u32[]{:S(2)}) collective-permute-start(bf16[1024,128]{1,0:T(8,128)(2,1)S(1)} %get-tuple-element.86), channel_id=1, source_target_pairs={{0,2},{1,3},{2,0},{3,1},{4,6},{5,7},{6,4},{7,5},{8,10},{9,11},{10,... | collective-permute-start | bytes 786440 | tf_op jit(solution)/shard_map/ppermute | solution.py:390
  77.7 10.1 %collective-permute-start.10 = (bf16[4,9,64,128]{3,2,1,0:T(8,128)(2,1)S(1)}, bf16[4,9,64,128]{3,2,1,0:T(8,128)(2,1)}, u32[]{:S(2)}, u32[]{:S(2)}) collective-permute-start(bf16[4,9,64,128]{3,2,1,0:T(8,128)(2,1)S(1)} %collective-permute-done.6.rest_1_), channel_id=1, source_target_pairs={{0,1},{1,0},{2,3},{3,2},{4,5},{5,4},{6,7},{7,6},{8,9},{9,8},{10,11... | collective-permute-start | bytes 1769480 | tf_op jit(solution)/shard_map/ppermute | solution.py:370
  78.2 10.1 %collective-permute-start.11 = (bf16[4,9,64,128]{3,2,1,0:T(8,128)(2,1)S(1)}, bf16[4,9,64,128]{3,2,1,0:T(8,128)(2,1)}, u32[]{:S(2)}, u32[]{:S(2)}) collective-permute-start(bf16[4,9,64,128]{3,2,1,0:T(8,128)(2,1)S(1)} %collective-permute-done.7.rest_2_), channel_id=1, source_target_pairs={{0,1},{1,0},{2,3},{3,2},{4,5},{5,4},{6,7},{7,6},{8,9},{9,8},{10,11... | collective-permute-start | bytes 1769480 | tf_op jit(solution)/shard_map/ppermute | solution.py:370
  84.5 18.5 %collective-permute-start.25 = (bf16[4,2,64,512]{3,2,1,0:T(8,128)(2,1)}, bf16[4,2,64,512]{3,2,1,0:T(8,128)(2,1)}, u32[]{:S(2)}, u32[]{:S(2)}) collective-permute-start(bf16[4,2,64,512]{3,2,1,0:T(8,128)(2,1)} %pad_maximum_fusion.2.rest_0_), channel_id=1, source_target_pairs={{0,1},{1,0},{2,3},{3,2},{4,5},{5,4},{6,7},{7,6},{8,9},{9,8},{10,11... | collective-permute-start | bytes 1572872 | tf_op jit(solution)/shard_map/ppermute | solution.py:370
  87.8 15.2 %collective-permute-start.26 = (bf16[4,2,64,512]{3,2,1,0:T(8,128)(2,1)}, bf16[4,2,64,512]{3,2,1,0:T(8,128)(2,1)}, u32[]{:S(2)}, u32[]{:S(2)}) collective-permute-start(bf16[4,2,64,512]{3,2,1,0:T(8,128)(2,1)} %collective-permute-done.22.rest_1_), channel_id=1, source_target_pairs={{0,1},{1,0},{2,3},{3,2},{4,5},{5,4},{6,7},{7,6},{8,9},{9,8},{10,11... | collective-permute-start | bytes 1572872 | tf_op jit(solution)/shard_map/ppermute | solution.py:370
  87.8 15.2 %collective-permute-start.27 = (bf16[4,2,64,512]{3,2,1,0:T(8,128)(2,1)}, bf16[4,2,64,512]{3,2,1,0:T(8,128)(2,1)}, u32[]{:S(2)}, u32[]{:S(2)}) collective-permute-start(bf16[4,2,64,512]{3,2,1,0:T(8,128)(2,1)} %copy-done.41), channel_id=1, source_target_pairs={{0,1},{1,0},{2,3},{3,2},{4,5},{5,4},{6,7},{7,6},{8,9},{9,8},{10,11... | collective-permute-start | bytes 1572872 | tf_op jit(solution)/shard_map/ppermute | solution.py:370
  88.3 14.7 %collective-permute-start.28 = (bf16[4,2,64,512]{3,2,1,0:T(8,128)(2,1)}, bf16[4,2,64,512]{3,2,1,0:T(8,128)(2,1)}, u32[]{:S(2)}, u32[]{:S(2)}) collective-permute-start(bf16[4,2,64,512]{3,2,1,0:T(8,128)(2,1)} %collective-permute-done.24.rest_3_), channel_id=1, source_target_pairs={{0,1},{1,0},{2,3},{3,2},{4,5},{5,4},{6,7},{7,6},{8,9},{9,8},{10,11... | collective-permute-start | bytes 1572872 | tf_op jit(solution)/shard_map/ppermute | solution.py:370
  89.0 13.3 %collective-permute-start.15 = (bf16[1024,128]{1,0:T(8,128)(2,1)}, bf16[1024,128]{1,0:T(8,128)(2,1)S(1)}, u32[]{:S(2)}, u32[]{:S(2)}) collective-permute-start(bf16[1024,128]{1,0:T(8,128)(2,1)} %get-tuple-element.83), channel_id=1, source_target_pairs={{0,3},{1,2},{2,1},{3,0},{4,7},{5,6},{6,5},{7,4},{8,11},{9,10},{10,... | collective-permute-start | bytes 786440 | tf_op jit(solution)/shard_map/ppermute | solution.py:390
  122.4 18.7 %collective-permute-start.41 = (bf16[2,2,4,2,64,512]{5,4,3,2,1,0:T(8,128)(2,1)}, bf16[2,2,4,2,64,512]{5,4,3,2,1,0:T(8,128)(2,1)}, u32[]{:S(2)}, u32[]{:S(2)}) collective-permute-start(bf16[2,2,4,2,64,512]{5,4,3,2,1,0:T(8,128)(2,1)} %slice_bitcast_fusion.3), channel_id=1, source_target_pairs={{0,1},{1,0},{2,3},{3,2},{4,5},{5,4},{6,7},{7,6},{8,9},{9,8},{10,11... | collective-permute-start | bytes 6291464 | tf_op jit(solution)/shard_map/ppermute | solution.py:370
  139.3 13.5 %collective-permute-start.35 = (bf16[2,2,4,9,64,128]{5,4,3,2,1,0:T(8,128)(2,1)S(1)}, bf16[2,2,4,9,64,128]{5,4,3,2,1,0:T(8,128)(2,1)}, u32[]{:S(2)}, u32[]{:S(2)}) collective-permute-start(bf16[2,2,4,9,64,128]{5,4,3,2,1,0:T(8,128)(2,1)S(1)} %slice_bitcast_fusion.1), channel_id=1, source_target_pairs={{0,1},{1,0},{2,3},{3,2},{4,5},{5,4},{6,7},{7,6},{8,9},{9,8},{10,11... | collective-permute-start | bytes 7077896 | tf_op jit(solution)/shard_map/ppermute | solution.py:370
  141.0 18.1 %collective-permute-start.52 = (f32[10,512]{1,0:T(8,128)S(1)}, f32[10,512]{1,0:T(8,128)S(1)}, u32[]{:S(2)}, u32[]{:S(2)}) collective-permute-start(f32[10,512]{1,0:T(8,128)S(1)} %pad_maximum_fusion.4), channel_id=1, source_target_pairs={{0,1},{1,0},{2,3},{3,2},{4,5},{5,4},{6,7},{7,6},{8,9},{9,8},{10,11... | collective-permute-start | bytes 61448 | tf_op jit(solution)/shard_map/ppermute | solution.py:370
  145.6 60.1 %collective-permute-start.42 = (bf16[2,4,2,64,512]{4,3,2,1,0:T(8,128)(2,1)}, bf16[2,4,2,64,512]{4,3,2,1,0:T(8,128)(2,1)}, u32[]{:S(2)}, u32[]{:S(2)}) collective-permute-start(bf16[2,4,2,64,512]{4,3,2,1,0:T(8,128)(2,1)} %fusion.4), channel_id=1, source_target_pairs={{0,2},{1,5},{2,0},{3,7},{4,6},{5,1},{6,4},{7,3},{8,10},{9,13},{10,... | collective-permute-start | bytes 3145736 | tf_op jit(solution)/shard_map/ppermute | solution.py:370
  157.9 50.2 %collective-permute-start.36 = (bf16[2,4,9,64,128]{4,3,2,1,0:T(8,128)(2,1)S(1)}, bf16[2,4,9,64,128]{4,3,2,1,0:T(8,128)(2,1)S(1)}, u32[]{:S(2)}, u32[]{:S(2)}) collective-permute-start(bf16[2,4,9,64,128]{4,3,2,1,0:T(8,128)(2,1)S(1)} %fusion.2), channel_id=1, source_target_pairs={{0,2},{1,5},{2,0},{3,7},{4,6},{5,1},{6,4},{7,3},{8,10},{9,13},{10,... | collective-permute-start | bytes 3538952 | tf_op jit(solution)/shard_map/ppermute | solution.py:370
  163.5 21.2 %collective-permute-start.54 = (f32[10,512]{1,0:T(8,128)S(1)}, f32[10,512]{1,0:T(8,128)S(1)}, u32[]{:S(2)}, u32[]{:S(2)}) collective-permute-start(f32[10,512]{1,0:T(8,128)S(1)} %add.202), channel_id=1, source_target_pairs={{0,2},{1,5},{2,0},{3,7},{4,6},{5,1},{6,4},{7,3},{8,10},{9,13},{10,... | collective-permute-start | bytes 61448 | tf_op jit(solution)/shard_map/ppermute | solution.py:370
  165.3 79.5 %collective-permute-start.32 = (bf16[1024,128]{1,0:T(8,128)(2,1)}, bf16[1024,128]{1,0:T(8,128)(2,1)}, u32[]{:S(2)}, u32[]{:S(2)}) collective-permute-start(bf16[1024,128]{1,0:T(8,128)(2,1)} %get-tuple-element.79), channel_id=1, source_target_pairs={{0,3},{1,2},{2,1},{3,0},{4,7},{5,6},{6,5},{7,4},{8,11},{9,10},{10,... | collective-permute-start | bytes 786440 | tf_op jit(solution)/shard_map/ppermute | solution.py:393
  165.3 79.7 %collective-permute-start.33 = (bf16[1024,128]{1,0:T(8,128)(2,1)}, bf16[1024,128]{1,0:T(8,128)(2,1)}, u32[]{:S(2)}, u32[]{:S(2)}) collective-permute-start(bf16[1024,128]{1,0:T(8,128)(2,1)} %get-tuple-element.78), channel_id=1, source_target_pairs={{0,2},{1,3},{2,0},{3,1},{4,6},{5,7},{6,4},{7,5},{8,10},{9,11},{10,... | collective-permute-start | bytes 786440 | tf_op jit(solution)/shard_map/ppermute | solution.py:393
  188.6 22.2 %collective-permute-start.56 = (f32[10,512]{1,0:T(8,128)S(1)}, f32[10,512]{1,0:T(8,128)S(1)}, u32[]{:S(2)}, u32[]{:S(2)}) collective-permute-start(f32[10,512]{1,0:T(8,128)S(1)} %add.204), channel_id=1, source_target_pairs={{0,16},{1,17},{2,18},{3,19},{4,20},{5,21},{6,22},{7,23},{8,24},{9,... | collective-permute-start | bytes 61448 | tf_op jit(solution)/shard_map/ppermute | solution.py:370
  208.8 14.8 %collective-permute-start.37 = (bf16[4,9,64,128]{3,2,1,0:T(8,128)(2,1)S(1)}, bf16[4,9,64,128]{3,2,1,0:T(8,128)(2,1)S(1)}, u32[]{:S(2)}, u32[]{:S(2)}) collective-permute-start(bf16[4,9,64,128]{3,2,1,0:T(8,128)(2,1)S(1)} %fusion.6), channel_id=1, source_target_pairs={{0,4},{1,3},{2,6},{3,1},{4,0},{5,7},{6,2},{7,5},{8,12},{9,11},{10,... | collective-permute-start | bytes 1769480 | tf_op jit(solution)/shard_map/ppermute | solution.py:370
  218.4 13.4 %collective-permute-start.45 = (bf16[2,64,512]{2,1,0:T(8,128)(2,1)S(1)}, bf16[2,64,512]{2,1,0:T(8,128)(2,1)S(1)}, u32[]{:S(2)}, u32[]{:S(2)}) collective-permute-start(bf16[2,64,512]{2,1,0:T(8,128)(2,1)S(1)} %get-tuple-element.96), channel_id=1, source_target_pairs={{0,16},{1,17},{2,18},{3,19},{4,20},{5,21},{6,22},{7,23},{8,24},{9,... | collective-permute-start | bytes 393224 | tf_op jit(solution)/shard_map/ppermute | solution.py:370
  233.6 12.2 %collective-permute-start.34 = (bf16[1024,128]{1,0:T(8,128)(2,1)}, bf16[1024,128]{1,0:T(8,128)(2,1)S(1)}, u32[]{:S(2)}, u32[]{:S(2)}) collective-permute-start(bf16[1024,128]{1,0:T(8,128)(2,1)} %get-tuple-element.77), channel_id=1, source_target_pairs={{0,1},{1,0},{2,3},{3,2},{4,5},{5,4},{6,7},{7,6},{8,9},{9,8},{10,11... | collective-permute-start | bytes 786440 | tf_op jit(solution)/shard_map/ppermute | solution.py:393
  (70 other events, 646.1 us)

commit v2 on v1

v2 whole, which is shorter than its diff:
```python
import functools

import jax
import jax.numpy as jnp
from jax import lax
from jax.experimental import pallas as pl
from jax.experimental.pallas import tpu as pltpu
from jax.sharding import PartitionSpec as P

KERNEL = 9
DILATION = 8
REACH = DILATION * (KERNEL // 2)
STEP = 10
ROWS = 256

NORM_EPS = 1e-05
BETA_ONE = 0.9
BETA_TWO = 0.999
ADAM_EPS = 1e-08
MATRIX_RATE = 0.03
VECTOR_RATE = 0.3
WEIGHT_DECAY = 0.01
CLIP_NORM = 1.0

f32 = jnp.float32
bf16 = jnp.bfloat16
NN = (((1,), (0,)), ((), ()))
NT = (((1,), (1,)), ((), ()))


def dot(a, b, dims=NN):
    return lax.dot_general(a, b, dims, preferred_element_type=f32)


def phi_of(v):
    return 0.5 * (1.0 + lax.erf(v * 0.7071067811865476))


def slope_of(v, phi):
    return phi + v * jnp.exp(-0.5 * v * v) * 0.3989422804014327


def norm_parts(v):
    centre = v - jnp.mean(v, axis=-1, keepdims=True)
    inverse = lax.rsqrt(jnp.mean(centre * centre, axis=-1, keepdims=True) + NORM_EPS)
    return centre * inverse, inverse


def norm_back(e, s, inverse):
    return inverse * (
        e - jnp.mean(e, axis=-1, keepdims=True) - s * jnp.mean(e * s, axis=-1, keepdims=True)
    )


def mult(v, n):
    return pl.multiple_of(v, n)


def relative(place, d, m, plain):
    dp, mp = place[0], place[1]
    fx = (dp & 1) ^ (d & 1)
    fy = (mp >> 1) ^ (m >> 1)
    dz = (dp >> 1) ^ (d >> 1)
    if plain or (m & 1):
        return fx, fy, dz
    return fy, fx, dz


def source_of(place, dc, b, a, dz, plain):
    dp, mp = place[0], place[1]
    if plain:
        fx, fy = b, a
    else:
        flip = (mp & 1) ^ dc
        fx = jnp.where(flip == 0, a, b)
        fy = jnp.where(flip == 0, b, a)
    d = ((dp >> 1) ^ dz) * 2 + ((dp & 1) ^ fx)
    m = ((mp >> 1) ^ fy) * 2 + ((mp & 1) ^ dc)
    return d, m


def store_shares(place, keep, give, m, plain, devices, store):
    same = (place[1] & 1) == (m & 1)

    @pl.when(same)
    def _():
        for d in range(devices):
            store(keep, relative(place, d, m, plain), d)

    @pl.when(jnp.logical_not(same))
    def _():
        for d in range(devices):
            store(give, relative(place, d, m, plain), d)


SLOTS = tuple((dc, b, a) for dc in (0, 1) for b, a in ((0, 0), (0, 1), (1, 0), (1, 1)))


def fetch(place, x_parts, x_full, x_sem, pieces, whole, sems):
    seq, own = x_full.shape[0], x_parts[0].shape[1]
    di, cols = pieces[0].shape[2:]
    rows = []
    for k, part in enumerate(x_parts):
        target = x_full.at[:, pl.ds(mult((place[1] ^ k) * own, own), own)]
        rows.append(pltpu.make_async_copy(part.at[pl.ds(0, seq), :], target, x_sem.at[k]))
        rows[-1].start()
    shards = []
    for slot, ((dc, b, a), piece) in enumerate(zip(SLOTS, pieces)):
        for z in range(piece.shape[0]):
            d, m = source_of(place, dc, b, a, z, False)
            target = whole.at[:, pl.ds(mult(d * di, di), di), pl.ds(mult(m * cols, cols), cols)]
            shards.append(pltpu.make_async_copy(piece.at[z], target, sems.at[slot, z]))
            shards[-1].start()
    return rows, shards


def conv_forward(place, x0, x1, x2, x3, vec, *rest):
    pieces = rest[:8]
    w_out, x_out, na_out, conv_out, bias_out, nf, nab, whole, extra, sems, x_sem = rest[8:]
    full = vec.shape[1]
    seq, own = x_out.shape[0], x0.shape[1]
    length = place[2]
    blocks = place[3]

    x_parts = (x0, x1, x2, x3)
    rows, shards = fetch(place, x_parts, x_out, x_sem.at[0], pieces, whole, sems)
    extras = [
        pltpu.make_async_copy(part.at[pl.ds(seq, extra.shape[1]), :], extra.at[k], x_sem.at[1, k])
        for k, part in enumerate(x_parts)
    ]
    for copy in extras:
        copy.start()
    for copy in rows + extras:
        copy.wait()
    for k in range(len(x_parts)):
        values = extra[k].astype(f32)
        units = values.shape[0] // 4
        bias_out[place[1] ^ k] = (values[0:units] + values[units : 2 * units]) + values[
            2 * units : 3 * units
        ]

    nf[...] = jnp.zeros_like(nf)
    na_out[...] = jnp.zeros_like(na_out)
    conv_out[...] = jnp.zeros_like(conv_out)
    gain = vec[0:1, :]
    shift = vec[1:2, :]

    def norm_step(i, _):
        rows = pl.ds(mult(i * 128, 128), 128)
        scaled, _ = norm_parts(x_out[rows, :].astype(f32))
        nf[pl.ds(mult(i * 128 + REACH, 8), 128), :] = scaled * gain + shift
        return 0

    lax.fori_loop(0, blocks * (ROWS // 128), norm_step, 0)
    padded = nab.shape[1]

    def shift_step(i, _):
        row = mult(i * 64, 64)
        nab[0, pl.ds(row, 64), :] = nf[pl.ds(row, 64), :].astype(bf16)
        nab[1, pl.ds(row, 64), :] = nf[pl.ds(mult(row + 8, 8), 64), :].astype(bf16)
        return 0

    lax.fori_loop(0, padded // 64, shift_step, 0)
    for copy in shards:
        copy.wait()
    w_copy = pltpu.make_async_copy(whole, w_out, x_sem.at[2, 0])
    w_copy.start()

    def conv_step(i, _):
        row = mult(i * ROWS, ROWS)
        na_out[pl.ds(row, ROWS), :] = nab[0, pl.ds(mult(row + REACH, 32), ROWS), :]
        window = jnp.concatenate(
            [
                nab[t & 1, pl.ds(mult(row + DILATION * (t - (t & 1)), 16), ROWS), :]
                for t in range(KERNEL)
            ],
            axis=1,
        )
        weights = whole[...].reshape(KERNEL * full, full)
        conv_out[pl.ds(row, ROWS), :] = dot(window, weights) + vec[2:3, :]
        return 0

    lax.fori_loop(0, blocks, conv_step, 0)
    w_copy.wait()


def ffn(place, x_full, conv_out, c0, c1, c2, c3, vec, hbias, *rest):
    pieces = rest[:8]
    block_out, resid_out, cab, keep, give, vgrad, hbgrad = rest[8:15]
    whole, cot, act, hg, sec, mg, cf, sems, c_sem = rest[15:]
    wh, wo = whole.at[0], whole.at[1]
    seq, full = x_full.shape
    hidden = hbias.shape[1]
    di, part = pieces[0].shape[2:]
    own = c0.shape[1]
    blocks = place[3]

    rows, shards = fetch(place, (c0, c1, c2, c3), cot, c_sem.at[0], pieces, whole, sems)
    vgrad[...] = jnp.zeros_like(vgrad)
    hbgrad[...] = jnp.zeros_like(hbgrad)
    cf[...] = jnp.zeros_like(cf)
    for copy in rows + shards:
        copy.wait()

    def out_store(rows, values):
        for m in range(full // own):
            block_out[place[1] ^ m, rows, :] = values[:, m * own : (m + 1) * own]

    def row_step(i, _):
        rows = pl.ds(mult(i * ROWS, ROWS), ROWS)
        conv = conv_out[rows, :]
        residual = x_full[rows, :].astype(f32) + conv * phi_of(conv)
        s, inverse = norm_parts(residual)
        second = (s * vec[3:4, :] + vec[4:5, :]).astype(bf16)
        sec[rows, :] = second
        grad = cot[rows, :]
        mg[rows, :] = grad
        for j in range(hidden // 512):
            cols = slice(j * 512, (j + 1) * 512)
            h = dot(second, wh[:, cols]) + hbias[0:1, cols]
            phi = phi_of(h)
            act[rows, cols] = (h * phi).astype(bf16)
            hidden_grad = (dot(grad, wo[:, cols]) * slope_of(h, phi)).astype(bf16)
            hg[rows, cols] = hidden_grad
            hbgrad[0:1, cols] += jnp.sum(hidden_grad.astype(f32), axis=0, keepdims=True)
        mixed = dot(act[rows, :], wo[...], NT)
        out_store(rows, (residual + (mixed + vec[5:6, :])).astype(bf16))
        second_grad = dot(hg[rows, :], wh[...], NT)
        up = grad.astype(f32)
        vgrad[3:4, :] += jnp.sum(second_grad * s, axis=0, keepdims=True)
        vgrad[4:5, :] += jnp.sum(second_grad, axis=0, keepdims=True)
        vgrad[5:6, :] += jnp.sum(up, axis=0, keepdims=True)
        resid_grad = up + norm_back(second_grad * vec[3:4, :], s, inverse)
        resid_out[rows, :] = resid_grad
        conv = conv_out[rows, :]
        conv_grad = (resid_grad * slope_of(conv, phi_of(conv))).astype(bf16)
        rounded = conv_grad.astype(f32)
        cf[pl.ds(mult(i * ROWS + REACH, 8), ROWS), :] = rounded
        vgrad[2:3, :] += jnp.sum(rounded, axis=0, keepdims=True)
        return 0

    def idle_step(i, _):
        rows = pl.ds(mult(i * ROWS, ROWS), ROWS)
        out_store(rows, x_full[rows, :])
        resid_out[rows, :] = cot[rows, :].astype(f32)
        for ref in (sec, mg):
            ref[rows, :] = jnp.zeros((ROWS, full), bf16)
        for ref in (act, hg):
            ref[rows, :] = jnp.zeros((ROWS, hidden), bf16)
        return 0

    lax.fori_loop(0, blocks, row_step, 0)
    lax.fori_loop(blocks, seq // ROWS, idle_step, 0)

    def shift_step(i, _):
        row = mult(i * 64, 64)
        cab[0, pl.ds(row, 64), :] = cf[pl.ds(row, 64), :].astype(bf16)
        cab[1, pl.ds(row, 64), :] = cf[pl.ds(mult(row + 8, 8), 64), :].astype(bf16)
        return 0

    lax.fori_loop(0, cab.shape[1] // 64, shift_step, 0)

    sec_t = sec[...].T
    mg_t = mg[...].T
    for m in range(hidden // part):
        cols = slice(m * part, (m + 1) * part)
        for w, (left, right) in enumerate(((sec_t, hg), (mg_t, act))):
            value = dot(left, right[:, cols]).astype(bf16)

            def store(ref, index, d):
                ref[(*index, w)] = value[d * di : (d + 1) * di, :]

            store_shares(place, keep, give, m, False, full // di, store)


def shifted_rows(cab, u, row, count):
    odd = u & 1
    return cab[odd, pl.ds(mult(row + (u - odd) * DILATION, 16), count), :]


def conv_weight_grad(place, na, cab, keep, give):
    seq, full = na.shape
    taps, di, own = keep.shape[3:]
    na_t = na[...].T

    def tap_step(t, _):
        value = dot(na_t, shifted_rows(cab, KERNEL - 1 - t, 0, seq)).astype(bf16)
        for m in range(full // own):

            def store(ref, index, d):
                ref[(*index, t)] = value[d * di : (d + 1) * di, m * own : (m + 1) * own]

            store_shares(place, keep, give, m, False, full // di, store)
        return 0

    lax.fori_loop(0, taps, tap_step, 0)


def conv_backward(place, x_full, cab, resid, w, vec, in_grad, vgrad):
    seq, full = x_full.shape
    own = in_grad.shape[2]
    blocks = place[3]
    vgrad[...] = jnp.zeros_like(vgrad)

    def in_store(rows, values):
        values = values.astype(bf16)
        for m in range(full // own):
            in_grad[place[1] ^ m, rows, :] = values[:, m * own : (m + 1) * own]

    def row_step(i, _):
        row = mult(i * ROWS, ROWS)
        rows = pl.ds(row, ROWS)
        total = jnp.zeros((ROWS, full), f32)
        for t in range(KERNEL):
            shifted = shifted_rows(cab, KERNEL - 1 - t, row, ROWS)
            total = total + dot(shifted, w[t], NT)
        s, inverse = norm_parts(x_full[rows, :].astype(f32))
        vgrad[0:1, :] += jnp.sum(total * s, axis=0, keepdims=True)
        vgrad[1:2, :] += jnp.sum(total, axis=0, keepdims=True)
        in_store(rows, resid[rows, :] + norm_back(total * vec[0:1, :], s, inverse))
        return 0

    def idle_step(i, _):
        rows = pl.ds(mult(i * ROWS, ROWS), ROWS)
        in_store(rows, resid[rows, :])
        return 0

    lax.fori_loop(0, blocks, row_step, 0)
    lax.fori_loop(blocks, seq // ROWS, idle_step, 0)


def tie(*values):
    return lax.optimization_barrier(values)


def call(kernel, place, args, outs, scratch, flops, mib, far=(), far_out=()):
    near = pl.BlockSpec(memory_space=pltpu.VMEM)
    left = pl.BlockSpec(memory_space=pl.ANY)
    moved = sum(a.size * a.dtype.itemsize for a in (*args, *outs))
    return pl.pallas_call(
        kernel,
        out_shape=outs,
        in_specs=[pl.BlockSpec(memory_space=pltpu.SMEM)]
        + [left if i in far else near for i in range(len(args))],
        out_specs=[left if i in far_out else near for i in range(len(outs))],
        scratch_shapes=scratch,
        compiler_params=pltpu.CompilerParams(vmem_limit_bytes=mib * 2**20),
        cost_estimate=pl.CostEstimate(flops=flops, bytes_accessed=moved, transcendentals=0),
    )(place, *args)


def adam_step(weight, first_mom, second, gradient, clip_scale, step_rate, decay_rate):
    clipped = gradient * clip_scale
    first_new = BETA_ONE * first_mom + (1.0 - BETA_ONE) * clipped
    second_new = BETA_TWO * second + (1.0 - BETA_TWO) * clipped * clipped
    update_dir = (
        first_new
        / (1.0 - BETA_ONE**STEP)
        / (jnp.sqrt(second_new / (1.0 - BETA_TWO**STEP)) + ADAM_EPS)
    )
    return (weight - step_rate * (update_dir + decay_rate * weight), first_new, second_new)


def square_sum(values):
    return jnp.sum(values * values)


def per_device(
    ndp,
    nmp,
    inputs,
    cotangent,
    lengths,
    conv_master,
    hidden_master,
    output_master,
    conv_first,
    hidden_first,
    output_first,
    conv_second,
    hidden_second,
    output_second,
    vectors,
    vector_first,
    vector_second,
    hidden_bias,
    bias_first,
    bias_second,
):
    axes = ("dp", "mp")
    nz = ndp // 2
    seq, own = inputs.shape[1:]
    full = vectors.shape[1]
    part = hidden_bias.shape[0]
    hidden = part * nmp
    di = full // ndp
    dp, mp = lax.axis_index("dp"), lax.axis_index("mp")

    def perm(move):
        pairs = []
        for i in range(ndp * nmp):
            d, m = divmod(i, nmp)
            z, x, y, c = move(d >> 1, d & 1, m >> 1, m & 1)
            pairs.append((i, (z * 2 + x) * nmp + y * 2 + c))
        return pairs

    across_z = [perm(lambda z, x, y, c, k=k: (z ^ k, x, y, c)) for k in range(nz)]
    step_x = perm(lambda z, x, y, c: (z, x ^ 1, y, c))
    step_y = perm(lambda z, x, y, c: (z, x, y ^ 1, c))
    step_c = perm(lambda z, x, y, c: (z, x, y, c ^ 1))
    step_xy = perm(lambda z, x, y, c: (z, x ^ 1, y, c) if c == 0 else (z, x, y ^ 1, c))
    step_yx = perm(lambda z, x, y, c: (z, x, y ^ 1, c) if c == 0 else (z, x ^ 1, y, c))
    within = [[(i, i ^ k) for i in range(nmp)] for k in range(nmp)]

    def send(values, pairs):
        return lax.ppermute(values, axes, pairs)

    def gather_z(shard):
        return [shard] + [send(shard, across_z[k]) for k in range(1, nz)]

    def add(*terms):
        total = terms[0].astype(f32)
        for term in terms[1:]:
            total = total + term.astype(f32)
        return total

    def scatter_b(k, r):
        return add(k[1], r[1]).astype(bf16)

    def scatter_a(k, r, rb):
        return add(k[0, 1], r[0, 1], rb[1]).astype(bf16)

    def scatter_z(k, r, rb, ra):
        total = add(k[0, 0, 0], r[0, 0, 0], rb[0, 0], ra[0])
        for j in range(1, nz):
            part = add(k[0, 0, j], r[0, 0, j], rb[0, j], ra[j]).astype(bf16)
            total = total + send(part, across_z[j]).astype(f32)
        return total

    def take_windows(values, extra=None):
        blocks = [lax.dynamic_index_in_dim(values, mp ^ k, 0, False) for k in range(nmp)]
        if extra is not None:
            blocks = [jnp.concatenate([block, extra]) for block in blocks]
        return blocks

    def swap(blocks):
        return [blocks[0]] + [lax.ppermute(blocks[k], "mp", within[k]) for k in range(1, nmp)]

    def in_order(pieces):
        for bit in range(nmp.bit_length() - 1):
            odd = ((mp >> bit) & 1) == 1
            pieces = [jnp.where(odd, pieces[k ^ (1 << bit)], pieces[k]) for k in range(nmp)]
        return jnp.stack(pieces)

    def all_sum(values, other):
        values = values + send(values, step_c)
        step = 1
        while step < nz:
            values = values + send(values, across_z[step])
            step *= 2
        values = values + send(values, step_x)
        values, other = tie(values, other)
        return values + send(values, step_y), other

    length = lax.dynamic_index_in_dim(lengths, mp, 0, False)
    place = jnp.stack([dp, mp, length, length // ROWS]).astype(jnp.int32)
    exact, rest = [], hidden_bias
    for _ in range(3):
        exact.append(lax.reduce_precision(rest, 8, 7))
        rest = rest - exact[-1]
    exact.append(jnp.zeros_like(rest))
    exact = jnp.concatenate(exact).reshape(4 * part // own, own).astype(bf16)
    vec = jnp.concatenate([vectors, jnp.zeros((2, full), f32)])
    ffn_shard = jnp.stack([hidden_master.astype(bf16), output_master.astype(bf16).T])

    x_blocks = take_windows(inputs, exact)
    *x_blocks, conv_shard = tie(*x_blocks, conv_master.astype(bf16))
    x_parts = swap(x_blocks)
    conv_z = gather_z(conv_shard)
    *tied, ffn_shard = tie(*x_parts, *conv_z, ffn_shard)
    x_parts, conv_z = tied[:nmp], jnp.stack(tied[nmp:])
    conv_a, conv_b = send(conv_z, step_xy), send(conv_z, step_yx)
    ffn_z = gather_z(ffn_shard)
    conv_z, conv_a, conv_b, *ffn_z = tie(conv_z, conv_a, conv_b, *ffn_z)
    ffn_z = jnp.stack(ffn_z)
    conv_ab = send(conv_a, step_yx)
    conv_far = [send(part_of, step_c) for part_of in (conv_z, conv_a, conv_b)]
    conv_ab, cotangent, *conv_far = tie(conv_ab, cotangent, *conv_far)
    conv_parts = [conv_z, conv_a, conv_b, conv_ab, *conv_far, send(conv_ab, step_c)]
    ffn_a, ffn_b = send(ffn_z, step_xy), send(ffn_z, step_yx)
    c_parts = swap(take_windows(cotangent))

    S = jax.ShapeDtypeStruct
    padded = seq + 2 * REACH
    ffn_a, *x_parts = tie(ffn_a, *x_parts)
    w_full, x_full, normed, conv_out, bias_all = call(
        conv_forward,
        place,
        (*x_parts, vec, *conv_parts),
        (
            S((KERNEL, full, full), bf16),
            S((seq, full), bf16),
            S((seq, full), bf16),
            S((seq, full), f32),
            S((nmp, part // own, own), f32),
        ),
        [
            pltpu.VMEM((padded + 8, full), f32),
            pltpu.VMEM((2, padded, full), bf16),
            pltpu.VMEM((KERNEL, full, full), bf16),
            pltpu.VMEM((nmp, 4 * part // own, own), bf16),
            pltpu.SemaphoreType.DMA((8, nz)),
            pltpu.SemaphoreType.DMA((3, nmp)),
        ],
        2 * seq * KERNEL * full * full,
        24,
        (0, 1, 2, 3, *range(5, 13)),
        (0,),
    )
    ffn_ab = send(ffn_a, step_yx)
    *tied, conv_out = tie(ffn_z, ffn_a, ffn_b, ffn_ab, *c_parts, conv_out)
    ffn_parts, c_parts = tied[:4], tied[4:]
    ffn_parts += [send(part_of, step_c) for part_of in ffn_parts]
    block_rel, resid_grad, conv_grad, ffn_keep, ffn_give, vgrad_two, bias_grad = call(
        ffn,
        place,
        (x_full, conv_out, *c_parts, vec, bias_all.reshape(1, hidden), *ffn_parts),
        (
            S((nmp, seq, own), bf16),
            S((seq, full), f32),
            S((2, padded, full), bf16),
            *(S((2, 2, nz, 2, di, part), bf16),) * 2,
            S((8, full), f32),
            S((1, hidden), f32),
        ),
        [
            pltpu.VMEM((2, full, hidden), bf16),
            pltpu.VMEM((seq, full), bf16),
            pltpu.VMEM((seq, hidden), bf16),
            pltpu.VMEM((seq, hidden), bf16),
            pltpu.VMEM((seq, full), bf16),
            pltpu.VMEM((seq, full), bf16),
            pltpu.VMEM((padded + 8, full), f32),
            pltpu.SemaphoreType.DMA((8, nz)),
            pltpu.SemaphoreType.DMA((1, nmp)),
        ],
        12 * seq * hidden * full,
        44,
        (2, 3, 4, 5, *range(8, 16)),
    )
    ffn_r = send(ffn_give, step_c)
    ffn_sum, conv_grad = tie(scatter_b(ffn_keep, ffn_r), conv_grad)
    ffn_rb = send(ffn_sum, step_yx)
    conv_keep, conv_give = call(
        conv_weight_grad,
        place,
        (normed, conv_grad),
        (S((2, 2, nz, KERNEL, di, own), bf16),) * 2,
        [],
        2 * seq * KERNEL * full * full,
        16,
    )
    conv_give, ffn_rb, conv_grad = tie(conv_give, ffn_rb, conv_grad)
    conv_r = send(conv_give, step_c)
    ffn_ra = send(scatter_a(ffn_keep, ffn_r, ffn_rb), step_xy)
    in_rel, vgrad_one = call(
        conv_backward,
        place,
        (x_full, conv_grad, resid_grad, w_full, vec),
        (S((nmp, seq, own), bf16), S((8, full), f32)),
        [],
        1,
        16,
    )
    conv_sum, ffn_ra, in_rel = tie(scatter_b(conv_keep, conv_r), ffn_ra, in_rel)
    conv_rb = send(conv_sum, step_yx)
    ffn_share = scatter_z(ffn_keep, ffn_r, ffn_rb, ffn_ra)
    conv_sum, ffn_share = tie(scatter_a(conv_keep, conv_r, conv_rb), ffn_share)
    conv_ra = send(conv_sum, step_xy)
    conv_ra, in_rel, block_rel = tie(conv_ra, in_rel, block_rel)
    conv_share = scatter_z(conv_keep, conv_r, conv_rb, conv_ra)
    out_parts = [jnp.stack([block_rel[k], in_rel[k]]) for k in range(nmp)]
    for k in range(1, nmp):
        out_parts[k] = lax.ppermute(out_parts[k], "mp", within[k])
    conv_share, *out_parts[:-1] = tie(conv_share, *out_parts[:-1])

    squares = square_sum(conv_share) + square_sum(ffn_share)
    small = jnp.concatenate(
        [
            (vgrad_one + vgrad_two)[:6],
            bias_grad.reshape(hidden // full, full),
            jnp.broadcast_to(squares, (1, full)),
        ]
    )
    small, out_parts[-1] = all_sum(small, out_parts[-1])
    outputs = in_order(out_parts)
    block_output, input_grad = outputs[:, 0], outputs[:, 1].astype(f32)
    vector_sum, bias_sum = small[:6], small[6:-1].reshape(hidden)
    hidden_share, output_share = ffn_share[0], ffn_share[1].T
    grad_norm = jnp.sqrt(small[-1, 0] + square_sum(small[:-1]))
    clip_scale = jnp.minimum(1.0, CLIP_NORM / (grad_norm + 1e-06))
    bias_share = lax.dynamic_slice_in_dim(bias_sum, mp * part, part, 0)
    matrices = (
        (conv_master, conv_first, conv_second, conv_share),
        (hidden_master, hidden_first, hidden_second, hidden_share),
        (output_master, output_first, output_second, output_share),
    )
    small_ones = (
        (vectors, vector_first, vector_second, vector_sum),
        (hidden_bias, bias_first, bias_second, bias_share),
    )
    updated = [adam_step(*m, clip_scale, MATRIX_RATE, WEIGHT_DECAY) for m in matrices]
    updated += [adam_step(*m, clip_scale, VECTOR_RATE, 0.0) for m in small_ones]
    return (block_output, input_grad, grad_norm, *(leaf for new in updated for leaf in new))


def solution(mesh):
    rows = P("dp", None, "mp")
    conv = P(None, "dp", "mp")
    hid = P("dp", "mp")
    out = P("mp", "dp")
    return jax.shard_map(
        functools.partial(per_device, mesh.shape["dp"], mesh.shape["mp"]),
        mesh=mesh,
        in_specs=(rows, rows, P("dp"), *(conv, hid, out) * 3, *(P(),) * 3, *(P("mp"),) * 3),
        out_specs=(
            rows,
            rows,
            P(),
            *(conv,) * 3,
            *(hid,) * 3,
            *(out,) * 3,
            *(P(),) * 3,
            *(P("mp"),) * 3,
        ),
        check_vma=False,
    )
```

time: 270 us -> 228 us (0.84)
  starting transfers between devices: 68.8 us -> 51 us
  local copies, waits for them, and re-layouts: 22.1 us -> 12.5 us
  other arithmetic: 28.5 us -> 21.3 us
  Pallas kernels: 38 us -> 32.2 us
    ppermute x15 -> x9, waiting for transfers between devices: 36.5 us -> 13.2 us  [the longest x6 13.2 us: swap(): lax.ppermute(blocks[k], 'mp', within[k])]
    ppermute x42 -> x37, waiting for transfers between devices: 67.1 us -> 89.4 us  [send(): return lax.ppermute(values, axes, pairs)]
    ppermute x42 -> x37, starting transfers between devices: 57.7 us -> 45.9 us  [send(): return lax.ppermute(values, axes, pairs)]
    squeeze x8 -> x2, local copies, waits for them, and re-layouts: 9.63 us -> 2.58 us  [take_windows(): lax.dynamic_index_in_dim(values, mp ^ k, 0, False)]
    add x10 -> x5, other arithmetic: 8.69 us -> 2.05 us  [the longest x2 1.96 us: scatter_z(): total = total + send(part, across_z[j]).astype(f32)]
    ppermute x15 -> x9, starting transfers between devices: 11.1 us -> 5.15 us  [the longest x6 3.68 us: swap(): lax.ppermute(blocks[k], 'mp', within[k])]
    pallas_call x3 -> x4, Pallas kernels: 38 us -> 32.2 us  [call(): pl.pallas_call(kernel, out_shape=outs, in_specs=[pl.BlockSpec(memory_spac...]
    convert_element_type x4 -> x8, other arithmetic: 3 us -> 7.08 us  [the longest x2 2 us: scatter_b(): return add(k[1], r[1]).astype(bf16)]
  transfers between devices with their start and end apart: 57 -> 46, of which waited for: 23 -> 24; matrix products, arithmetic and copies ran while one was open for 12% -> 7% of each run, Pallas kernels for 8% -> 7%
where the time goes in v2:
time: 228 us; the launch traced here: 227 us
  waiting for transfers between devices  103 us (45%)
  starting transfers between devices  51 us (22%)
  Pallas kernels  32.2 us (14%)
  other arithmetic  21.3 us (9%)
  local copies, waits for them, and re-layouts  12.5 us (5%)
  between operations  7.67 us (3%)
    ppermute x37, waiting for transfers between devices, send(): return lax.ppermute(values, axes, pairs)  89.4 us
    ppermute x37, starting transfers between devices, send(): return lax.ppermute(values, axes, pairs)  45.9 us
    pallas_call x4, Pallas kernels, call(): pl.pallas_call(kernel, out_shape=outs, in_specs=[pl.BlockSpec(memory_spac...  32.2 us
    ppermute x6, waiting for transfers between devices, swap(): lax.ppermute(blocks[k], 'mp', within[k])  13.2 us
    unnamed x76, local copies, waits for them, and re-layouts  6.28 us
  transfers between devices with their start and end apart: 46, of which 24 were waited for; matrix products, arithmetic and copies ran while one was open for 7% of the time, Pallas kernels for 7%

profile of v2, /device:TPU:0, one launch (start us, length us, event | category | flops | bytes accessed | tf_op | source)
XLA Modules:
  0.0 227.3 jit_solution(1479540170300238076)
XLA Ops:
  3.4 3.1 %collective-permute-start.3 = (bf16[9,64,128]{2,1,0:T(8,128)(2,1)S(1)}, bf16[9,64,128]{2,1,0:T(8,128)(2,1)S(1)}, u32[]{:S(2)}, u32[]{:S(2)}) collective-permute-start(bf16[9,64,128]{2,1,0:T(8,128)(2,1)S(1)} %convert_element_type.274), channel_id=1, source_target_pairs={{0,8},{1,9},{2,10},{3,11},{4,12},{5,13},{6,14},{7,15},{8,0},{9,1},... | collective-permute-start | bytes 442376 | tf_op jit(solution)/shard_map/ppermute | solution.py:416
  6.5 2.6 %collective-permute-start.4 = (bf16[9,64,128]{2,1,0:T(8,128)(2,1)S(1)}, bf16[9,64,128]{2,1,0:T(8,128)(2,1)S(1)}, u32[]{:S(2)}, u32[]{:S(2)}) collective-permute-start(bf16[9,64,128]{2,1,0:T(8,128)(2,1)S(1)} %convert_element_type.274), channel_id=1, source_target_pairs={{0,16},{1,17},{2,18},{3,19},{4,20},{5,21},{6,22},{7,23},{8,24},{9,... | collective-permute-start | bytes 442376 | tf_op jit(solution)/shard_map/ppermute | solution.py:416
  12.4 8.1 %collective-permute-done.4 = bf16[9,64,128]{2,1,0:T(8,128)(2,1)S(1)} collective-permute-done((bf16[9,64,128]{2,1,0:T(8,128)(2,1)S(1)}, bf16[9,64,128]{2,1,0:T(8,128)(2,1)S(1)}, u32[]{:S(2)}, u32[]{:S(2)}) %collective-permute-start.4) | collective-permute-done | bytes 147488 | tf_op jit(solution)/shard_map/ppermute | solution.py:416
  21.2 2.0 collective-permute-done.2.x3
  24.0 1.8 collective-permute-start.6
  28.0 3.5 %collective-permute-start.9 = (bf16[2,64,512]{2,1,0:T(8,128)(2,1)S(1)}, bf16[2,64,512]{2,1,0:T(8,128)(2,1)S(1)}, u32[]{:S(2)}, u32[]{:S(2)}) collective-permute-start(bf16[2,64,512]{2,1,0:T(8,128)(2,1)S(1)} %pad_maximum_fusion.7), channel_id=1, source_target_pairs={{0,16},{1,17},{2,18},{3,19},{4,20},{5,21},{6,22},{7,23},{8,24},{9,... | collective-permute-start | bytes 393224 | tf_op jit(solution)/shard_map/ppermute | solution.py:416
  31.7 2.3 %collective-permute-done.8 = bf16[2,64,512]{2,1,0:T(8,128)(2,1)S(1)} collective-permute-done((bf16[2,64,512]{2,1,0:T(8,128)(2,1)S(1)}, bf16[2,64,512]{2,1,0:T(8,128)(2,1)S(1)}, u32[]{:S(2)}, u32[]{:S(2)}) %collective-permute-start.8) | collective-permute-done | bytes 131104 | tf_op jit(solution)/shard_map/ppermute | solution.py:416
  34.0 7.4 %collective-permute-done.9 = bf16[2,64,512]{2,1,0:T(8,128)(2,1)S(1)} collective-permute-done((bf16[2,64,512]{2,1,0:T(8,128)(2,1)S(1)}, bf16[2,64,512]{2,1,0:T(8,128)(2,1)S(1)}, u32[]{:S(2)}, u32[]{:S(2)}) %collective-permute-start.9) | collective-permute-done | bytes 131104 | tf_op jit(solution)/shard_map/ppermute | solution.py:416
  43.6 13.4 %collective-permute-done.12.rest_3_ = bf16[4,9,64,128]{3,2,1,0:T(8,128)(2,1)S(1)} collective-permute-done((bf16[4,9,64,128]{3,2,1,0:T(8,128)(2,1)S(1)}, bf16[4,9,64,128]{3,2,1,0:T(8,128)(2,1)S(1)}, u32[]{:S(2)}, u32[]{:S(2)}) %collective-permute-start.12) | collective-permute-done | bytes 589856 | tf_op jit(solution)/shard_map/ppermute | solution.py:416
  63.7 2.0 collective-permute-start.18
  69.8 4.8 %shard_map.313 = (bf16[9,512,512]{2,1,0:T(8,128)(2,1)S(1)}, bf16[1024,512]{1,0:T(8,128)(2,1)S(1)}, bf16[1024,512]{1,0:T(8,128)(2,1)S(1)}, f32[1024,512]{1,0:T(8,128)S(1)}, f32[4,4,128]{2,1,0:T(4,128)S(1)}) custom-call(s32[4]{0:T(128)S(1)} %pad_add_fusion.place, bf16[1040,128]{1,0:T(8,128)(2,1)S(1)} %concatenate.37.x0, ...), custom_call_target="tpu_custom_call" | custom-call | flops 4831838208 | bytes 14721024 | tf_op jit(solution)/shard_map/pallas_call | solution.py:340
  76.0 10.9 %collective-permute-done.20.c2 = bf16[1024,128]{1,0:T(8,128)(2,1)S(1)} collective-permute-done((bf16[1024,128]{1,0:T(8,128)(2,1)S(1)}, bf16[1024,128]{1,0:T(8,128)(2,1)S(1)}, u32[]{:S(2)}, u32[]{:S(2)}) %collective-permute-start.20) | collective-permute-done | bytes 262176 | tf_op jit(solution)/shard_map/ppermute | solution.py:447
  87.2 2.3 %collective-permute-start.22 = (bf16[4,2,64,512]{3,2,1,0:T(8,128)(2,1)S(1)}, bf16[4,2,64,512]{3,2,1,0:T(8,128)(2,1)S(1)}, u32[]{:S(2)}, u32[]{:S(2)}) collective-permute-start(bf16[4,2,64,512]{3,2,1,0:T(8,128)(2,1)S(1)} %pad_maximum_fusion.2.rest_0_), channel_id=1, source_target_pairs={{0,1},{1,0},{2,3},{3,2},{4,5},{5,4},{6,7},{7,6},{8,9},{9,8},{10,11... | collective-permute-start | bytes 1572872 | tf_op jit(solution)/shard_map/ppermute | solution.py:416
  93.3 16.8 %shard_map.314 = (bf16[4,1024,128]{2,1,0:T(8,128)(2,1)S(1)}, f32[1024,512]{1,0:T(8,128)S(1)}, bf16[2,1088,512]{2,1,0:T(8,128)(2,1)}, bf16[2,2,4,2,64,512]{5,4,3,...) custom-call(s32[4]{0:T(128)S(1)} %pad_add_fusion.place, ...), custom_call_target="tpu_custom_call" | custom-call | flops 12884901888 | bytes 18006016 | tf_op jit(solution)/shard_map/pallas_call | solution.py:340
  110.6 4.0 %collective-permute-done.26 = bf16[2,2,4,2,64,512]{5,4,3,2,1,0:T(8,128)(2,1)S(1)} collective-permute-done((bf16[2,2,4,2,64,512]{5,4,3,2,1,0:T(8,128)(2,1)}, bf16[2,2,4,2,64,512]{5,4,3,2,1,0:T(8,128)(2,1)S(1)}, u32[]{:S(2)}, u32[]{:S(2)}) %collective-permute-start.26) | collective-permute-done | bytes 2097184 | tf_op jit(solution)/shard_map/ppermute | solution.py:416
  116.3 8.3 %shard_map.315 = (bf16[2,2,4,9,64,128]{5,4,3,2,1,0:T(8,128)(2,1)S(1)}, bf16[2,2,4,9,64,128]{5,4,3,2,1,0:T(8,128)(2,1)S(1)}) custom-call(s32[4]{0:T(128)S(1)} %pad_add_fusion.place, bf16[1024,512]{1,0:T(8,128)(2,1)S(1)} %get-tuple-element.123.na, bf16[2,1088,512]{2,1,0:T(8,128)(2,1)S(1)} %copy-done), custom_call_target="tpu_custom_call" | custom-call | flops 4831838208 | bytes 7995392 | tf_op jit(solution)/shard_map/pallas_call | solution.py:340
  124.6 6.4 %collective-permute-done.27 = bf16[2,4,2,64,512]{4,3,2,1,0:T(8,128)(2,1)S(1)} collective-permute-done((bf16[2,4,2,64,512]{4,3,2,1,0:T(8,128)(2,1)S(1)}, bf16[2,4,2,64,512]{4,3,2,1,0:T(8,128)(2,1)S(1)}, u32[]{:S(2)}, u32[]{:S(2)}) %collective-permute-start.27) | collective-permute-done | bytes 1048608 | tf_op jit(solution)/shard_map/ppermute | solution.py:416
  131.4 2.3 shard_map.316
  133.7 1.8 collective-permute-done.28
  136.0 4.5 %collective-permute-done.29 = bf16[4,2,64,512]{3,2,1,0:T(8,128)(2,1)S(1)} collective-permute-done((bf16[4,2,64,512]{3,2,1,0:T(8,128)(2,1)S(1)}, bf16[4,2,64,512]{3,2,1,0:T(8,128)(2,1)S(1)}, u32[]{:S(2)}, u32[]{:S(2)}) %collective-permute-start.29) | collective-permute-done | bytes 524320 | tf_op jit(solution)/shard_map/ppermute | solution.py:416
  140.8 13.2 %collective-permute-start.33 = (bf16[2,64,512]{2,1,0:T(8,128)(2,1)S(1)}, bf16[2,64,512]{2,1,0:T(8,128)(2,1)S(1)}, u32[]{:S(2)}, u32[]{:S(2)}) collective-permute-start(bf16[2,64,512]{2,1,0:T(8,128)(2,1)S(1)} %get-tuple-element.187), channel_id=1, source_target_pairs={{0,24},{1,25},{2,26},{3,27},{4,28},{5,29},{6,30},{7,31},{8,16},{9,... | collective-permute-start | bytes 393224 | tf_op jit(solution)/shard_map/ppermute | solution.py:416
  154.6 3.3 %collective-permute-done.33 = bf16[2,64,512]{2,1,0:T(8,128)(2,1)S(1)} collective-permute-done((bf16[2,64,512]{2,1,0:T(8,128)(2,1)S(1)}, bf16[2,64,512]{2,1,0:T(8,128)(2,1)S(1)}, u32[]{:S(2)}, u32[]{:S(2)}) %collective-permute-start.33) | collective-permute-done | bytes 131104 | tf_op jit(solution)/shard_map/ppermute | solution.py:416
  157.9 6.6 %collective-permute-done.32 = bf16[2,64,512]{2,1,0:T(8,128)(2,1)S(1)} collective-permute-done((bf16[2,64,512]{2,1,0:T(8,128)(2,1)S(1)}, bf16[2,64,512]{2,1,0:T(8,128)(2,1)S(1)}, u32[]{:S(2)}, u32[]{:S(2)}) %collective-permute-start.32) | collective-permute-done | bytes 131104 | tf_op jit(solution)/shard_map/ppermute | solution.py:416
  170.6 6.2 %collective-permute-done.34 = bf16[4,9,64,128]{3,2,1,0:T(8,128)(2,1)} collective-permute-done((bf16[4,9,64,128]{3,2,1,0:T(8,128)(2,1)}, bf16[4,9,64,128]{3,2,1,0:T(8,128)(2,1)}, u32[]{:S(2)}, u32[]{:S(2)}) %collective-permute-start.34) | collective-permute-done | bytes 589856 | tf_op jit(solution)/shard_map/ppermute | solution.py:416
  181.3 3.2 %collective-permute-start.37 = (bf16[9,64,128]{2,1,0:T(8,128)(2,1)S(1)}, bf16[9,64,128]{2,1,0:T(8,128)(2,1)S(1)}, u32[]{:S(2)}, u32[]{:S(2)}) collective-permute-start(bf16[9,64,128]{2,1,0:T(8,128)(2,1)S(1)} %get-tuple-element.184), channel_id=1, source_target_pairs={{0,24},{1,25},{2,26},{3,27},{4,28},{5,29},{6,30},{7,31},{8,16},{9,... | collective-permute-start | bytes 442376 | tf_op jit(solution)/shard_map/ppermute | solution.py:416
  186.6 3.3 %collective-permute-done.37 = bf16[9,64,128]{2,1,0:T(8,128)(2,1)S(1)} collective-permute-done((bf16[9,64,128]{2,1,0:T(8,128)(2,1)S(1)}, bf16[9,64,128]{2,1,0:T(8,128)(2,1)S(1)}, u32[]{:S(2)}, u32[]{:S(2)}) %collective-permute-start.37) | collective-permute-done | bytes 147488 | tf_op jit(solution)/shard_map/ppermute | solution.py:416
  189.9 6.7 %collective-permute-done.36 = bf16[9,64,128]{2,1,0:T(8,128)(2,1)S(1)} collective-permute-done((bf16[9,64,128]{2,1,0:T(8,128)(2,1)S(1)}, bf16[9,64,128]{2,1,0:T(8,128)(2,1)S(1)}, u32[]{:S(2)}, u32[]{:S(2)}) %collective-permute-start.36) | collective-permute-done | bytes 147488 | tf_op jit(solution)/shard_map/ppermute | solution.py:416
  201.5 3.7 %collective-permute-done.41 = f32[11,512]{1,0:T(8,128)S(1)} collective-permute-done((f32[11,512]{1,0:T(8,128)S(1)}, f32[11,512]{1,0:T(8,128)S(1)}, u32[]{:S(2)}, u32[]{:S(2)}) %collective-permute-start.41) | collective-permute-done | bytes 22560 | tf_op jit(solution)/shard_map/ppermute | solution.py:416
  206.4 3.7 %collective-permute-done.42 = f32[11,512]{1,0:T(8,128)S(1)} collective-permute-done((f32[11,512]{1,0:T(8,128)S(1)}, f32[11,512]{1,0:T(8,128)S(1)}, u32[]{:S(2)}, u32[]{:S(2)}) %collective-permute-start.42) | collective-permute-done | bytes 22560 | tf_op jit(solution)/shard_map/ppermute | solution.py:416
  210.1 2.0 collective-permute-start.43
  212.1 1.9 collective-permute-done.43
  217.6 1.9 fusion.3
  (193 shorter events, 55.6 us)
Async XLA Ops:
  3.4 8.9 %collective-permute-start.3 = (bf16[9,64,128]{2,1,0:T(8,128)(2,1)S(1)}, bf16[9,64,128]{2,1,0:T(8,128)(2,1)S(1)}, u32[]{:S(2)}, u32[]{:S(2)}) collective-permute-start(bf16[9,64,128]{2,1,0:T(8,128)(2,1)S(1)} %convert_element_type.274), channel_id=1, source_target_pairs={{0,8},{1,9},{2,10},{3,11},{4,12},{5,13},{6,14},{7,15},{8,0},{9,1},... | collective-permute-start | bytes 442376 | tf_op jit(solution)/shard_map/ppermute | solution.py:416
  6.5 14.0 %collective-permute-start.4 = (bf16[9,64,128]{2,1,0:T(8,128)(2,1)S(1)}, bf16[9,64,128]{2,1,0:T(8,128)(2,1)S(1)}, u32[]{:S(2)}, u32[]{:S(2)}) collective-permute-start(bf16[9,64,128]{2,1,0:T(8,128)(2,1)S(1)} %convert_element_type.274), channel_id=1, source_target_pairs={{0,16},{1,17},{2,18},{3,19},{4,20},{5,21},{6,22},{7,23},{8,24},{9,... | collective-permute-start | bytes 442376 | tf_op jit(solution)/shard_map/ppermute | solution.py:416
  9.1 11.4 %collective-permute-start.5 = (bf16[9,64,128]{2,1,0:T(8,128)(2,1)S(1)}, bf16[9,64,128]{2,1,0:T(8,128)(2,1)S(1)}, u32[]{:S(2)}, u32[]{:S(2)}) collective-permute-start(bf16[9,64,128]{2,1,0:T(8,128)(2,1)S(1)} %convert_element_type.274), channel_id=1, source_target_pairs={{0,24},{1,25},{2,26},{3,27},{4,28},{5,29},{6,30},{7,31},{8,16},{9,... | collective-permute-start | bytes 442376 | tf_op jit(solution)/shard_map/ppermute | solution.py:416
  9.1 11.4 %collective-permute-start = (bf16[1040,128]{1,0:T(8,128)(2,1)S(1)}, bf16[1040,128]{1,0:T(8,128)(2,1)S(1)}, u32[]{:S(2)}, u32[]{:S(2)}) collective-permute-start(bf16[1040,128]{1,0:T(8,128)(2,1)S(1)} %concatenate.38), channel_id=1, source_target_pairs={{0,1},{1,0},{2,3},{3,2},{4,5},{5,4},{6,7},{7,6},{8,9},{9,8},{10,11... | collective-permute-start | bytes 798728 | tf_op jit(solution)/shard_map/ppermute | solution.py:447
  9.1 11.4 %collective-permute-start.1 = (bf16[1040,128]{1,0:T(8,128)(2,1)S(1)}, bf16[1040,128]{1,0:T(8,128)(2,1)S(1)}, u32[]{:S(2)}, u32[]{:S(2)}) collective-permute-start(bf16[1040,128]{1,0:T(8,128)(2,1)S(1)} %concatenate.39), channel_id=1, source_target_pairs={{0,2},{1,3},{2,0},{3,1},{4,6},{5,7},{6,4},{7,5},{8,10},{9,11},{10,... | collective-permute-start | bytes 798728 | tf_op jit(solution)/shard_map/ppermute | solution.py:447
  12.3 10.9 %collective-permute-start.2 = (bf16[1040,128]{1,0:T(8,128)(2,1)S(1)}, bf16[1040,128]{1,0:T(8,128)(2,1)S(1)}, u32[]{:S(2)}, u32[]{:S(2)}) collective-permute-start(bf16[1040,128]{1,0:T(8,128)(2,1)S(1)} %concatenate.40), channel_id=1, source_target_pairs={{0,3},{1,2},{2,1},{3,0},{4,7},{5,6},{6,5},{7,4},{8,11},{9,10},{10,... | collective-permute-start | bytes 798728 | tf_op jit(solution)/shard_map/ppermute | solution.py:447
  24.0 17.5 %collective-permute-start.6 = (bf16[4,9,64,128]{3,2,1,0:T(8,128)(2,1)S(1)}, bf16[4,9,64,128]{3,2,1,0:T(8,128)(2,1)S(1)}, u32[]{:S(2)}, u32[]{:S(2)}) collective-permute-start(bf16[4,9,64,128]{3,2,1,0:T(8,128)(2,1)S(1)} %pad_maximum_fusion.1.rest_0_), channel_id=1, source_target_pairs={{0,4},{1,3},{2,6},{3,1},{4,0},{5,7},{6,2},{7,5},{8,12},{9,11},{10,... | collective-permute-start | bytes 1769480 | tf_op jit(solution)/shard_map/ppermute | solution.py:416
  25.8 15.7 %collective-permute-start.7 = (bf16[4,9,64,128]{3,2,1,0:T(8,128)(2,1)S(1)}, bf16[4,9,64,128]{3,2,1,0:T(8,128)(2,1)S(1)}, u32[]{:S(2)}, u32[]{:S(2)}) collective-permute-start(bf16[4,9,64,128]{3,2,1,0:T(8,128)(2,1)S(1)} %pad_maximum_fusion.1.rest_0_), channel_id=1, source_target_pairs={{0,2},{1,5},{2,0},{3,7},{4,6},{5,1},{6,4},{7,3},{8,10},{9,13},{10,... | collective-permute-start | bytes 1769480 | tf_op jit(solution)/shard_map/ppermute | solution.py:416
  28.0 13.5 %collective-permute-start.9 = (bf16[2,64,512]{2,1,0:T(8,128)(2,1)S(1)}, bf16[2,64,512]{2,1,0:T(8,128)(2,1)S(1)}, u32[]{:S(2)}, u32[]{:S(2)}) collective-permute-start(bf16[2,64,512]{2,1,0:T(8,128)(2,1)S(1)} %pad_maximum_fusion.7), channel_id=1, source_target_pairs={{0,16},{1,17},{2,18},{3,19},{4,20},{5,21},{6,22},{7,23},{8,24},{9,... | collective-permute-start | bytes 393224 | tf_op jit(solution)/shard_map/ppermute | solution.py:416
  31.5 10.0 %collective-permute-start.10 = (bf16[2,64,512]{2,1,0:T(8,128)(2,1)S(1)}, bf16[2,64,512]{2,1,0:T(8,128)(2,1)S(1)}, u32[]{:S(2)}, u32[]{:S(2)}) collective-permute-start(bf16[2,64,512]{2,1,0:T(8,128)(2,1)S(1)} %pad_maximum_fusion.7), channel_id=1, source_target_pairs={{0,24},{1,25},{2,26},{3,27},{4,28},{5,29},{6,30},{7,31},{8,16},{9,... | collective-permute-start | bytes 393224 | tf_op jit(solution)/shard_map/ppermute | solution.py:416
  41.5 15.6 %collective-permute-start.12 = (bf16[4,9,64,128]{3,2,1,0:T(8,128)(2,1)S(1)}, bf16[4,9,64,128]{3,2,1,0:T(8,128)(2,1)S(1)}, u32[]{:S(2)}, u32[]{:S(2)}) collective-permute-start(bf16[4,9,64,128]{3,2,1,0:T(8,128)(2,1)S(1)} %collective-permute-done.6.rest_1_), channel_id=1, source_target_pairs={{0,2},{1,5},{2,0},{3,7},{4,6},{5,1},{6,4},{7,3},{8,10},{9,13},{10,... | collective-permute-start | bytes 1769480 | tf_op jit(solution)/shard_map/ppermute | solution.py:416
  42.0 15.8 %collective-permute-start.14 = (bf16[4,9,64,128]{3,2,1,0:T(8,128)(2,1)S(1)}, bf16[4,9,64,128]{3,2,1,0:T(8,128)(2,1)S(1)}, u32[]{:S(2)}, u32[]{:S(2)}) collective-permute-start(bf16[4,9,64,128]{3,2,1,0:T(8,128)(2,1)S(1)} %collective-permute-done.6.rest_1_), channel_id=1, source_target_pairs={{0,1},{1,0},{2,3},{3,2},{4,5},{5,4},{6,7},{7,6},{8,9},{9,8},{10,11... | collective-permute-start | bytes 1769480 | tf_op jit(solution)/shard_map/ppermute | solution.py:416
  42.1 15.0 %collective-permute-start.13 = (bf16[4,9,64,128]{3,2,1,0:T(8,128)(2,1)S(1)}, bf16[4,9,64,128]{3,2,1,0:T(8,128)(2,1)S(1)}, u32[]{:S(2)}, u32[]{:S(2)}) collective-permute-start(bf16[4,9,64,128]{3,2,1,0:T(8,128)(2,1)S(1)} %pad_maximum_fusion.1.rest_0_), channel_id=1, source_target_pairs={{0,1},{1,0},{2,3},{3,2},{4,5},{5,4},{6,7},{7,6},{8,9},{9,8},{10,11... | collective-permute-start | bytes 1769480 | tf_op jit(solution)/shard_map/ppermute | solution.py:416
  42.6 16.1 %collective-permute-start.15 = (bf16[4,9,64,128]{3,2,1,0:T(8,128)(2,1)S(1)}, bf16[4,9,64,128]{3,2,1,0:T(8,128)(2,1)S(1)}, u32[]{:S(2)}, u32[]{:S(2)}) collective-permute-start(bf16[4,9,64,128]{3,2,1,0:T(8,128)(2,1)S(1)} %collective-permute-done.7.rest_2_), channel_id=1, source_target_pairs={{0,1},{1,0},{2,3},{3,2},{4,5},{5,4},{6,7},{7,6},{8,9},{9,8},{10,11... | collective-permute-start | bytes 1769480 | tf_op jit(solution)/shard_map/ppermute | solution.py:416
  42.6 21.0 %collective-permute-start.11 = (bf16[4,2,64,512]{3,2,1,0:T(8,128)(2,1)S(1)}, bf16[4,2,64,512]{3,2,1,0:T(8,128)(2,1)}, u32[]{:S(2)}, u32[]{:S(2)}) collective-permute-start(bf16[4,2,64,512]{3,2,1,0:T(8,128)(2,1)S(1)} %pad_maximum_fusion.2.rest_0_), channel_id=1, source_target_pairs={{0,4},{1,3},{2,6},{3,1},{4,0},{5,7},{6,2},{7,5},{8,12},{9,11},{10,... | collective-permute-start | bytes 1572872 | tf_op jit(solution)/shard_map/ppermute | solution.py:416
  63.6 12.4 %collective-permute-start.17 = (bf16[4,2,64,512]{3,2,1,0:T(8,128)(2,1)S(1)}, bf16[4,2,64,512]{3,2,1,0:T(8,128)(2,1)S(1)}, u32[]{:S(2)}, u32[]{:S(2)}) collective-permute-start(bf16[4,2,64,512]{3,2,1,0:T(8,128)(2,1)S(1)} %pad_maximum_fusion.2.rest_0_), channel_id=1, source_target_pairs={{0,2},{1,5},{2,0},{3,7},{4,6},{5,1},{6,4},{7,3},{8,10},{9,13},{10,... | collective-permute-start | bytes 1572872 | tf_op jit(solution)/shard_map/ppermute | solution.py:416
  63.7 23.5 %collective-permute-start.18 = (bf16[4,2,64,512]{3,2,1,0:T(8,128)(2,1)}, bf16[4,2,64,512]{3,2,1,0:T(8,128)(2,1)S(1)}, u32[]{:S(2)}, u32[]{:S(2)}) collective-permute-start(bf16[4,2,64,512]{3,2,1,0:T(8,128)(2,1)} %collective-permute-done.11.rest_1_), channel_id=1, source_target_pairs={{0,2},{1,5},{2,0},{3,7},{4,6},{5,1},{6,4},{7,3},{8,10},{9,13},{10,... | collective-permute-start | bytes 1572872 | tf_op jit(solution)/shard_map/ppermute | solution.py:416
  66.9 9.1 %collective-permute-start.19 = (bf16[1024,128]{1,0:T(8,128)(2,1)S(1)}, bf16[1024,128]{1,0:T(8,128)(2,1)S(1)}, u32[]{:S(2)}, u32[]{:S(2)}) collective-permute-start(bf16[1024,128]{1,0:T(8,128)(2,1)S(1)} %get-tuple-element.205), channel_id=1, source_target_pairs={{0,1},{1,0},{2,3},{3,2},{4,5},{5,4},{6,7},{7,6},{8,9},{9,8},{10,11... | collective-permute-start | bytes 786440 | tf_op jit(solution)/shard_map/ppermute | solution.py:447
  67.0 19.9 %collective-permute-start.20 = (bf16[1024,128]{1,0:T(8,128)(2,1)S(1)}, bf16[1024,128]{1,0:T(8,128)(2,1)S(1)}, u32[]{:S(2)}, u32[]{:S(2)}) collective-permute-start(bf16[1024,128]{1,0:T(8,128)(2,1)S(1)} %get-tuple-element.204), channel_id=1, source_target_pairs={{0,2},{1,3},{2,0},{3,1},{4,6},{5,7},{6,4},{7,5},{8,10},{9,11},{10,... | collective-permute-start | bytes 786440 | tf_op jit(solution)/shard_map/ppermute | solution.py:447
  67.2 20.0 %collective-permute-start.21 = (bf16[1024,128]{1,0:T(8,128)(2,1)S(1)}, bf16[1024,128]{1,0:T(8,128)(2,1)S(1)}, u32[]{:S(2)}, u32[]{:S(2)}) collective-permute-start(bf16[1024,128]{1,0:T(8,128)(2,1)S(1)} %get-tuple-element.203), channel_id=1, source_target_pairs={{0,3},{1,2},{2,1},{3,0},{4,7},{5,6},{6,5},{7,4},{8,11},{9,10},{10,... | collective-permute-start | bytes 786440 | tf_op jit(solution)/shard_map/ppermute | solution.py:447
  116.1 14.9 %collective-permute-start.27 = (bf16[2,4,2,64,512]{4,3,2,1,0:T(8,128)(2,1)S(1)}, bf16[2,4,2,64,512]{4,3,2,1,0:T(8,128)(2,1)S(1)}, u32[]{:S(2)}, u32[]{:S(2)}) collective-permute-start(bf16[2,4,2,64,512]{4,3,2,1,0:T(8,128)(2,1)S(1)} %fusion.2), channel_id=1, source_target_pairs={{0,2},{1,5},{2,0},{3,7},{4,6},{5,1},{6,4},{7,3},{8,10},{9,13},{10,... | collective-permute-start | bytes 3145736 | tf_op jit(solution)/shard_map/ppermute | solution.py:416
  131.2 9.2 %collective-permute-start.29 = (bf16[4,2,64,512]{3,2,1,0:T(8,128)(2,1)S(1)}, bf16[4,2,64,512]{3,2,1,0:T(8,128)(2,1)S(1)}, u32[]{:S(2)}, u32[]{:S(2)}) collective-permute-start(bf16[4,2,64,512]{3,2,1,0:T(8,128)(2,1)S(1)} %fusion.4), channel_id=1, source_target_pairs={{0,4},{1,3},{2,6},{3,1},{4,0},{5,7},{6,2},{7,5},{8,12},{9,11},{10,... | collective-permute-start | bytes 1572872 | tf_op jit(solution)/shard_map/ppermute | solution.py:416
  140.5 24.9 %collective-permute-start.30 = (bf16[2,4,9,64,128]{4,3,2,1,0:T(8,128)(2,1)S(1)}, bf16[2,4,9,64,128]{4,3,2,1,0:T(8,128)(2,1)S(1)}, u32[]{:S(2)}, u32[]{:S(2)}) collective-permute-start(bf16[2,4,9,64,128]{4,3,2,1,0:T(8,128)(2,1)S(1)} %fusion), channel_id=1, source_target_pairs={{0,2},{1,5},{2,0},{3,7},{4,6},{5,1},{6,4},{7,3},{8,10},{9,13},{10,... | collective-permute-start | bytes 3538952 | tf_op jit(solution)/shard_map/ppermute | solution.py:416
  140.8 17.2 %collective-permute-start.33 = (bf16[2,64,512]{2,1,0:T(8,128)(2,1)S(1)}, bf16[2,64,512]{2,1,0:T(8,128)(2,1)S(1)}, u32[]{:S(2)}, u32[]{:S(2)}) collective-permute-start(bf16[2,64,512]{2,1,0:T(8,128)(2,1)S(1)} %get-tuple-element.187), channel_id=1, source_target_pairs={{0,24},{1,25},{2,26},{3,27},{4,28},{5,29},{6,30},{7,31},{8,16},{9,... | collective-permute-start | bytes 393224 | tf_op jit(solution)/shard_map/ppermute | solution.py:416
  154.0 10.6 %collective-permute-start.32 = (bf16[2,64,512]{2,1,0:T(8,128)(2,1)S(1)}, bf16[2,64,512]{2,1,0:T(8,128)(2,1)S(1)}, u32[]{:S(2)}, u32[]{:S(2)}) collective-permute-start(bf16[2,64,512]{2,1,0:T(8,128)(2,1)S(1)} %get-tuple-element.188), channel_id=1, source_target_pairs={{0,16},{1,17},{2,18},{3,19},{4,20},{5,21},{6,22},{7,23},{8,24},{9,... | collective-permute-start | bytes 393224 | tf_op jit(solution)/shard_map/ppermute | solution.py:416
  154.0 10.6 %collective-permute-start.31 = (bf16[2,64,512]{2,1,0:T(8,128)(2,1)S(1)}, bf16[2,64,512]{2,1,0:T(8,128)(2,1)S(1)}, u32[]{:S(2)}, u32[]{:S(2)}) collective-permute-start(bf16[2,64,512]{2,1,0:T(8,128)(2,1)S(1)} %get-tuple-element.186), channel_id=1, source_target_pairs={{0,8},{1,9},{2,10},{3,11},{4,12},{5,13},{6,14},{7,15},{8,0},{9,1},... | collective-permute-start | bytes 393224 | tf_op jit(solution)/shard_map/ppermute | solution.py:416
  166.6 10.2 %collective-permute-start.34 = (bf16[4,9,64,128]{3,2,1,0:T(8,128)(2,1)}, bf16[4,9,64,128]{3,2,1,0:T(8,128)(2,1)}, u32[]{:S(2)}, u32[]{:S(2)}) collective-permute-start(bf16[4,9,64,128]{3,2,1,0:T(8,128)(2,1)} %fusion.1), channel_id=1, source_target_pairs={{0,4},{1,3},{2,6},{3,1},{4,0},{5,7},{6,2},{7,5},{8,12},{9,11},{10,... | collective-permute-start | bytes 1769480 | tf_op jit(solution)/shard_map/ppermute | solution.py:416
  178.2 19.6 %collective-permute-start.38 = (bf16[2,1024,128]{2,1,0:T(8,128)(2,1)S(1)}, bf16[2,1024,128]{2,1,0:T(8,128)(2,1)}, u32[]{:S(2)}, u32[]{:S(2)}) collective-permute-start(bf16[2,1024,128]{2,1,0:T(8,128)(2,1)S(1)} %pad_maximum_fusion.4), channel_id=1, source_target_pairs={{0,1},{1,0},{2,3},{3,2},{4,5},{5,4},{6,7},{7,6},{8,9},{9,8},{10,11... | collective-permute-start | bytes 1572872 | tf_op jit(solution)/shard_map/ppermute | solution.py:584
  178.3 19.5 %collective-permute-start.39 = (bf16[2,1024,128]{2,1,0:T(8,128)(2,1)S(1)}, bf16[2,1024,128]{2,1,0:T(8,128)(2,1)}, u32[]{:S(2)}, u32[]{:S(2)}) collective-permute-start(bf16[2,1024,128]{2,1,0:T(8,128)(2,1)S(1)} %pad_maximum_fusion.5), channel_id=1, source_target_pairs={{0,2},{1,3},{2,0},{3,1},{4,6},{5,7},{6,4},{7,5},{8,10},{9,11},{10,... | collective-permute-start | bytes 1572872 | tf_op jit(solution)/shard_map/ppermute | solution.py:584
  184.5 12.1 %collective-permute-start.36 = (bf16[9,64,128]{2,1,0:T(8,128)(2,1)S(1)}, bf16[9,64,128]{2,1,0:T(8,128)(2,1)S(1)}, u32[]{:S(2)}, u32[]{:S(2)}) collective-permute-start(bf16[9,64,128]{2,1,0:T(8,128)(2,1)S(1)} %get-tuple-element.185), channel_id=1, source_target_pairs={{0,16},{1,17},{2,18},{3,19},{4,20},{5,21},{6,22},{7,23},{8,24},{9,... | collective-permute-start | bytes 442376 | tf_op jit(solution)/shard_map/ppermute | solution.py:416
  184.5 12.1 %collective-permute-start.35 = (bf16[9,64,128]{2,1,0:T(8,128)(2,1)S(1)}, bf16[9,64,128]{2,1,0:T(8,128)(2,1)S(1)}, u32[]{:S(2)}, u32[]{:S(2)}) collective-permute-start(bf16[9,64,128]{2,1,0:T(8,128)(2,1)S(1)} %get-tuple-element.183), channel_id=1, source_target_pairs={{0,8},{1,9},{2,10},{3,11},{4,12},{5,13},{6,14},{7,15},{8,0},{9,1},... | collective-permute-start | bytes 442376 | tf_op jit(solution)/shard_map/ppermute | solution.py:416
  189.9 24.1 %collective-permute-start.44 = (bf16[2,1024,128]{2,1,0:T(8,128)(2,1)}, bf16[2,1024,128]{2,1,0:T(8,128)(2,1)}, u32[]{:S(2)}, u32[]{:S(2)}) collective-permute-start(bf16[2,1024,128]{2,1,0:T(8,128)(2,1)} %pad_maximum_fusion.6), channel_id=1, source_target_pairs={{0,3},{1,2},{2,1},{3,0},{4,7},{5,6},{6,5},{7,4},{8,11},{9,10},{10,... | collective-permute-start | bytes 1572872 | tf_op jit(solution)/shard_map/ppermute | solution.py:584
  (51 other events, 366.5 us)

commit v3 on v2

--- a/solution.py
+++ b/solution.py
@@ -56,62 +56,64 @@
     return pl.multiple_of(v, n)
 
 
-def relative(place, d, m, plain):
+def relative(place, d, m):
     dp, mp = place[0], place[1]
     fx = (dp & 1) ^ (d & 1)
     fy = (mp >> 1) ^ (m >> 1)
     dz = (dp >> 1) ^ (d >> 1)
-    if plain or (m & 1):
+    if m & 1:
         return fx, fy, dz
     return fy, fx, dz
 
 
-def source_of(place, dc, b, a, dz, plain):
+def source_of(place, dc, b, a, dz):
     dp, mp = place[0], place[1]
-    if plain:
-        fx, fy = b, a
-    else:
-        flip = (mp & 1) ^ dc
-        fx = jnp.where(flip == 0, a, b)
-        fy = jnp.where(flip == 0, b, a)
+    flip = (mp & 1) ^ dc
+    fx = jnp.where(flip == 0, a, b)
+    fy = jnp.where(flip == 0, b, a)
     d = ((dp >> 1) ^ dz) * 2 + ((dp & 1) ^ fx)
     m = ((mp >> 1) ^ fy) * 2 + ((mp & 1) ^ dc)
     return d, m
 
 
-def store_shares(place, keep, give, m, plain, devices, store):
+def store_shares(place, keep, give, m, devices, store):
     same = (place[1] & 1) == (m & 1)
 
     @pl.when(same)
     def _():
         for d in range(devices):
-            store(keep, relative(place, d, m, plain), d)
+            store(keep, relative(place, d, m), d)
 
     @pl.when(jnp.logical_not(same))
     def _():
         for d in range(devices):
-            store(give, relative(place, d, m, plain), d)
+            store(give, relative(place, d, m), d)
 
 
 SLOTS = tuple((dc, b, a) for dc in (0, 1) for b, a in ((0, 0), (0, 1), (1, 0), (1, 1)))
 
 
-def fetch(place, x_parts, x_full, x_sem, pieces, whole, sems):
-    seq, own = x_full.shape[0], x_parts[0].shape[1]
-    di, cols = pieces[0].shape[2:]
-    rows = []
-    for k, part in enumerate(x_parts):
-        target = x_full.at[:, pl.ds(mult((place[1] ^ k) * own, own), own)]
-        rows.append(pltpu.make_async_copy(part.at[pl.ds(0, seq), :], target, x_sem.at[k]))
-        rows[-1].start()
-    shards = []
-    for slot, ((dc, b, a), piece) in enumerate(zip(SLOTS, pieces)):
-        for z in range(piece.shape[0]):
-            d, m = source_of(place, dc, b, a, z, False)
-            target = whole.at[:, pl.ds(mult(d * di, di), di), pl.ds(mult(m * cols, cols), cols)]
-            shards.append(pltpu.make_async_copy(piece.at[z], target, sems.at[slot, z]))
-            shards[-1].start()
-    return rows, shards
+def fetch_rows(place, parts, whole, sems):
+    seq, own = whole.shape[0], parts[0].shape[1]
+    copies = []
+    for k, part in enumerate(parts):
+        target = whole.at[:, pl.ds(mult((place[1] ^ k) * own, own), own)]
+        copies.append(pltpu.make_async_copy(part.at[pl.ds(0, seq), :], target, sems.at[k]))
+        copies[-1].start()
+    return copies
+
+
+def fetch_shards(shards, sems):
+    copies = []
+    for index, shard, whole, d, m in shards:
+        di, cols = shard.shape[-2:]
+        target = whole.at[
+            (slice(None),) * (len(shard.shape) - 2)
+            + (pl.ds(mult(d * di, di), di), pl.ds(mult(m * cols, cols), cols))
+        ]
+        copies.append(pltpu.make_async_copy(shard, target, sems.at[index]))
+        copies[-1].start()
+    return copies
 
 
 def conv_forward(place, x0, x1, x2, x3, vec, *rest):
@@ -119,11 +121,18 @@
     w_out, x_out, na_out, conv_out, bias_out, nf, nab, whole, extra, sems, x_sem = rest[8:]
     full = vec.shape[1]
     seq, own = x_out.shape[0], x0.shape[1]
-    length = place[2]
     blocks = place[3]
 
     x_parts = (x0, x1, x2, x3)
-    rows, shards = fetch(place, x_parts, x_out, x_sem.at[0], pieces, whole, sems)
+    rows = fetch_rows(place, x_parts, x_out, x_sem.at[0])
+    shards = fetch_shards(
+        [
+            ((slot, z), piece.at[z], whole, *source_of(place, *index, z))
+            for slot, (index, piece) in enumerate(zip(SLOTS, pieces))
+            for z in range(piece.shape[0])
+        ],
+        sems,
+    )
     extras = [
         pltpu.make_async_copy(part.at[pl.ds(seq, extra.shape[1]), :], extra.at[k], x_sem.at[1, k])
         for k, part in enumerate(x_parts)
@@ -186,16 +195,24 @@
 
 def ffn(place, x_full, conv_out, c0, c1, c2, c3, vec, hbias, *rest):
     pieces = rest[:8]
-    block_out, resid_out, cab, keep, give, vgrad, hbgrad = rest[8:15]
-    whole, cot, act, hg, sec, mg, cf, sems, c_sem = rest[15:]
+    block_out, resid_out, cab, act, hg, sec, mg, vgrad, hbgrad = rest[8:17]
+    whole, cf, sems, c_sem = rest[17:]
     wh, wo = whole.at[0], whole.at[1]
     seq, full = x_full.shape
     hidden = hbias.shape[1]
-    di, part = pieces[0].shape[2:]
     own = c0.shape[1]
     blocks = place[3]
 
-    rows, shards = fetch(place, (c0, c1, c2, c3), cot, c_sem.at[0], pieces, whole, sems)
+    rows = fetch_rows(place, (c0, c1, c2, c3), mg, c_sem)
+    shards = []
+    for slot, piece in enumerate(pieces):
+        w, dc, dx = slot >> 2, (slot >> 1) & 1, slot & 1
+        for z in range(piece.shape[0]):
+            for dy in (0, 1):
+                d = ((place[0] >> 1) ^ z) * 2 + ((place[0] & 1) ^ dx)
+                m = place[1] ^ (dy * 2 + dc)
+                shards.append(((slot, z, dy), piece.at[z, dy], whole.at[w], d, m))
+    shards = fetch_shards(shards, sems)
     vgrad[...] = jnp.zeros_like(vgrad)
     hbgrad[...] = jnp.zeros_like(hbgrad)
     cf[...] = jnp.zeros_like(cf)
@@ -213,8 +230,7 @@
         s, inverse = norm_parts(residual)
         second = (s * vec[3:4, :] + vec[4:5, :]).astype(bf16)
         sec[rows, :] = second
-        grad = cot[rows, :]
-        mg[rows, :] = grad
+        grad = mg[rows, :]
         for j in range(hidden // 512):
             cols = slice(j * 512, (j + 1) * 512)
             h = dot(second, wh[:, cols]) + hbias[0:1, cols]
@@ -242,7 +258,7 @@
     def idle_step(i, _):
         rows = pl.ds(mult(i * ROWS, ROWS), ROWS)
         out_store(rows, x_full[rows, :])
-        resid_out[rows, :] = cot[rows, :].astype(f32)
+        resid_out[rows, :] = mg[rows, :].astype(f32)
         for ref in (sec, mg):
             ref[rows, :] = jnp.zeros((ROWS, full), bf16)
         for ref in (act, hg):
@@ -260,6 +276,10 @@
 
     lax.fori_loop(0, cab.shape[1] // 64, shift_step, 0)
 
+
+def ffn_weight_grad(place, sec, hg, mg, act, keep, give):
+    full, hidden = sec.shape[1], hg.shape[1]
+    di, part = keep.shape[4:]
     sec_t = sec[...].T
     mg_t = mg[...].T
     for m in range(hidden // part):
@@ -270,7 +290,7 @@
             def store(ref, index, d):
                 ref[(*index, w)] = value[d * di : (d + 1) * di, :]
 
-            store_shares(place, keep, give, m, False, full // di, store)
+            store_shares(place, keep, give, m, full // di, store)
 
 
 def shifted_rows(cab, u, row, count):
@@ -290,7 +310,7 @@
             def store(ref, index, d):
                 ref[(*index, t)] = value[d * di : (d + 1) * di, m * own : (m + 1) * own]
 
-            store_shares(place, keep, give, m, False, full // di, store)
+            store_shares(place, keep, give, m, full // di, store)
         return 0
 
     lax.fori_loop(0, taps, tap_step, 0)
@@ -333,12 +353,21 @@
     return lax.optimization_barrier(values)
 
 
-def call(kernel, place, args, outs, scratch, flops, mib, far=(), far_out=()):
+def placed(kernel):
+    def run(lengths, *refs):
+        mp = lax.axis_index("mp")
+        length = lengths[mp]
+        kernel((lax.axis_index("dp"), mp, length, length // ROWS), *refs)
+
+    return run
+
+
+def call(kernel, lengths, args, outs, scratch, flops, mib, far=(), far_out=()):
     near = pl.BlockSpec(memory_space=pltpu.VMEM)
-    left = pl.BlockSpec(memory_space=pl.ANY)
+    left = pl.BlockSpec(memory_space=pltpu.HBM)
     moved = sum(a.size * a.dtype.itemsize for a in (*args, *outs))
     return pl.pallas_call(
-        kernel,
+        placed(kernel),
         out_shape=outs,
         in_specs=[pl.BlockSpec(memory_space=pltpu.SMEM)]
         + [left if i in far else near for i in range(len(args))],
@@ -346,7 +375,7 @@
         scratch_shapes=scratch,
         compiler_params=pltpu.CompilerParams(vmem_limit_bytes=mib * 2**20),
         cost_estimate=pl.CostEstimate(flops=flops, bytes_accessed=moved, transcendentals=0),
-    )(place, *args)
+    )(lengths, *args)
 
 
 def adam_step(weight, first_mom, second, gradient, clip_scale, step_rate, decay_rate):
@@ -394,7 +423,7 @@
     part = hidden_bias.shape[0]
     hidden = part * nmp
     di = full // ndp
-    dp, mp = lax.axis_index("dp"), lax.axis_index("mp")
+    mp = lax.axis_index("mp")
 
     def perm(move):
         pairs = []
@@ -452,51 +481,55 @@
             pieces = [jnp.where(odd, pieces[k ^ (1 << bit)], pieces[k]) for k in range(nmp)]
         return jnp.stack(pieces)
 
-    def all_sum(values, other):
+    def all_sum(values):
         values = values + send(values, step_c)
         step = 1
         while step < nz:
             values = values + send(values, across_z[step])
             step *= 2
         values = values + send(values, step_x)
-        values, other = tie(values, other)
-        return values + send(values, step_y), other
-
-    length = lax.dynamic_index_in_dim(lengths, mp, 0, False)
-    place = jnp.stack([dp, mp, length, length // ROWS]).astype(jnp.int32)
+        return values + send(values, step_y)
+
     exact, rest = [], hidden_bias
     for _ in range(3):
         exact.append(lax.reduce_precision(rest, 8, 7))
         rest = rest - exact[-1]
     exact.append(jnp.zeros_like(rest))
     exact = jnp.concatenate(exact).reshape(4 * part // own, own).astype(bf16)
-    vec = jnp.concatenate([vectors, jnp.zeros((2, full), f32)])
     ffn_shard = jnp.stack([hidden_master.astype(bf16), output_master.astype(bf16).T])
 
     x_blocks = take_windows(inputs, exact)
     *x_blocks, conv_shard = tie(*x_blocks, conv_master.astype(bf16))
     x_parts = swap(x_blocks)
     conv_z = gather_z(conv_shard)
-    *tied, ffn_shard = tie(*x_parts, *conv_z, ffn_shard)
+    ffn_y = send(ffn_shard, step_y)
+    *tied, ffn_shard, ffn_y = tie(*x_parts, *conv_z, ffn_shard, ffn_y)
     x_parts, conv_z = tied[:nmp], jnp.stack(tied[nmp:])
+    first, last = [jnp.stack([ffn_shard[w], ffn_y[w]]) for w in (0, 1)]
     conv_a, conv_b = send(conv_z, step_xy), send(conv_z, step_yx)
-    ffn_z = gather_z(ffn_shard)
-    conv_z, conv_a, conv_b, *ffn_z = tie(conv_z, conv_a, conv_b, *ffn_z)
-    ffn_z = jnp.stack(ffn_z)
+    first = gather_z(first)
+    conv_z, conv_a, conv_b, last, *first = tie(conv_z, conv_a, conv_b, last, *first)
     conv_ab = send(conv_a, step_yx)
-    conv_far = [send(part_of, step_c) for part_of in (conv_z, conv_a, conv_b)]
-    conv_ab, cotangent, *conv_far = tie(conv_ab, cotangent, *conv_far)
-    conv_parts = [conv_z, conv_a, conv_b, conv_ab, *conv_far, send(conv_ab, step_c)]
-    ffn_a, ffn_b = send(ffn_z, step_xy), send(ffn_z, step_yx)
+    first = jnp.stack(first)
+    first_x = send(first, step_x)
+    last = gather_z(last)
+    conv_z, conv_a, conv_b, conv_ab, cotangent, first, *last = tie(
+        conv_z, conv_a, conv_b, conv_ab, cotangent, first, *last
+    )
+    conv_parts = [conv_z, conv_a, conv_b, conv_ab]
+    conv_parts += [send(part_of, step_c) for part_of in conv_parts]
+    last = jnp.stack(last)
+    last_x = send(last, step_x)
     c_parts = swap(take_windows(cotangent))
 
     S = jax.ShapeDtypeStruct
     padded = seq + 2 * REACH
-    ffn_a, *x_parts = tie(ffn_a, *x_parts)
+    last, *x_parts = tie(last, *x_parts)
+    first_c, last_c = send(first, step_c), send(last, step_c)
     w_full, x_full, normed, conv_out, bias_all = call(
         conv_forward,
-        place,
-        (*x_parts, vec, *conv_parts),
+        lengths,
+        (*x_parts, vectors, *conv_parts),
         (
             S((KERNEL, full, full), bf16),
             S((seq, full), bf16),
@@ -517,72 +550,79 @@
         (0, 1, 2, 3, *range(5, 13)),
         (0,),
     )
-    ffn_ab = send(ffn_a, step_yx)
-    *tied, conv_out = tie(ffn_z, ffn_a, ffn_b, ffn_ab, *c_parts, conv_out)
-    ffn_parts, c_parts = tied[:4], tied[4:]
-    ffn_parts += [send(part_of, step_c) for part_of in ffn_parts]
-    block_rel, resid_grad, conv_grad, ffn_keep, ffn_give, vgrad_two, bias_grad = call(
+    *tied, conv_out = tie(first, first_x, first_c, last, last_x, last_c, *c_parts, conv_out)
+    first, first_x, first_c, last, last_x, last_c, *c_parts = tied
+    ffn_parts = [first, first_x, first_c, send(first_x, step_c)]
+    ffn_parts += [last, last_x, last_c, send(last_x, step_c)]
+    block_rel, resid_grad, conv_grad, active, hidden_grad, second, mix_grad, vgrad_two, bias_grad = call(
         ffn,
-        place,
-        (x_full, conv_out, *c_parts, vec, bias_all.reshape(1, hidden), *ffn_parts),
+        lengths,
+        (x_full, conv_out, *c_parts, vectors, bias_all.reshape(1, hidden), *ffn_parts),
         (
             S((nmp, seq, own), bf16),
             S((seq, full), f32),
             S((2, padded, full), bf16),
-            *(S((2, 2, nz, 2, di, part), bf16),) * 2,
+            *(S((seq, hidden), bf16),) * 2,
+            *(S((seq, full), bf16),) * 2,
             S((8, full), f32),
             S((1, hidden), f32),
         ),
         [
             pltpu.VMEM((2, full, hidden), bf16),
-            pltpu.VMEM((seq, full), bf16),
-            pltpu.VMEM((seq, hidden), bf16),
-            pltpu.VMEM((seq, hidden), bf16),
-            pltpu.VMEM((seq, full), bf16),
-            pltpu.VMEM((seq, full), bf16),
             pltpu.VMEM((padded + 8, full), f32),
-            pltpu.SemaphoreType.DMA((8, nz)),
-            pltpu.SemaphoreType.DMA((1, nmp)),
+            pltpu.SemaphoreType.DMA((8, nz, 2)),
+            pltpu.SemaphoreType.DMA((nmp,)),
         ],
-        12 * seq * hidden * full,
-        44,
+        8 * seq * hidden * full,
+        20,
         (2, 3, 4, 5, *range(8, 16)),
     )
+    ffn_keep, ffn_give = call(
+        ffn_weight_grad,
+        lengths,
+        (second, hidden_grad, mix_grad, active),
+        (S((2, 2, nz, 2, di, part), bf16),) * 2,
+        [],
+        4 * seq * hidden * full,
+        12,
+    )
     ffn_r = send(ffn_give, step_c)
-    ffn_sum, conv_grad = tie(scatter_b(ffn_keep, ffn_r), conv_grad)
-    ffn_rb = send(ffn_sum, step_yx)
+    ffn_keep, normed = tie(ffn_keep, normed)
     conv_keep, conv_give = call(
         conv_weight_grad,
-        place,
+        lengths,
         (normed, conv_grad),
         (S((2, 2, nz, KERNEL, di, own), bf16),) * 2,
         [],
         2 * seq * KERNEL * full * full,
         16,
     )
-    conv_give, ffn_rb, conv_grad = tie(conv_give, ffn_rb, conv_grad)
     conv_r = send(conv_give, step_c)
-    ffn_ra = send(scatter_a(ffn_keep, ffn_r, ffn_rb), step_xy)
+    ffn_sum, conv_keep, conv_grad = tie(scatter_b(ffn_keep, ffn_r), conv_keep, conv_grad)
+    ffn_rb = send(ffn_sum, step_yx)
     in_rel, vgrad_one = call(
         conv_backward,
-        place,
-        (x_full, conv_grad, resid_grad, w_full, vec),
+        lengths,
+        (x_full, conv_grad, resid_grad, w_full, vectors),
         (S((nmp, seq, own), bf16), S((8, full), f32)),
         [],
         1,
         16,
     )
-    conv_sum, ffn_ra, in_rel = tie(scatter_b(conv_keep, conv_r), ffn_ra, in_rel)
+    conv_sum, in_rel = tie(scatter_b(conv_keep, conv_r), in_rel)
     conv_rb = send(conv_sum, step_yx)
+    ffn_ra = send(scatter_a(ffn_keep, ffn_r, ffn_rb), step_xy)
+    conv_ra = send(scatter_a(conv_keep, conv_r, conv_rb), step_xy)
     ffn_share = scatter_z(ffn_keep, ffn_r, ffn_rb, ffn_ra)
-    conv_sum, ffn_share = tie(scatter_a(conv_keep, conv_r, conv_rb), ffn_share)
-    conv_ra = send(conv_sum, step_xy)
     conv_ra, in_rel, block_rel = tie(conv_ra, in_rel, block_rel)
     conv_share = scatter_z(conv_keep, conv_r, conv_rb, conv_ra)
     out_parts = [jnp.stack([block_rel[k], in_rel[k]]) for k in range(nmp)]
     for k in range(1, nmp):
         out_parts[k] = lax.ppermute(out_parts[k], "mp", within[k])
     conv_share, *out_parts[:-1] = tie(conv_share, *out_parts[:-1])
+    ffn_share, out_parts[-1] = tie(ffn_share, out_parts[-1])
+    outputs = in_order(out_parts)
+    block_output, input_grad = outputs[:, 0], outputs[:, 1].astype(f32)
 
     squares = square_sum(conv_share) + square_sum(ffn_share)
     small = jnp.concatenate(
@@ -592,9 +632,7 @@
             jnp.broadcast_to(squares, (1, full)),
         ]
     )
-    small, out_parts[-1] = all_sum(small, out_parts[-1])
-    outputs = in_order(out_parts)
-    block_output, input_grad = outputs[:, 0], outputs[:, 1].astype(f32)
+    small = all_sum(small)
     vector_sum, bias_sum = small[:6], small[6:-1].reshape(hidden)
     hidden_share, output_share = ffn_share[0], ffn_share[1].T
     grad_norm = jnp.sqrt(small[-1, 0] + square_sum(small[:-1]))

time: 228 us -> 211 us (0.925)
  waiting for transfers between devices: 103 us -> 89.2 us
  starting transfers between devices: 51 us -> 61.6 us
  local copies, waits for them, and re-layouts: 12.5 us -> 3.44 us
  Pallas kernels: 32.2 us -> 29 us
  between operations: 7.67 us -> 5 us
    ppermute x37 -> x40, waiting for transfers between devices: 89.4 us -> 76.2 us  [send(): return lax.ppermute(values, axes, pairs)]
    ppermute x37 -> x40, starting transfers between devices: 45.9 us -> 54.9 us  [send(): return lax.ppermute(values, axes, pairs)]
    unnamed x76 -> x58, local copies, waits for them, and re-layouts: 6.28 us -> 0.14 us
    ppermute x6, waiting for transfers between devices: 13.2 us -> 9.18 us  [swap(): lax.ppermute(blocks[k], 'mp', within[k])]
    ppermute x3, waiting for transfers between devices: 0.01 us -> 3.87 us  [per_device(): out_parts[k] = lax.ppermute(out_parts[k], 'mp', within[k])]
    pallas_call x4 -> x5, Pallas kernels: 32.2 us -> 29 us  [call(): pl.pallas_call(placed(kernel), out_shape=outs, in_specs=[pl.BlockSpec(mem...]
  transfers between devices with their start and end apart: 46 -> 49, of which waited for: 24 -> 23; matrix products, arithmetic and copies ran while one was open for 7% -> 7% of each run, Pallas kernels for 7% -> 7%
where the time goes in v3:
time: 211 us; the launch traced here: 209 us
  waiting for transfers between devices  89.2 us (42%)
  starting transfers between devices  61.6 us (29%)
  Pallas kernels  29 us (14%)
  other arithmetic  20.4 us (10%)
  between operations  5 us (2%)
  local copies, waits for them, and re-layouts  3.44 us (2%)
    ppermute x40, waiting for transfers between devices, send(): return lax.ppermute(values, axes, pairs)  76.2 us
    ppermute x40, starting transfers between devices, send(): return lax.ppermute(values, axes, pairs)  54.9 us
    pallas_call x5, Pallas kernels, call(): pl.pallas_call(placed(kernel), out_shape=outs, in_specs=[pl.BlockSpec(mem...  29 us
    ppermute x6, waiting for transfers between devices, swap(): lax.ppermute(blocks[k], 'mp', within[k])  9.18 us
    ppermute x6, starting transfers between devices, swap(): lax.ppermute(blocks[k], 'mp', within[k])  4.54 us
  transfers between devices with their start and end apart: 49, of which 23 were waited for; matrix products, arithmetic and copies ran while one was open for 7% of the time, Pallas kernels for 7%

profile of v3, /device:TPU:0, one launch (start us, length us, event | category | flops | bytes accessed | tf_op | source)
XLA Modules:
  0.0 208.7 jit_solution(8228515597091299092)
XLA Ops:
  3.4 3.1 %collective-permute-start.3 = (bf16[9,64,128]{2,1,0:T(8,128)(2,1)S(1)}, bf16[9,64,128]{2,1,0:T(8,128)(2,1)S(1)}, u32[]{:S(2)}, u32[]{:S(2)}) collective-permute-start(bf16[9,64,128]{2,1,0:T(8,128)(2,1)S(1)} %convert_element_type.274), channel_id=1, source_target_pairs={{0,8},{1,9},{2,10},{3,11},{4,12},{5,13},{6,14},{7,15},{8,0},{9,1},... | collective-permute-start | bytes 442376 | tf_op jit(solution)/shard_map/ppermute | solution.py:445
  10.0 2.0 collective-permute-done.6
  12.0 2.6 %collective-permute-start.4 = (bf16[9,64,128]{2,1,0:T(8,128)(2,1)S(1)}, bf16[9,64,128]{2,1,0:T(8,128)(2,1)S(1)}, u32[]{:S(2)}, u32[]{:S(2)}) collective-permute-start(bf16[9,64,128]{2,1,0:T(8,128)(2,1)S(1)} %convert_element_type.274), channel_id=1, source_target_pairs={{0,16},{1,17},{2,18},{3,19},{4,20},{5,21},{6,22},{7,23},{8,24},{9,... | collective-permute-start | bytes 442376 | tf_op jit(solution)/shard_map/ppermute | solution.py:445
  14.9 9.5 %collective-permute-done.4 = bf16[9,64,128]{2,1,0:T(8,128)(2,1)S(1)} collective-permute-done((bf16[9,64,128]{2,1,0:T(8,128)(2,1)S(1)}, bf16[9,64,128]{2,1,0:T(8,128)(2,1)S(1)}, u32[]{:S(2)}, u32[]{:S(2)}) %collective-permute-start.4) | collective-permute-done | bytes 147488 | tf_op jit(solution)/shard_map/ppermute | solution.py:445
  26.0 1.9 collective-permute-start.8
  27.9 3.3 %collective-permute-start.10 = (bf16[2,64,512]{2,1,0:T(8,128)(2,1)S(1)}, bf16[2,64,512]{2,1,0:T(8,128)(2,1)S(1)}, u32[]{:S(2)}, u32[]{:S(2)}) collective-permute-start(bf16[2,64,512]{2,1,0:T(8,128)(2,1)S(1)} %pad_maximum_fusion.10), channel_id=1, source_target_pairs={{0,16},{1,17},{2,18},{3,19},{4,20},{5,21},{6,22},{7,23},{8,24},{9,... | collective-permute-start | bytes 393224 | tf_op jit(solution)/shard_map/ppermute | solution.py:445
  32.5 7.4 %collective-permute-done.10 = bf16[2,64,512]{2,1,0:T(8,128)(2,1)S(1)} collective-permute-done((bf16[2,64,512]{2,1,0:T(8,128)(2,1)S(1)}, bf16[2,64,512]{2,1,0:T(8,128)(2,1)S(1)}, u32[]{:S(2)}, u32[]{:S(2)}) %collective-permute-start.10) | collective-permute-done | bytes 131104 | tf_op jit(solution)/shard_map/ppermute | solution.py:445
  41.9 2.6 %collective-permute-start.13 = (bf16[2,64,512]{2,1,0:T(8,128)(2,1)S(1)}, bf16[2,64,512]{2,1,0:T(8,128)(2,1)S(1)}, u32[]{:S(2)}, u32[]{:S(2)}) collective-permute-start(bf16[2,64,512]{2,1,0:T(8,128)(2,1)S(1)} %pad_maximum_fusion.9), channel_id=1, source_target_pairs={{0,8},{1,9},{2,10},{3,11},{4,12},{5,13},{6,14},{7,15},{8,0},{9,1},... | collective-permute-start | bytes 393224 | tf_op jit(solution)/shard_map/ppermute | solution.py:445
  47.2 1.7 collective-permute-done.13
  48.9 7.5 %collective-permute-done.14 = bf16[2,64,512]{2,1,0:T(8,128)(2,1)S(1)} collective-permute-done((bf16[2,64,512]{2,1,0:T(8,128)(2,1)S(1)}, bf16[2,64,512]{2,1,0:T(8,128)(2,1)S(1)}, u32[]{:S(2)}, u32[]{:S(2)}) %collective-permute-start.14) | collective-permute-done | bytes 131104 | tf_op jit(solution)/shard_map/ppermute | solution.py:445
  58.8 2.5 %collective-permute-done.24.refs_3_ = bf16[1024,128]{1,0:T(8,128)(2,1)S(1)} collective-permute-done((bf16[1024,128]{1,0:T(8,128)(2,1)S(1)}, bf16[1024,128]{1,0:T(8,128)(2,1)S(1)}, u32[]{:S(2)}, u32[]{:S(2)}) %collective-permute-start.24) | collective-permute-done | bytes 262176 | tf_op jit(solution)/shard_map/ppermute | solution.py:476
  64.8 4.9 %shard_map.313 = (bf16[9,512,512]{2,1,0:T(8,128)(2,1)S(1)}, bf16[1024,512]{1,0:T(8,128)(2,1)S(1)}, bf16[1024,512]{1,0:T(8,128)(2,1)S(1)}, f32[1024,512]{1,0:T(8,128)S(1)}, f32[4,4,128]{2,1,0:T(4,128)S(1)}) custom-call(s32[4]{0:T(128)S(1)} %copy-done.4, bf16[1040,128]{1,0:T(8,128)(2,1)S(1)} %concatenate.34.refs_0_, ...), custom_call_target="tpu_custom_call" | custom-call | flops 4831838208 | bytes 14716928 | tf_op jit(solution)/shard_map/pallas_call | solution.py:369
  69.7 2.9 %collective-permute-done.25.refs_4_ = bf16[1024,128]{1,0:T(8,128)(2,1)S(1)} collective-permute-done((bf16[1024,128]{1,0:T(8,128)(2,1)S(1)}, bf16[1024,128]{1,0:T(8,128)(2,1)S(1)}, u32[]{:S(2)}, u32[]{:S(2)}) %collective-permute-start.25) | collective-permute-done | bytes 262176 | tf_op jit(solution)/shard_map/ppermute | solution.py:476
  72.5 3.8 %collective-permute-done.26.refs_5_ = bf16[1024,128]{1,0:T(8,128)(2,1)S(1)} collective-permute-done((bf16[1024,128]{1,0:T(8,128)(2,1)S(1)}, bf16[1024,128]{1,0:T(8,128)(2,1)S(1)}, u32[]{:S(2)}, u32[]{:S(2)}) %collective-permute-start.26) | collective-permute-done | bytes 262176 | tf_op jit(solution)/shard_map/ppermute | solution.py:476
  79.5 7.1 %shard_map.314 = (bf16[4,1024,128]{2,1,0:T(8,128)(2,1)S(1)}, f32[1024,512]{1,0:T(8,128)S(1)}, bf16[2,1088,512]{2,1,0:T(8,128)(2,1)S(1)}, bf16[1024,2048]{1,0:T(8...) custom-call(s32[4]{0:T(128)S(1)} %copy-done.4, ...), custom_call_target="tpu_custom_call" | custom-call | flops 8589934592 | bytes 24293376 | tf_op jit(solution)/shard_map/pallas_call | solution.py:369
  86.5 6.8 %shard_map.315 = (bf16[2,2,4,2,64,512]{5,4,3,2,1,0:T(8,128)(2,1)S(1)}, bf16[2,2,4,2,64,512]{5,4,3,2,1,0:T(8,128)(2,1)S(1)}) custom-call(s32[4]{0:T(128)S(1)} %copy-done.4, bf16[1024,512]{1,0:T(8,128)(2,1)S(1)} %get-tuple-element.155.refs_0_, bf16[1024,2048]{1,0:T(8,128)(2,1)S(1)} %get-tuple-element.156.refs_1_, ...), custom_call_target="tpu_custom_call" | custom-call | flops 4294967296 | bytes 14680064 | tf_op jit(solution)/shard_map/pallas_call | solution.py:369
  93.8 8.0 %shard_map.316 = (bf16[2,2,4,9,64,128]{5,4,3,2,1,0:T(8,128)(2,1)S(1)}, bf16[2,2,4,9,64,128]{5,4,3,2,1,0:T(8,128)(2,1)S(1)}) custom-call(s32[4]{0:T(128)S(1)} %copy-done.4, bf16[1024,512]{1,0:T(8,128)(2,1)S(1)} %get-tuple-element.163.refs_0_, bf16[2,1088,512]{2,1,0:T(8,128)(2,1)S(1)} %get-tuple-element.169.refs_1_), custom_call_target="tpu_custom_call" | custom-call | flops 4831838208 | bytes 7995392 | tf_op jit(solution)/shard_map/pallas_call | solution.py:369
  102.7 2.3 %shard_map.317 = (bf16[4,1024,128]{2,1,0:T(8,128)(2,1)S(1)}, f32[8,512]{1,0:T(8,128)S(1)}) custom-call(s32[4]{0:T(128)S(1)} %copy-done.4, bf16[1024,512]{1,0:T(8,128)(2,1)S(1)} %get-tuple-element.138.refs_0_, bf16[2,1088,512]{2,1,0:T(8,128)(2,1)S(1)} %get-tuple-element.169.refs_1_, f32[1024,512]{1,0:T(8,128)S(1)} %get-tuple-element.170.refs_2_, ...), custom_call_target="tpu_custom_call" | custom-call | flops 1 | bytes 11169792 | tf_op jit(solution)/shard_map/pallas_call | solution.py:369
  107.3 10.0 %collective-permute-done.30 = bf16[2,4,2,64,512]{4,3,2,1,0:T(8,128)(2,1)S(1)} collective-permute-done((bf16[2,4,2,64,512]{4,3,2,1,0:T(8,128)(2,1)S(1)}, bf16[2,4,2,64,512]{4,3,2,1,0:T(8,128)(2,1)S(1)}, u32[]{:S(2)}, u32[]{:S(2)}) %collective-permute-start.30) | collective-permute-done | bytes 1048608 | tf_op jit(solution)/shard_map/ppermute | solution.py:445
  118.9 16.6 %collective-permute-done.36 = bf16[2,4,9,64,128]{4,3,2,1,0:T(8,128)(2,1)S(1)} collective-permute-done((bf16[2,4,9,64,128]{4,3,2,1,0:T(8,128)(2,1)S(1)}, bf16[2,4,9,64,128]{4,3,2,1,0:T(8,128)(2,1)S(1)}, u32[]{:S(2)}, u32[]{:S(2)}) %collective-permute-start.36) | collective-permute-done | bytes 1179680 | tf_op jit(solution)/shard_map/ppermute | solution.py:445
  138.5 1.7 fusion.14
  140.2 9.7 %collective-permute-start.32 = (bf16[2,64,512]{2,1,0:T(8,128)(2,1)S(1)}, bf16[2,64,512]{2,1,0:T(8,128)(2,1)S(1)}, u32[]{:S(2)}, u32[]{:S(2)}) collective-permute-start(bf16[2,64,512]{2,1,0:T(8,128)(2,1)S(1)} %get-tuple-element.206), channel_id=1, source_target_pairs={{0,8},{1,9},{2,10},{3,11},{4,12},{5,13},{6,14},{7,15},{8,0},{9,1},... | collective-permute-start | bytes 393224 | tf_op jit(solution)/shard_map/ppermute | solution.py:445
  149.9 2.8 %collective-permute-start.33 = (bf16[2,64,512]{2,1,0:T(8,128)(2,1)S(1)}, bf16[2,64,512]{2,1,0:T(8,128)(2,1)S(1)}, u32[]{:S(2)}, u32[]{:S(2)}) collective-permute-start(bf16[2,64,512]{2,1,0:T(8,128)(2,1)S(1)} %get-tuple-element.208), channel_id=1, source_target_pairs={{0,16},{1,17},{2,18},{3,19},{4,20},{5,21},{6,22},{7,23},{8,24},{9,... | collective-permute-start | bytes 393224 | tf_op jit(solution)/shard_map/ppermute | solution.py:445
  153.0 2.1 collective-permute-start.43
  156.7 4.3 %collective-permute-start.39 = (bf16[9,64,128]{2,1,0:T(8,128)(2,1)S(1)}, bf16[9,64,128]{2,1,0:T(8,128)(2,1)S(1)}, u32[]{:S(2)}, u32[]{:S(2)}) collective-permute-start(bf16[9,64,128]{2,1,0:T(8,128)(2,1)S(1)} %get-tuple-element.203), channel_id=1, source_target_pairs={{0,8},{1,9},{2,10},{3,11},{4,12},{5,13},{6,14},{7,15},{8,0},{9,1},... | collective-permute-start | bytes 442376 | tf_op jit(solution)/shard_map/ppermute | solution.py:445
  162.9 2.9 %collective-permute-start.41 = (bf16[9,64,128]{2,1,0:T(8,128)(2,1)S(1)}, bf16[9,64,128]{2,1,0:T(8,128)(2,1)S(1)}, u32[]{:S(2)}, u32[]{:S(2)}) collective-permute-start(bf16[9,64,128]{2,1,0:T(8,128)(2,1)S(1)} %get-tuple-element.204), channel_id=1, source_target_pairs={{0,24},{1,25},{2,26},{3,27},{4,28},{5,29},{6,30},{7,31},{8,16},{9,... | collective-permute-start | bytes 442376 | tf_op jit(solution)/shard_map/ppermute | solution.py:445
  167.7 7.1 %collective-permute-done.40 = bf16[9,64,128]{2,1,0:T(8,128)(2,1)S(1)} collective-permute-done((bf16[9,64,128]{2,1,0:T(8,128)(2,1)S(1)}, bf16[9,64,128]{2,1,0:T(8,128)(2,1)S(1)}, u32[]{:S(2)}, u32[]{:S(2)}) %collective-permute-start.40) | collective-permute-done | bytes 147488 | tf_op jit(solution)/shard_map/ppermute | solution.py:445
  176.7 3.9 %collective-permute-done.38 = bf16[2,1024,128]{2,1,0:T(8,128)(2,1)} collective-permute-done((bf16[2,1024,128]{2,1,0:T(8,128)(2,1)S(1)}, bf16[2,1024,128]{2,1,0:T(8,128)(2,1)}, u32[]{:S(2)}, u32[]{:S(2)}) %collective-permute-start.38) | collective-permute-done | bytes 524320 | tf_op jit(solution)/shard_map/ppermute | solution.py:621
  183.9 2.4 %collective-permute-start.45 = (f32[11,512]{1,0:T(8,128)S(1)}, f32[11,512]{1,0:T(8,128)S(1)}, u32[]{:S(2)}, u32[]{:S(2)}) collective-permute-start(f32[11,512]{1,0:T(8,128)S(1)} %fusion.30), channel_id=1, source_target_pairs={{0,8},{1,9},{2,10},{3,11},{4,12},{5,13},{6,14},{7,15},{8,0},{9,1},... | collective-permute-start | bytes 67592 | tf_op jit(solution)/shard_map/ppermute | solution.py:445
  186.3 1.9 collective-permute-done.45
  193.9 3.1 %collective-permute-done.47 = f32[11,512]{1,0:T(8,128)S(1)} collective-permute-done((f32[11,512]{1,0:T(8,128)S(1)}, f32[11,512]{1,0:T(8,128)S(1)}, u32[]{:S(2)}, u32[]{:S(2)}) %collective-permute-start.47) | collective-permute-done | bytes 22560 | tf_op jit(solution)/shard_map/ppermute | solution.py:445
  197.6 1.9 fusion.3
  (184 shorter events, 53.6 us)
Async XLA Ops:
  3.4 11.2 %collective-permute-start.3 = (bf16[9,64,128]{2,1,0:T(8,128)(2,1)S(1)}, bf16[9,64,128]{2,1,0:T(8,128)(2,1)S(1)}, u32[]{:S(2)}, u32[]{:S(2)}) collective-permute-start(bf16[9,64,128]{2,1,0:T(8,128)(2,1)S(1)} %convert_element_type.274), channel_id=1, source_target_pairs={{0,8},{1,9},{2,10},{3,11},{4,12},{5,13},{6,14},{7,15},{8,0},{9,1},... | collective-permute-start | bytes 442376 | tf_op jit(solution)/shard_map/ppermute | solution.py:445
  8.1 16.3 %collective-permute-start = (bf16[1040,128]{1,0:T(8,128)(2,1)S(1)}, bf16[1040,128]{1,0:T(8,128)(2,1)S(1)}, u32[]{:S(2)}, u32[]{:S(2)}) collective-permute-start(bf16[1040,128]{1,0:T(8,128)(2,1)S(1)} %concatenate.35), channel_id=1, source_target_pairs={{0,1},{1,0},{2,3},{3,2},{4,5},{5,4},{6,7},{7,6},{8,9},{9,8},{10,11... | collective-permute-start | bytes 798728 | tf_op jit(solution)/shard_map/ppermute | solution.py:476
  8.1 16.3 %collective-permute-start.1 = (bf16[1040,128]{1,0:T(8,128)(2,1)S(1)}, bf16[1040,128]{1,0:T(8,128)(2,1)S(1)}, u32[]{:S(2)}, u32[]{:S(2)}) collective-permute-start(bf16[1040,128]{1,0:T(8,128)(2,1)S(1)} %concatenate.36), channel_id=1, source_target_pairs={{0,2},{1,3},{2,0},{3,1},{4,6},{5,7},{6,4},{7,5},{8,10},{9,11},{10,... | collective-permute-start | bytes 798728 | tf_op jit(solution)/shard_map/ppermute | solution.py:476
  8.6 15.8 %collective-permute-start.2 = (bf16[1040,128]{1,0:T(8,128)(2,1)S(1)}, bf16[1040,128]{1,0:T(8,128)(2,1)S(1)}, u32[]{:S(2)}, u32[]{:S(2)}) collective-permute-start(bf16[1040,128]{1,0:T(8,128)(2,1)S(1)} %concatenate.37), channel_id=1, source_target_pairs={{0,3},{1,2},{2,1},{3,0},{4,7},{5,6},{6,5},{7,4},{8,11},{9,10},{10,... | collective-permute-start | bytes 798728 | tf_op jit(solution)/shard_map/ppermute | solution.py:476
  12.0 12.4 %collective-permute-start.4 = (bf16[9,64,128]{2,1,0:T(8,128)(2,1)S(1)}, bf16[9,64,128]{2,1,0:T(8,128)(2,1)S(1)}, u32[]{:S(2)}, u32[]{:S(2)}) collective-permute-start(bf16[9,64,128]{2,1,0:T(8,128)(2,1)S(1)} %convert_element_type.274), channel_id=1, source_target_pairs={{0,16},{1,17},{2,18},{3,19},{4,20},{5,21},{6,22},{7,23},{8,24},{9,... | collective-permute-start | bytes 442376 | tf_op jit(solution)/shard_map/ppermute | solution.py:445
  14.6 9.8 %collective-permute-start.5 = (bf16[9,64,128]{2,1,0:T(8,128)(2,1)S(1)}, bf16[9,64,128]{2,1,0:T(8,128)(2,1)S(1)}, u32[]{:S(2)}, u32[]{:S(2)}) collective-permute-start(bf16[9,64,128]{2,1,0:T(8,128)(2,1)S(1)} %convert_element_type.274), channel_id=1, source_target_pairs={{0,24},{1,25},{2,26},{3,27},{4,28},{5,29},{6,30},{7,31},{8,16},{9,... | collective-permute-start | bytes 442376 | tf_op jit(solution)/shard_map/ppermute | solution.py:445
  24.5 15.8 %collective-permute-start.7 = (bf16[4,9,64,128]{3,2,1,0:T(8,128)(2,1)S(1)}, bf16[4,9,64,128]{3,2,1,0:T(8,128)(2,1)S(1)}, u32[]{:S(2)}, u32[]{:S(2)}) collective-permute-start(bf16[4,9,64,128]{3,2,1,0:T(8,128)(2,1)S(1)} %pad_maximum_fusion.1.refs_5_), channel_id=1, source_target_pairs={{0,4},{1,3},{2,6},{3,1},{4,0},{5,7},{6,2},{7,5},{8,12},{9,11},{10,... | collective-permute-start | bytes 1769480 | tf_op jit(solution)/shard_map/ppermute | solution.py:445
  26.0 14.3 %collective-permute-start.8 = (bf16[4,9,64,128]{3,2,1,0:T(8,128)(2,1)S(1)}, bf16[4,9,64,128]{3,2,1,0:T(8,128)(2,1)S(1)}, u32[]{:S(2)}, u32[]{:S(2)}) collective-permute-start(bf16[4,9,64,128]{3,2,1,0:T(8,128)(2,1)S(1)} %pad_maximum_fusion.1.refs_5_), channel_id=1, source_target_pairs={{0,2},{1,5},{2,0},{3,7},{4,6},{5,1},{6,4},{7,3},{8,10},{9,13},{10,... | collective-permute-start | bytes 1769480 | tf_op jit(solution)/shard_map/ppermute | solution.py:445
  27.9 12.0 %collective-permute-start.10 = (bf16[2,64,512]{2,1,0:T(8,128)(2,1)S(1)}, bf16[2,64,512]{2,1,0:T(8,128)(2,1)S(1)}, u32[]{:S(2)}, u32[]{:S(2)}) collective-permute-start(bf16[2,64,512]{2,1,0:T(8,128)(2,1)S(1)} %pad_maximum_fusion.10), channel_id=1, source_target_pairs={{0,16},{1,17},{2,18},{3,19},{4,20},{5,21},{6,22},{7,23},{8,24},{9,... | collective-permute-start | bytes 393224 | tf_op jit(solution)/shard_map/ppermute | solution.py:445
  40.3 16.1 %collective-permute-start.12 = (bf16[4,9,64,128]{3,2,1,0:T(8,128)(2,1)S(1)}, bf16[4,9,64,128]{3,2,1,0:T(8,128)(2,1)S(1)}, u32[]{:S(2)}, u32[]{:S(2)}) collective-permute-start(bf16[4,9,64,128]{3,2,1,0:T(8,128)(2,1)S(1)} %collective-permute-done.7.refs_6_), channel_id=1, source_target_pairs={{0,2},{1,5},{2,0},{3,7},{4,6},{5,1},{6,4},{7,3},{8,10},{9,13},{10,... | collective-permute-start | bytes 1769480 | tf_op jit(solution)/shard_map/ppermute | solution.py:445
  40.9 16.6 %collective-permute-start.20 = (bf16[4,2,64,512]{3,2,1,0:T(8,128)(2,1)S(1)}, bf16[4,2,64,512]{3,2,1,0:T(8,128)(2,1)S(1)}, u32[]{:S(2)}, u32[]{:S(2)}) collective-permute-start(bf16[4,2,64,512]{3,2,1,0:T(8,128)(2,1)S(1)} %pad_maximum_fusion.2.refs_8_), channel_id=1, source_target_pairs={{0,4},{1,5},{2,6},{3,7},{4,0},{5,1},{6,2},{7,3},{8,12},{9,13},{10,... | collective-permute-start | bytes 1572872 | tf_op jit(solution)/shard_map/ppermute | solution.py:445
  44.5 11.9 %collective-permute-start.14 = (bf16[2,64,512]{2,1,0:T(8,128)(2,1)S(1)}, bf16[2,64,512]{2,1,0:T(8,128)(2,1)S(1)}, u32[]{:S(2)}, u32[]{:S(2)}) collective-permute-start(bf16[2,64,512]{2,1,0:T(8,128)(2,1)S(1)} %pad_maximum_fusion.9), channel_id=1, source_target_pairs={{0,16},{1,17},{2,18},{3,19},{4,20},{5,21},{6,22},{7,23},{8,24},{9,... | collective-permute-start | bytes 393224 | tf_op jit(solution)/shard_map/ppermute | solution.py:445
  45.7 10.7 %collective-permute-start.15 = (bf16[2,64,512]{2,1,0:T(8,128)(2,1)S(1)}, bf16[2,64,512]{2,1,0:T(8,128)(2,1)S(1)}, u32[]{:S(2)}, u32[]{:S(2)}) collective-permute-start(bf16[2,64,512]{2,1,0:T(8,128)(2,1)S(1)} %pad_maximum_fusion.9), channel_id=1, source_target_pairs={{0,24},{1,25},{2,26},{3,27},{4,28},{5,29},{6,30},{7,31},{8,16},{9,... | collective-permute-start | bytes 393224 | tf_op jit(solution)/shard_map/ppermute | solution.py:445
  61.3 15.1 %collective-permute-start.22 = (bf16[4,2,64,512]{3,2,1,0:T(8,128)(2,1)S(1)}, bf16[4,2,64,512]{3,2,1,0:T(8,128)(2,1)S(1)}, u32[]{:S(2)}, u32[]{:S(2)}) collective-permute-start(bf16[4,2,64,512]{3,2,1,0:T(8,128)(2,1)S(1)} %pad_maximum_fusion.3.refs_12_), channel_id=1, source_target_pairs={{0,4},{1,5},{2,6},{3,7},{4,0},{5,1},{6,2},{7,3},{8,12},{9,13},{10,... | collective-permute-start | bytes 1572872 | tf_op jit(solution)/shard_map/ppermute | solution.py:445
  62.9 13.5 %collective-permute-start.23 = (bf16[4,2,64,512]{3,2,1,0:T(8,128)(2,1)S(1)}, bf16[4,2,64,512]{3,2,1,0:T(8,128)(2,1)S(1)}, u32[]{:S(2)}, u32[]{:S(2)}) collective-permute-start(bf16[4,2,64,512]{3,2,1,0:T(8,128)(2,1)S(1)} %pad_maximum_fusion.3.refs_12_), channel_id=1, source_target_pairs={{0,1},{1,0},{2,3},{3,2},{4,5},{5,4},{6,7},{7,6},{8,9},{9,8},{10,11... | collective-permute-start | bytes 1572872 | tf_op jit(solution)/shard_map/ppermute | solution.py:445
  62.9 13.5 %collective-permute-start.21 = (bf16[4,2,64,512]{3,2,1,0:T(8,128)(2,1)S(1)}, bf16[4,2,64,512]{3,2,1,0:T(8,128)(2,1)S(1)}, u32[]{:S(2)}, u32[]{:S(2)}) collective-permute-start(bf16[4,2,64,512]{3,2,1,0:T(8,128)(2,1)S(1)} %pad_maximum_fusion.2.refs_8_), channel_id=1, source_target_pairs={{0,1},{1,0},{2,3},{3,2},{4,5},{5,4},{6,7},{7,6},{8,9},{9,8},{10,11... | collective-permute-start | bytes 1572872 | tf_op jit(solution)/shard_map/ppermute | solution.py:445
  63.4 9.2 %collective-permute-start.25 = (bf16[1024,128]{1,0:T(8,128)(2,1)S(1)}, bf16[1024,128]{1,0:T(8,128)(2,1)S(1)}, u32[]{:S(2)}, u32[]{:S(2)}) collective-permute-start(bf16[1024,128]{1,0:T(8,128)(2,1)S(1)} %get-tuple-element.224), channel_id=1, source_target_pairs={{0,2},{1,3},{2,0},{3,1},{4,6},{5,7},{6,4},{7,5},{8,10},{9,11},{10,... | collective-permute-start | bytes 786440 | tf_op jit(solution)/shard_map/ppermute | solution.py:476
  63.4 13.0 %collective-permute-start.26 = (bf16[1024,128]{1,0:T(8,128)(2,1)S(1)}, bf16[1024,128]{1,0:T(8,128)(2,1)S(1)}, u32[]{:S(2)}, u32[]{:S(2)}) collective-permute-start(bf16[1024,128]{1,0:T(8,128)(2,1)S(1)} %get-tuple-element.223), channel_id=1, source_target_pairs={{0,3},{1,2},{2,1},{3,0},{4,7},{5,6},{6,5},{7,4},{8,11},{9,10},{10,... | collective-permute-start | bytes 786440 | tf_op jit(solution)/shard_map/ppermute | solution.py:476
  93.3 8.7 %collective-permute-start.29 = (bf16[2,2,4,2,64,512]{5,4,3,2,1,0:T(8,128)(2,1)S(1)}, bf16[2,2,4,2,64,512]{5,4,3,2,1,0:T(8,128)(2,1)S(1)}, u32[]{:S(2)}, u32[]{:S(2)}) collective-permute-start(bf16[2,2,4,2,64,512]{5,4,3,2,1,0:T(8,128)(2,1)S(1)} %get-tuple-element.162), channel_id=1, source_target_pairs={{0,1},{1,0},{2,3},{3,2},{4,5},{5,4},{6,7},{7,6},{8,9},{9,8},{10,11... | collective-permute-start | bytes 6291464 | tf_op jit(solution)/shard_map/ppermute | solution.py:445
  102.4 14.9 %collective-permute-start.30 = (bf16[2,4,2,64,512]{4,3,2,1,0:T(8,128)(2,1)S(1)}, bf16[2,4,2,64,512]{4,3,2,1,0:T(8,128)(2,1)S(1)}, u32[]{:S(2)}, u32[]{:S(2)}) collective-permute-start(bf16[2,4,2,64,512]{4,3,2,1,0:T(8,128)(2,1)S(1)} %fusion.2), channel_id=1, source_target_pairs={{0,2},{1,5},{2,0},{3,7},{4,6},{5,1},{6,4},{7,3},{8,10},{9,13},{10,... | collective-permute-start | bytes 3145736 | tf_op jit(solution)/shard_map/ppermute | solution.py:445
  106.9 28.6 %collective-permute-start.36 = (bf16[2,4,9,64,128]{4,3,2,1,0:T(8,128)(2,1)S(1)}, bf16[2,4,9,64,128]{4,3,2,1,0:T(8,128)(2,1)S(1)}, u32[]{:S(2)}, u32[]{:S(2)}) collective-permute-start(bf16[2,4,9,64,128]{4,3,2,1,0:T(8,128)(2,1)S(1)} %fusion), channel_id=1, source_target_pairs={{0,2},{1,5},{2,0},{3,7},{4,6},{5,1},{6,4},{7,3},{8,10},{9,13},{10,... | collective-permute-start | bytes 3538952 | tf_op jit(solution)/shard_map/ppermute | solution.py:445
  118.4 20.1 %collective-permute-start.31 = (bf16[4,2,64,512]{3,2,1,0:T(8,128)(2,1)}, bf16[4,2,64,512]{3,2,1,0:T(8,128)(2,1)}, u32[]{:S(2)}, u32[]{:S(2)}) collective-permute-start(bf16[4,2,64,512]{3,2,1,0:T(8,128)(2,1)} %fusion.4), channel_id=1, source_target_pairs={{0,4},{1,3},{2,6},{3,1},{4,0},{5,7},{6,2},{7,5},{8,12},{9,11},{10,... | collective-permute-start | bytes 1572872 | tf_op jit(solution)/shard_map/ppermute | solution.py:445
  136.8 16.0 %collective-permute-start.37 = (bf16[4,9,64,128]{3,2,1,0:T(8,128)(2,1)}, bf16[4,9,64,128]{3,2,1,0:T(8,128)(2,1)}, u32[]{:S(2)}, u32[]{:S(2)}) collective-permute-start(bf16[4,9,64,128]{3,2,1,0:T(8,128)(2,1)} %fusion.1), channel_id=1, source_target_pairs={{0,4},{1,3},{2,6},{3,1},{4,0},{5,7},{6,2},{7,5},{8,12},{9,11},{10,... | collective-permute-start | bytes 1769480 | tf_op jit(solution)/shard_map/ppermute | solution.py:445
  140.2 20.9 %collective-permute-start.32 = (bf16[2,64,512]{2,1,0:T(8,128)(2,1)S(1)}, bf16[2,64,512]{2,1,0:T(8,128)(2,1)S(1)}, u32[]{:S(2)}, u32[]{:S(2)}) collective-permute-start(bf16[2,64,512]{2,1,0:T(8,128)(2,1)S(1)} %get-tuple-element.206), channel_id=1, source_target_pairs={{0,8},{1,9},{2,10},{3,11},{4,12},{5,13},{6,14},{7,15},{8,0},{9,1},... | collective-permute-start | bytes 393224 | tf_op jit(solution)/shard_map/ppermute | solution.py:445
  149.9 11.3 %collective-permute-start.33 = (bf16[2,64,512]{2,1,0:T(8,128)(2,1)S(1)}, bf16[2,64,512]{2,1,0:T(8,128)(2,1)S(1)}, u32[]{:S(2)}, u32[]{:S(2)}) collective-permute-start(bf16[2,64,512]{2,1,0:T(8,128)(2,1)S(1)} %get-tuple-element.208), channel_id=1, source_target_pairs={{0,16},{1,17},{2,18},{3,19},{4,20},{5,21},{6,22},{7,23},{8,24},{9,... | collective-permute-start | bytes 393224 | tf_op jit(solution)/shard_map/ppermute | solution.py:445
  152.8 10.1 %collective-permute-start.34 = (bf16[2,64,512]{2,1,0:T(8,128)(2,1)S(1)}, bf16[2,64,512]{2,1,0:T(8,128)(2,1)S(1)}, u32[]{:S(2)}, u32[]{:S(2)}) collective-permute-start(bf16[2,64,512]{2,1,0:T(8,128)(2,1)S(1)} %get-tuple-element.207), channel_id=1, source_target_pairs={{0,24},{1,25},{2,26},{3,27},{4,28},{5,29},{6,30},{7,31},{8,16},{9,... | collective-permute-start | bytes 393224 | tf_op jit(solution)/shard_map/ppermute | solution.py:445
  153.0 22.9 %collective-permute-start.43 = (bf16[2,1024,128]{2,1,0:T(8,128)(2,1)S(1)}, bf16[2,1024,128]{2,1,0:T(8,128)(2,1)}, u32[]{:S(2)}, u32[]{:S(2)}) collective-permute-start(bf16[2,1024,128]{2,1,0:T(8,128)(2,1)S(1)} %pad_maximum_fusion.7), channel_id=1, source_target_pairs={{0,2},{1,3},{2,0},{3,1},{4,6},{5,7},{6,4},{7,5},{8,10},{9,11},{10,... | collective-permute-start | bytes 1572872 | tf_op jit(solution)/shard_map/ppermute | solution.py:621
  156.7 9.7 %collective-permute-start.39 = (bf16[9,64,128]{2,1,0:T(8,128)(2,1)S(1)}, bf16[9,64,128]{2,1,0:T(8,128)(2,1)S(1)}, u32[]{:S(2)}, u32[]{:S(2)}) collective-permute-start(bf16[9,64,128]{2,1,0:T(8,128)(2,1)S(1)} %get-tuple-element.203), channel_id=1, source_target_pairs={{0,8},{1,9},{2,10},{3,11},{4,12},{5,13},{6,14},{7,15},{8,0},{9,1},... | collective-permute-start | bytes 442376 | tf_op jit(solution)/shard_map/ppermute | solution.py:445
  161.1 14.9 %collective-permute-start.42 = (bf16[2,1024,128]{2,1,0:T(8,128)(2,1)S(1)}, bf16[2,1024,128]{2,1,0:T(8,128)(2,1)}, u32[]{:S(2)}, u32[]{:S(2)}) collective-permute-start(bf16[2,1024,128]{2,1,0:T(8,128)(2,1)S(1)} %pad_maximum_fusion.6), channel_id=1, source_target_pairs={{0,1},{1,0},{2,3},{3,2},{4,5},{5,4},{6,7},{7,6},{8,9},{9,8},{10,11... | collective-permute-start | bytes 1572872 | tf_op jit(solution)/shard_map/ppermute | solution.py:621
  161.2 13.6 %collective-permute-start.40 = (bf16[9,64,128]{2,1,0:T(8,128)(2,1)S(1)}, bf16[9,64,128]{2,1,0:T(8,128)(2,1)S(1)}, u32[]{:S(2)}, u32[]{:S(2)}) collective-permute-start(bf16[9,64,128]{2,1,0:T(8,128)(2,1)S(1)} %get-tuple-element.205), channel_id=1, source_target_pairs={{0,16},{1,17},{2,18},{3,19},{4,20},{5,21},{6,22},{7,23},{8,24},{9,... | collective-permute-start | bytes 442376 | tf_op jit(solution)/shard_map/ppermute | solution.py:445
  162.9 12.0 %collective-permute-start.41 = (bf16[9,64,128]{2,1,0:T(8,128)(2,1)S(1)}, bf16[9,64,128]{2,1,0:T(8,128)(2,1)S(1)}, u32[]{:S(2)}, u32[]{:S(2)}) collective-permute-start(bf16[9,64,128]{2,1,0:T(8,128)(2,1)S(1)} %get-tuple-element.204), channel_id=1, source_target_pairs={{0,24},{1,25},{2,26},{3,27},{4,28},{5,29},{6,30},{7,31},{8,16},{9,... | collective-permute-start | bytes 442376 | tf_op jit(solution)/shard_map/ppermute | solution.py:445
  166.4 14.1 %collective-permute-start.38 = (bf16[2,1024,128]{2,1,0:T(8,128)(2,1)S(1)}, bf16[2,1024,128]{2,1,0:T(8,128)(2,1)}, u32[]{:S(2)}, u32[]{:S(2)}) collective-permute-start(bf16[2,1024,128]{2,1,0:T(8,128)(2,1)S(1)} %pad_maximum_fusion.4), channel_id=1, source_target_pairs={{0,3},{1,2},{2,1},{3,0},{4,7},{5,6},{6,5},{7,4},{8,11},{9,10},{10,... | collective-permute-start | bytes 1572872 | tf_op jit(solution)/shard_map/ppermute | solution.py:621
  (45 other events, 419.8 us)

commit v4 on v3

--- a/solution.py
+++ b/solution.py
@@ -118,7 +118,7 @@
 
 def conv_forward(place, x0, x1, x2, x3, vec, *rest):
     pieces = rest[:8]
-    w_out, x_out, na_out, conv_out, bias_out, nf, nab, whole, extra, sems, x_sem = rest[8:]
+    w_out, x_out, na_out, resid, slope, bias_out, nf, nab, whole, extra, sems, x_sem = rest[8:]
     full = vec.shape[1]
     seq, own = x_out.shape[0], x0.shape[1]
     blocks = place[3]
@@ -150,7 +150,6 @@
 
     nf[...] = jnp.zeros_like(nf)
     na_out[...] = jnp.zeros_like(na_out)
-    conv_out[...] = jnp.zeros_like(conv_out)
     gain = vec[0:1, :]
     shift = vec[1:2, :]
 
@@ -186,24 +185,28 @@
             axis=1,
         )
         weights = whole[...].reshape(KERNEL * full, full)
-        conv_out[pl.ds(row, ROWS), :] = dot(window, weights) + vec[2:3, :]
+        rows = pl.ds(row, ROWS)
+        conv = dot(window, weights) + vec[2:3, :]
+        phi = phi_of(conv)
+        resid[rows, :] = x_out[rows, :].astype(f32) + conv * phi
+        slope[rows, :] = slope_of(conv, phi)
         return 0
 
     lax.fori_loop(0, blocks, conv_step, 0)
     w_copy.wait()
 
 
-def ffn(place, x_full, conv_out, c0, c1, c2, c3, vec, hbias, *rest):
+def ffn_hidden(place, x_full, resid, c0, c1, c2, c3, vec, hbias, *rest):
     pieces = rest[:8]
-    block_out, resid_out, cab, act, hg, sec, mg, vgrad, hbgrad = rest[8:17]
-    whole, cf, sems, c_sem = rest[17:]
+    block_out, act, hg, sec, mg, wh_out, hbgrad = rest[8:15]
+    whole, sems, c_sem = rest[15:]
     wh, wo = whole.at[0], whole.at[1]
     seq, full = x_full.shape
     hidden = hbias.shape[1]
     own = c0.shape[1]
     blocks = place[3]
 
-    rows = fetch_rows(place, (c0, c1, c2, c3), mg, c_sem)
+    rows = fetch_rows(place, (c0, c1, c2, c3), mg, c_sem.at[0])
     shards = []
     for slot, piece in enumerate(pieces):
         w, dc, dx = slot >> 2, (slot >> 1) & 1, slot & 1
@@ -213,11 +216,11 @@
                 m = place[1] ^ (dy * 2 + dc)
                 shards.append(((slot, z, dy), piece.at[z, dy], whole.at[w], d, m))
     shards = fetch_shards(shards, sems)
-    vgrad[...] = jnp.zeros_like(vgrad)
     hbgrad[...] = jnp.zeros_like(hbgrad)
-    cf[...] = jnp.zeros_like(cf)
     for copy in rows + shards:
         copy.wait()
+    wh_copy = pltpu.make_async_copy(wh, wh_out, c_sem.at[1, 0])
+    wh_copy.start()
 
     def out_store(rows, values):
         for m in range(full // own):
@@ -225,9 +228,8 @@
 
     def row_step(i, _):
         rows = pl.ds(mult(i * ROWS, ROWS), ROWS)
-        conv = conv_out[rows, :]
-        residual = x_full[rows, :].astype(f32) + conv * phi_of(conv)
-        s, inverse = norm_parts(residual)
+        residual = resid[rows, :]
+        s, _ = norm_parts(residual)
         second = (s * vec[3:4, :] + vec[4:5, :]).astype(bf16)
         sec[rows, :] = second
         grad = mg[rows, :]
@@ -241,28 +243,45 @@
             hbgrad[0:1, cols] += jnp.sum(hidden_grad.astype(f32), axis=0, keepdims=True)
         mixed = dot(act[rows, :], wo[...], NT)
         out_store(rows, (residual + (mixed + vec[5:6, :])).astype(bf16))
+        return 0
+
+    def idle_step(i, _):
+        rows = pl.ds(mult(i * ROWS, ROWS), ROWS)
+        out_store(rows, x_full[rows, :])
+        sec[rows, :] = jnp.zeros((ROWS, full), bf16)
+        for ref in (act, hg):
+            ref[rows, :] = jnp.zeros((ROWS, hidden), bf16)
+        return 0
+
+    lax.fori_loop(0, blocks, row_step, 0)
+    lax.fori_loop(blocks, seq // ROWS, idle_step, 0)
+    wh_copy.wait()
+
+
+def norm_backward(place, resid, slope, grad, hg, wh, vec, resid_out, cab, vgrad, cf):
+    seq = resid.shape[0]
+    blocks = place[3]
+    vgrad[...] = jnp.zeros_like(vgrad)
+    cf[...] = jnp.zeros_like(cf)
+
+    def row_step(i, _):
+        rows = pl.ds(mult(i * ROWS, ROWS), ROWS)
         second_grad = dot(hg[rows, :], wh[...], NT)
-        up = grad.astype(f32)
+        s, inverse = norm_parts(resid[rows, :])
+        up = grad[rows, :].astype(f32)
         vgrad[3:4, :] += jnp.sum(second_grad * s, axis=0, keepdims=True)
         vgrad[4:5, :] += jnp.sum(second_grad, axis=0, keepdims=True)
         vgrad[5:6, :] += jnp.sum(up, axis=0, keepdims=True)
         resid_grad = up + norm_back(second_grad * vec[3:4, :], s, inverse)
         resid_out[rows, :] = resid_grad
-        conv = conv_out[rows, :]
-        conv_grad = (resid_grad * slope_of(conv, phi_of(conv))).astype(bf16)
-        rounded = conv_grad.astype(f32)
+        rounded = (resid_grad * slope[rows, :]).astype(bf16).astype(f32)
         cf[pl.ds(mult(i * ROWS + REACH, 8), ROWS), :] = rounded
         vgrad[2:3, :] += jnp.sum(rounded, axis=0, keepdims=True)
         return 0
 
     def idle_step(i, _):
         rows = pl.ds(mult(i * ROWS, ROWS), ROWS)
-        out_store(rows, x_full[rows, :])
-        resid_out[rows, :] = mg[rows, :].astype(f32)
-        for ref in (sec, mg):
-            ref[rows, :] = jnp.zeros((ROWS, full), bf16)
-        for ref in (act, hg):
-            ref[rows, :] = jnp.zeros((ROWS, hidden), bf16)
+        resid_out[rows, :] = grad[rows, :].astype(f32)
         return 0
 
     lax.fori_loop(0, blocks, row_step, 0)
@@ -378,7 +397,21 @@
     )(lengths, *args)
 
 
-def adam_step(weight, first_mom, second, gradient, clip_scale, step_rate, decay_rate):
+def total_share(place, conv_own, c1, c2, c3, ffn_share, v1, v2, bias_grad, conv_share, small):
+    full = small.shape[1]
+    total = conv_own[...]
+    for part in (c1, c2, c3):
+        total = total + part[...].astype(f32)
+    conv_share[...] = total
+    squares = jnp.sum(total * total) + jnp.sum(ffn_share[...] * ffn_share[...])
+    small[0:6, :] = (v1[...] + v2[...])[0:6, :]
+    units = bias_grad.shape[1] // full
+    for row in range(units):
+        small[6 + row : 7 + row, :] = bias_grad[:, row * full : (row + 1) * full]
+    small[6 + units :, :] = jnp.full((small.shape[0] - 6 - units, full), squares, f32)
+
+
+def adam(weight, first_mom, second, gradient, clip_scale, step_rate, decay_rate):
     clipped = gradient * clip_scale
     first_new = BETA_ONE * first_mom + (1.0 - BETA_ONE) * clipped
     second_new = BETA_TWO * second + (1.0 - BETA_TWO) * clipped * clipped
@@ -390,8 +423,28 @@
     return (weight - step_rate * (update_dir + decay_rate * weight), first_new, second_new)
 
 
-def square_sum(values):
-    return jnp.sum(values * values)
+def update(place, small, small_far, conv_share, ffn_share, *rest):
+    states, outs, total = rest[:15], rest[15:31], rest[31]
+    total[...] = small[...] + small_far[...]
+    rows = total.shape[0] - 1
+    own_rows = total[0:rows, :]
+    squares = jnp.sum(own_rows * own_rows, axis=(0, 1), keepdims=True) + total[rows:, 0:1]
+    norm = jnp.sqrt(squares)
+    outs[15][...] = jnp.broadcast_to(norm, outs[15].shape)
+    clip_scale = jnp.minimum(1.0, CLIP_NORM / (norm + 1e-06))
+    gradients = [
+        conv_share[...],
+        ffn_share[0],
+        ffn_share[1],
+        total[0:6, :],
+        total[pl.ds(6 + place[1], 1), :],
+    ]
+    for i, gradient in enumerate(gradients):
+        rates = (MATRIX_RATE, WEIGHT_DECAY) if i < 3 else (VECTOR_RATE, 0.0)
+        scale = clip_scale.reshape((1,) * gradient.ndim)
+        state = [ref[...] for ref in states[3 * i : 3 * i + 3]]
+        for ref, value in zip(outs[3 * i : 3 * i + 3], adam(*state, gradient, scale, *rates)):
+            ref[...] = value
 
 
 def per_device(
@@ -460,11 +513,9 @@
         return add(k[0, 1], r[0, 1], rb[1]).astype(bf16)
 
     def scatter_z(k, r, rb, ra):
-        total = add(k[0, 0, 0], r[0, 0, 0], rb[0, 0], ra[0])
-        for j in range(1, nz):
-            part = add(k[0, 0, j], r[0, 0, j], rb[0, j], ra[j]).astype(bf16)
-            total = total + send(part, across_z[j]).astype(f32)
-        return total
+        own_part = add(k[0, 0, 0], r[0, 0, 0], rb[0, 0], ra[0])
+        parts = [add(k[0, 0, j], r[0, 0, j], rb[0, j], ra[j]).astype(bf16) for j in range(1, nz)]
+        return own_part, [send(part_of, across_z[j + 1]) for j, part_of in enumerate(parts)]
 
     def take_windows(values, extra=None):
         blocks = [lax.dynamic_index_in_dim(values, mp ^ k, 0, False) for k in range(nmp)]
@@ -488,7 +539,7 @@
             values = values + send(values, across_z[step])
             step *= 2
         values = values + send(values, step_x)
-        return values + send(values, step_y)
+        return values, send(values, step_y)
 
     exact, rest = [], hidden_bias
     for _ in range(3):
@@ -513,20 +564,21 @@
     first = jnp.stack(first)
     first_x = send(first, step_x)
     last = gather_z(last)
-    conv_z, conv_a, conv_b, conv_ab, cotangent, first, *last = tie(
-        conv_z, conv_a, conv_b, conv_ab, cotangent, first, *last
+    conv_z, conv_a, conv_b, conv_ab, cotangent, first, first_x, *last = tie(
+        conv_z, conv_a, conv_b, conv_ab, cotangent, first, first_x, *last
     )
     conv_parts = [conv_z, conv_a, conv_b, conv_ab]
     conv_parts += [send(part_of, step_c) for part_of in conv_parts]
     last = jnp.stack(last)
     last_x = send(last, step_x)
-    c_parts = swap(take_windows(cotangent))
+    c_blocks = take_windows(cotangent)
+    c_parts = [lax.ppermute(c_blocks[k], "mp", within[k]) for k in range(2, nmp)]
 
     S = jax.ShapeDtypeStruct
     padded = seq + 2 * REACH
     last, *x_parts = tie(last, *x_parts)
     first_c, last_c = send(first, step_c), send(last, step_c)
-    w_full, x_full, normed, conv_out, bias_all = call(
+    w_full, x_full, normed, residual, slope, bias_all = call(
         conv_forward,
         lengths,
         (*x_parts, vectors, *conv_parts),
@@ -534,7 +586,7 @@
             S((KERNEL, full, full), bf16),
             S((seq, full), bf16),
             S((seq, full), bf16),
-            S((seq, full), f32),
+            *(S((seq, full), f32),) * 2,
             S((nmp, part // own, own), f32),
         ),
         [
@@ -550,33 +602,35 @@
         (0, 1, 2, 3, *range(5, 13)),
         (0,),
     )
-    *tied, conv_out = tie(first, first_x, first_c, last, last_x, last_c, *c_parts, conv_out)
+    *tied, residual = tie(first, first_x, first_c, last, last_x, last_c, *c_blocks[:2], *c_parts, residual)
     first, first_x, first_c, last, last_x, last_c, *c_parts = tied
+    c_parts[1] = lax.ppermute(c_parts[1], "mp", within[1])
     ffn_parts = [first, first_x, first_c, send(first_x, step_c)]
     ffn_parts += [last, last_x, last_c, send(last_x, step_c)]
-    block_rel, resid_grad, conv_grad, active, hidden_grad, second, mix_grad, vgrad_two, bias_grad = call(
-        ffn,
+    block_rel, active, hidden_grad, second, mix_grad, hidden_full, bias_grad = call(
+        ffn_hidden,
         lengths,
-        (x_full, conv_out, *c_parts, vectors, bias_all.reshape(1, hidden), *ffn_parts),
+        (x_full, residual, *c_parts, vectors, bias_all.reshape(1, hidden), *ffn_parts),
         (
             S((nmp, seq, own), bf16),
-            S((seq, full), f32),
-            S((2, padded, full), bf16),
             *(S((seq, hidden), bf16),) * 2,
             *(S((seq, full), bf16),) * 2,
-            S((8, full), f32),
+            S((full, hidden), bf16),
             S((1, hidden), f32),
         ),
         [
             pltpu.VMEM((2, full, hidden), bf16),
-            pltpu.VMEM((padded + 8, full), f32),
             pltpu.SemaphoreType.DMA((8, nz, 2)),
-            pltpu.SemaphoreType.DMA((nmp,)),
+            pltpu.SemaphoreType.DMA((2, nmp)),
         ],
-        8 * seq * hidden * full,
+        6 * seq * hidden * full,
         20,
         (2, 3, 4, 5, *range(8, 16)),
-    )
+        (5,),
+    )
+    block_parts = [block_rel[k] for k in range(nmp)]
+    for k in (1, 2):
+        block_parts[k] = lax.ppermute(block_parts[k], "mp", within[k])
     ffn_keep, ffn_give = call(
         ffn_weight_grad,
         lengths,
@@ -586,8 +640,22 @@
         4 * seq * hidden * full,
         12,
     )
+    ffn_give, ffn_keep, hidden_grad, *block_parts[1:] = tie(
+        ffn_give, ffn_keep, hidden_grad, *block_parts[1:]
+    )
     ffn_r = send(ffn_give, step_c)
-    ffn_keep, normed = tie(ffn_keep, normed)
+    block_parts[3] = lax.ppermute(block_parts[3], "mp", within[3])
+    resid_grad, conv_grad, vgrad_two = call(
+        norm_backward,
+        lengths,
+        (residual, slope, mix_grad, hidden_grad, hidden_full, vectors),
+        (S((seq, full), f32), S((2, padded, full), bf16), S((8, full), f32)),
+        [pltpu.VMEM((padded + 8, full), f32)],
+        2 * seq * hidden * full,
+        16,
+    )
+    ffn_sum, conv_grad, block_parts[3] = tie(scatter_b(ffn_keep, ffn_r), conv_grad, block_parts[3])
+    ffn_rb = send(ffn_sum, step_yx)
     conv_keep, conv_give = call(
         conv_weight_grad,
         lengths,
@@ -597,9 +665,9 @@
         2 * seq * KERNEL * full * full,
         16,
     )
+    conv_give, conv_keep, conv_grad, ffn_rb = tie(conv_give, conv_keep, conv_grad, ffn_rb)
     conv_r = send(conv_give, step_c)
-    ffn_sum, conv_keep, conv_grad = tie(scatter_b(ffn_keep, ffn_r), conv_keep, conv_grad)
-    ffn_rb = send(ffn_sum, step_yx)
+    ffn_ra = send(scatter_a(ffn_keep, ffn_r, ffn_rb), step_xy)
     in_rel, vgrad_one = call(
         conv_backward,
         lengths,
@@ -609,47 +677,52 @@
         1,
         16,
     )
-    conv_sum, in_rel = tie(scatter_b(conv_keep, conv_r), in_rel)
+    conv_sum, in_rel, ffn_ra = tie(scatter_b(conv_keep, conv_r), in_rel, ffn_ra)
     conv_rb = send(conv_sum, step_yx)
-    ffn_ra = send(scatter_a(ffn_keep, ffn_r, ffn_rb), step_xy)
-    conv_ra = send(scatter_a(conv_keep, conv_r, conv_rb), step_xy)
-    ffn_share = scatter_z(ffn_keep, ffn_r, ffn_rb, ffn_ra)
-    conv_ra, in_rel, block_rel = tie(conv_ra, in_rel, block_rel)
-    conv_share = scatter_z(conv_keep, conv_r, conv_rb, conv_ra)
-    out_parts = [jnp.stack([block_rel[k], in_rel[k]]) for k in range(nmp)]
-    for k in range(1, nmp):
-        out_parts[k] = lax.ppermute(out_parts[k], "mp", within[k])
-    conv_share, *out_parts[:-1] = tie(conv_share, *out_parts[:-1])
-    ffn_share, out_parts[-1] = tie(ffn_share, out_parts[-1])
-    outputs = in_order(out_parts)
-    block_output, input_grad = outputs[:, 0], outputs[:, 1].astype(f32)
-
-    squares = square_sum(conv_share) + square_sum(ffn_share)
-    small = jnp.concatenate(
-        [
-            (vgrad_one + vgrad_two)[:6],
-            bias_grad.reshape(hidden // full, full),
-            jnp.broadcast_to(squares, (1, full)),
-        ]
-    )
-    small = all_sum(small)
-    vector_sum, bias_sum = small[:6], small[6:-1].reshape(hidden)
-    hidden_share, output_share = ffn_share[0], ffn_share[1].T
-    grad_norm = jnp.sqrt(small[-1, 0] + square_sum(small[:-1]))
-    clip_scale = jnp.minimum(1.0, CLIP_NORM / (grad_norm + 1e-06))
-    bias_share = lax.dynamic_slice_in_dim(bias_sum, mp * part, part, 0)
+    ffn_own, ffn_rest = scatter_z(ffn_keep, ffn_r, ffn_rb, ffn_ra)
+    ffn_share = add(ffn_own, *ffn_rest)
+    conv_sum, ffn_share = tie(scatter_a(conv_keep, conv_r, conv_rb), ffn_share)
+    conv_ra = send(conv_sum, step_xy)
+    conv_ra, in_rel = tie(conv_ra, in_rel)
+    conv_own, conv_rest = scatter_z(conv_keep, conv_r, conv_rb, conv_ra)
+    for part_of in conv_rest[3:]:
+        conv_own = conv_own + part_of.astype(f32)
+    in_parts = swap([in_rel[k] for k in range(nmp)])
+    conv_own, *tied = tie(conv_own, *conv_rest[:3], *in_parts)
+    conv_rest, in_parts = tied[:3], tied[3:]
+    block_output = in_order(block_parts)
+    input_grad = in_order(in_parts).astype(f32)
+
+    conv_share, small = call(
+        total_share,
+        lengths,
+        (conv_own, *conv_rest, ffn_share, vgrad_one, vgrad_two, bias_grad),
+        (S((KERNEL, di, own), f32), S((7 + hidden // full, full), f32)),
+        [],
+        1,
+        16,
+    )
+    small, small_far = all_sum(small)
     matrices = (
-        (conv_master, conv_first, conv_second, conv_share),
-        (hidden_master, hidden_first, hidden_second, hidden_share),
-        (output_master, output_first, output_second, output_share),
-    )
-    small_ones = (
-        (vectors, vector_first, vector_second, vector_sum),
-        (hidden_bias, bias_first, bias_second, bias_share),
-    )
-    updated = [adam_step(*m, clip_scale, MATRIX_RATE, WEIGHT_DECAY) for m in matrices]
-    updated += [adam_step(*m, clip_scale, VECTOR_RATE, 0.0) for m in small_ones]
-    return (block_output, input_grad, grad_norm, *(leaf for new in updated for leaf in new))
+        *(conv_master, conv_first, conv_second),
+        *(hidden_master, hidden_first, hidden_second),
+        *(output_master.T, output_first.T, output_second.T),
+    )
+    vector_ones = (vectors, vector_first, vector_second)
+    bias_ones = [v.reshape(1, part) for v in (hidden_bias, bias_first, bias_second)]
+    states = (*matrices, *vector_ones, *bias_ones)
+    *updated, norm = call(
+        update,
+        lengths,
+        (small, small_far, conv_share, ffn_share, *states),
+        (*(S(v.shape, f32) for v in states), S((1, 1), f32)),
+        [pltpu.VMEM(small.shape, f32)],
+        1,
+        16,
+    )
+    updated[6:9] = [v.T for v in updated[6:9]]
+    updated[12:] = [v.reshape(part) for v in updated[12:]]
+    return (block_output, input_grad, norm.reshape(()), *updated)
 
 
 def solution(mesh):

time: 211 us -> 202 us (0.957); the launches traced: 209 us -> 203 us
  other arithmetic: 20.4 us -> 6.64 us
  starting transfers between devices: 61.6 us -> 68.3 us
  Pallas kernels: 29 us -> 33 us
  between operations: 5 us -> 1.36 us
    ppermute x6, waiting for transfers between devices: 9.18 us -> 0.02 us  [swap(): lax.ppermute(blocks[k], 'mp', within[k])]
    ppermute x3 -> x6, waiting for transfers between devices: 3.87 us -> 12.7 us  [the longest x2 6.97 us: per_device(): lax.ppermute(c_blocks[k], 'mp', within[k])]
    pallas_call x5 -> x8, Pallas kernels: 29 us -> 33 us  [call(): pl.pallas_call(placed(kernel), out_shape=outs, in_specs=[pl.BlockSpec(mem...]
    sub x5 -> x0, other arithmetic: 3.99 us -> none  [adam_step(): weight - step_rate * (update_dir + decay_rate * weight)]
    ppermute x3 -> x6, starting transfers between devices: 2.16 us -> 5.92 us  [the longest x2 3.17 us: per_device(): block_parts[k] = lax.ppermute(block_parts[k], 'mp', within[k])]
    ppermute x40, starting transfers between devices: 54.9 us -> 58.6 us  [send(): return lax.ppermute(values, axes, pairs)]
    convert_element_type x3, other arithmetic: 5.12 us -> 2.11 us  [the longest x1 1.5 us: per_device(): input_grad = in_order(in_parts).astype(f32)]
    add x4 -> x1, other arithmetic: 2.36 us -> 0.12 us  [add(): total = total + term.astype(f32)]
  transfers between devices with their start and end apart: 49 -> 52, of which waited for: 23 -> 25; matrix products, arithmetic and copies ran while one was open for 7% -> 2% of each run, Pallas kernels for 7% -> 12%
where the time goes in v4:
time: 202 us; the launch traced here: 203 us
  waiting for transfers between devices  90.2 us (45%)
  starting transfers between devices  68.3 us (34%)
  Pallas kernels  33 us (16%)
  other arithmetic  6.64 us (3%)
  local copies, waits for them, and re-layouts  2.96 us (1%)
    ppermute x40, waiting for transfers between devices, send(): return lax.ppermute(values, axes, pairs)  77.5 us
    ppermute x40, starting transfers between devices, send(): return lax.ppermute(values, axes, pairs)  58.6 us
    pallas_call x8, Pallas kernels, call(): pl.pallas_call(placed(kernel), out_shape=outs, in_specs=[pl.BlockSpec(mem...  33 us
    ppermute x2, waiting for transfers between devices, per_device(): lax.ppermute(c_blocks[k], 'mp', within[k])  6.97 us
  transfers between devices with their start and end apart: 52, of which 25 were waited for; matrix products, arithmetic and copies ran while one was open for 2% of the time, Pallas kernels for 12%

profile of v4, /device:TPU:0, one launch (start us, length us, event | category | flops | bytes accessed | tf_op | source)
XLA Modules:
  0.0 202.6 jit_solution(16535984739868640468)
XLA Ops:
  3.4 3.1 %collective-permute-start.3 = (bf16[9,64,128]{2,1,0:T(8,128)(2,1)S(1)}, bf16[9,64,128]{2,1,0:T(8,128)(2,1)S(1)}, u32[]{:S(2)}, u32[]{:S(2)}) collective-permute-start(bf16[9,64,128]{2,1,0:T(8,128)(2,1)S(1)} %convert_element_type.262), channel_id=1, source_target_pairs={{0,8},{1,9},{2,10},{3,11},{4,12},{5,13},{6,14},{7,15},{8,0},{9,1},... | collective-permute-start | bytes 442376 | tf_op jit(solution)/shard_map/ppermute | solution.py:498
  12.0 2.6 %collective-permute-start.4 = (bf16[9,64,128]{2,1,0:T(8,128)(2,1)S(1)}, bf16[9,64,128]{2,1,0:T(8,128)(2,1)S(1)}, u32[]{:S(2)}, u32[]{:S(2)}) collective-permute-start(bf16[9,64,128]{2,1,0:T(8,128)(2,1)S(1)} %convert_element_type.262), channel_id=1, source_target_pairs={{0,16},{1,17},{2,18},{3,19},{4,20},{5,21},{6,22},{7,23},{8,24},{9,... | collective-permute-start | bytes 442376 | tf_op jit(solution)/shard_map/ppermute | solution.py:498
  14.9 9.5 %collective-permute-done.4 = bf16[9,64,128]{2,1,0:T(8,128)(2,1)S(1)} collective-permute-done((bf16[9,64,128]{2,1,0:T(8,128)(2,1)S(1)}, bf16[9,64,128]{2,1,0:T(8,128)(2,1)S(1)}, u32[]{:S(2)}, u32[]{:S(2)}) %collective-permute-start.4) | collective-permute-done | bytes 147488 | tf_op jit(solution)/shard_map/ppermute | solution.py:498
  28.0 3.3 %collective-permute-start.10 = (bf16[2,64,512]{2,1,0:T(8,128)(2,1)S(1)}, bf16[2,64,512]{2,1,0:T(8,128)(2,1)S(1)}, u32[]{:S(2)}, u32[]{:S(2)}) collective-permute-start(bf16[2,64,512]{2,1,0:T(8,128)(2,1)S(1)} %pad_maximum_fusion.6), channel_id=1, source_target_pairs={{0,16},{1,17},{2,18},{3,19},{4,20},{5,21},{6,22},{7,23},{8,24},{9,... | collective-permute-start | bytes 393224 | tf_op jit(solution)/shard_map/ppermute | solution.py:498
  32.5 7.4 %collective-permute-done.10 = bf16[2,64,512]{2,1,0:T(8,128)(2,1)S(1)} collective-permute-done((bf16[2,64,512]{2,1,0:T(8,128)(2,1)S(1)}, bf16[2,64,512]{2,1,0:T(8,128)(2,1)S(1)}, u32[]{:S(2)}, u32[]{:S(2)}) %collective-permute-start.10) | collective-permute-done | bytes 131104 | tf_op jit(solution)/shard_map/ppermute | solution.py:498
  41.9 2.6 %collective-permute-start.14 = (bf16[2,64,512]{2,1,0:T(8,128)(2,1)S(1)}, bf16[2,64,512]{2,1,0:T(8,128)(2,1)S(1)}, u32[]{:S(2)}, u32[]{:S(2)}) collective-permute-start(bf16[2,64,512]{2,1,0:T(8,128)(2,1)S(1)} %pad_maximum_fusion.5), channel_id=1, source_target_pairs={{0,8},{1,9},{2,10},{3,11},{4,12},{5,13},{6,14},{7,15},{8,0},{9,1},... | collective-permute-start | bytes 393224 | tf_op jit(solution)/shard_map/ppermute | solution.py:498
  48.9 7.5 %collective-permute-done.15 = bf16[2,64,512]{2,1,0:T(8,128)(2,1)S(1)} collective-permute-done((bf16[2,64,512]{2,1,0:T(8,128)(2,1)S(1)}, bf16[2,64,512]{2,1,0:T(8,128)(2,1)S(1)}, u32[]{:S(2)}, u32[]{:S(2)}) %collective-permute-start.15) | collective-permute-done | bytes 131104 | tf_op jit(solution)/shard_map/ppermute | solution.py:498
  56.4 2.4 %collective-permute-start.17 = (bf16[4,9,64,128]{3,2,1,0:T(8,128)(2,1)S(1)}, bf16[4,9,64,128]{3,2,1,0:T(8,128)(2,1)S(1)}, u32[]{:S(2)}, u32[]{:S(2)}) collective-permute-start(bf16[4,9,64,128]{3,2,1,0:T(8,128)(2,1)S(1)} %pad_maximum_fusion.1.refs_5_), channel_id=1, source_target_pairs={{0,1},{1,0},{2,3},{3,2},{4,5},{5,4},{6,7},{7,6},{8,9},{9,8},{10,11... | collective-permute-start | bytes 1769480 | tf_op jit(solution)/shard_map/ppermute | solution.py:498
  63.8 4.9 %shard_map.313 = (bf16[9,512,512]{2,1,0:T(8,128)(2,1)S(1)}, bf16[1024,512]{1,0:T(8,128)(2,1)S(1)}, bf16[1024,512]{1,0:T(8,128)(2,1)S(1)}, f32[1024,512]{1,0:T(8,...) custom-call(s32[4]{0:T(128)S(1)} %copy-done.12, bf16[1040,128]{1,0:T(8,128)(2,1)S(1)} %concatenate.28.refs_0_, ...), custom_call_target="tpu_custom_call" | custom-call | flops 4831838208 | bytes 16814080 | tf_op jit(solution)/shard_map/pallas_call | solution.py:388
  68.7 2.5 %collective-permute-done.24.refs_4_ = bf16[1024,128]{1,0:T(8,128)(2,1)S(1)} collective-permute-done((bf16[1024,128]{1,0:T(8,128)(2,1)S(1)}, bf16[1024,128]{1,0:T(8,128)(2,1)S(1)}, u32[]{:S(2)}, u32[]{:S(2)}) %collective-permute-start.24) | collective-permute-done | bytes 262176 | tf_op jit(solution)/shard_map/ppermute | solution.py:575
  71.2 4.5 %collective-permute-done.25.refs_5_ = bf16[1024,128]{1,0:T(8,128)(2,1)S(1)} collective-permute-done((bf16[1024,128]{1,0:T(8,128)(2,1)S(1)}, bf16[1024,128]{1,0:T(8,128)(2,1)S(1)}, u32[]{:S(2)}, u32[]{:S(2)}) %collective-permute-start.25) | collective-permute-done | bytes 262176 | tf_op jit(solution)/shard_map/ppermute | solution.py:575
  76.7 2.2 %collective-permute-done.26.refs_3_ = bf16[1024,128]{1,0:T(8,128)(2,1)S(1)} collective-permute-done((bf16[1024,128]{1,0:T(8,128)(2,1)S(1)}, bf16[1024,128]{1,0:T(8,128)(2,1)S(1)}, u32[]{:S(2)}, u32[]{:S(2)}) %collective-permute-start.26) | collective-permute-done | bytes 262176 | tf_op jit(solution)/shard_map/ppermute | solution.py:607
  78.8 5.7 %shard_map.314 = (bf16[4,1024,128]{2,1,0:T(8,128)(2,1)S(1)}, bf16[1024,2048]{1,0:T(8,128)(2,1)S(1)}, bf16[1024,2048]{1,0:T(8,128)(2,1)S(1)}, bf16[1024,512]{1,0:...) custom-call(s32[4]{0:T(128)S(1)} %copy-done.12, ...), custom_call_target="tpu_custom_call" | custom-call | flops 6442450944 | bytes 22048768 | tf_op jit(solution)/shard_map/pallas_call | solution.py:388
  85.1 2.7 %collective-permute-start.30 = (bf16[1024,128]{1,0:T(8,128)(2,1)S(1)}, bf16[1024,128]{1,0:T(8,128)(2,1)S(1)}, u32[]{:S(2)}, u32[]{:S(2)}) collective-permute-start(bf16[1024,128]{1,0:T(8,128)(2,1)S(1)} %get-tuple-element.274), channel_id=1, source_target_pairs={{0,2},{1,3},{2,0},{3,1},{4,6},{5,7},{6,4},{7,5},{8,10},{9,11},{10,... | collective-permute-start | bytes 786440 | tf_op jit(solution)/shard_map/ppermute | solution.py:633
  87.8 6.8 %shard_map.315 = (bf16[2,2,4,2,64,512]{5,4,3,2,1,0:T(8,128)(2,1)S(1)}, bf16[2,2,4,2,64,512]{5,4,3,2,1,0:T(8,128)(2,1)S(1)}) custom-call(s32[4]{0:T(128)S(1)} %copy-done.12, bf16[1024,512]{1,0:T(8,128)(2,1)S(1)} %get-tuple-element.189.refs_0_, bf16[1024,2048]{1,0:T(8,128)(2,1)S(1)} %get-tuple-element.199.refs_1_.refs_3_, ...), custom_call_target="tpu_custom_call" | custom-call | flops 4294967296 | bytes 14680064 | tf_op jit(solution)/shard_map/pallas_call | solution.py:388
  96.2 2.1 %shard_map.316 = (f32[1024,512]{1,0:T(8,128)S(1)}, bf16[2,1088,512]{2,1,0:T(8,128)(2,1)S(1)}, f32[8,512]{1,0:T(8,128)S(1)}) custom-call(s32[4]{0:T(128)S(1)} %copy-done.12, f32[1024,512]{1,0:T(8,128)S(1)} %get-tuple-element.177.refs_1_.refs_0_, f32[1024,512]{1,0:T(8,128)S(1)} %get-tuple-element.198.refs_1_, ...), custom_call_target="tpu_custom_call" | custom-call | flops 2147483648 | bytes 15888384 | tf_op jit(solution)/shard_map/pallas_call | solution.py:388
  99.2 3.6 %collective-permute-done.32 = bf16[1024,128]{1,0:T(8,128)(2,1)S(1)} collective-permute-done((bf16[1024,128]{1,0:T(8,128)(2,1)S(1)}, bf16[1024,128]{1,0:T(8,128)(2,1)S(1)}, u32[]{:S(2)}, u32[]{:S(2)}) %collective-permute-start.32) | collective-permute-done | bytes 262176 | tf_op jit(solution)/shard_map/ppermute | solution.py:647
  104.1 8.1 %shard_map.317 = (bf16[2,2,4,9,64,128]{5,4,3,2,1,0:T(8,128)(2,1)S(1)}, bf16[2,2,4,9,64,128]{5,4,3,2,1,0:T(8,128)(2,1)S(1)}) custom-call(s32[4]{0:T(128)S(1)} %copy-done.12, bf16[1024,512]{1,0:T(8,128)(2,1)S(1)} %get-tuple-element.206.refs_0_, bf16[2,1088,512]{2,1,0:T(8,128)(2,1)S(1)} %get-tuple-element.213.refs_1_), custom_call_target="tpu_custom_call" | custom-call | flops 4831838208 | bytes 7995392 | tf_op jit(solution)/shard_map/pallas_call | solution.py:388
  112.2 5.5 %collective-permute-done.33 = bf16[2,4,2,64,512]{4,3,2,1,0:T(8,128)(2,1)S(1)} collective-permute-done((bf16[2,4,2,64,512]{4,3,2,1,0:T(8,128)(2,1)S(1)}, bf16[2,4,2,64,512]{4,3,2,1,0:T(8,128)(2,1)S(1)}, u32[]{:S(2)}, u32[]{:S(2)}) %collective-permute-start.33) | collective-permute-done | bytes 1048608 | tf_op jit(solution)/shard_map/ppermute | solution.py:498
  118.0 2.4 %collective-permute-start.35 = (bf16[4,2,64,512]{3,2,1,0:T(8,128)(2,1)S(1)}, bf16[4,2,64,512]{3,2,1,0:T(8,128)(2,1)S(1)}, u32[]{:S(2)}, u32[]{:S(2)}) collective-permute-start(bf16[4,2,64,512]{3,2,1,0:T(8,128)(2,1)S(1)} %fusion.3), channel_id=1, source_target_pairs={{0,4},{1,3},{2,6},{3,1},{4,0},{5,7},{6,2},{7,5},{8,12},{9,11},{10,... | collective-permute-start | bytes 1572872 | tf_op jit(solution)/shard_map/ppermute | solution.py:498
  120.4 2.3 %shard_map.318 = (bf16[4,1024,128]{2,1,0:T(8,128)(2,1)S(1)}, f32[8,512]{1,0:T(8,128)S(1)}) custom-call(s32[4]{0:T(128)S(1)} %copy-done.12, bf16[1024,512]{1,0:T(8,128)(2,1)S(1)} %get-tuple-element.171.refs_0_, bf16[2,1088,512]{2,1,0:T(8,128)(2,1)S(1)} %get-tuple-element.213.refs_1_, f32[1024,512]{1,0:T(8,128)S(1)} %get-tuple-element.214.refs_2_, ...), custom_call_target="tpu_custom_call" | custom-call | flops 1 | bytes 11169792 | tf_op jit(solution)/shard_map/pallas_call | solution.py:388
  123.1 4.4 %collective-permute-done.35 = bf16[4,2,64,512]{3,2,1,0:T(8,128)(2,1)S(1)} collective-permute-done((bf16[4,2,64,512]{3,2,1,0:T(8,128)(2,1)S(1)}, bf16[4,2,64,512]{3,2,1,0:T(8,128)(2,1)S(1)}, u32[]{:S(2)}, u32[]{:S(2)}) %collective-permute-start.35) | collective-permute-done | bytes 524320 | tf_op jit(solution)/shard_map/ppermute | solution.py:498
  128.6 7.9 %collective-permute-start.37 = (bf16[2,64,512]{2,1,0:T(8,128)(2,1)S(1)}, bf16[2,64,512]{2,1,0:T(8,128)(2,1)S(1)}, u32[]{:S(2)}, u32[]{:S(2)}) collective-permute-start(bf16[2,64,512]{2,1,0:T(8,128)(2,1)S(1)} %get-tuple-element.258), channel_id=1, source_target_pairs={{0,8},{1,9},{2,10},{3,11},{4,12},{5,13},{6,14},{7,15},{8,0},{9,1},... | collective-permute-start | bytes 393224 | tf_op jit(solution)/shard_map/ppermute | solution.py:498
  140.8 8.4 %collective-permute-done.38 = bf16[2,64,512]{2,1,0:T(8,128)(2,1)S(1)} collective-permute-done((bf16[2,64,512]{2,1,0:T(8,128)(2,1)S(1)}, bf16[2,64,512]{2,1,0:T(8,128)(2,1)S(1)}, u32[]{:S(2)}, u32[]{:S(2)}) %collective-permute-start.38) | collective-permute-done | bytes 131104 | tf_op jit(solution)/shard_map/ppermute | solution.py:498
  149.8 9.7 %collective-permute-done.40 = bf16[4,9,64,128]{3,2,1,0:T(8,128)(2,1)S(1)} collective-permute-done((bf16[4,9,64,128]{3,2,1,0:T(8,128)(2,1)S(1)}, bf16[4,9,64,128]{3,2,1,0:T(8,128)(2,1)S(1)}, u32[]{:S(2)}, u32[]{:S(2)}) %collective-permute-start.40) | collective-permute-done | bytes 589856 | tf_op jit(solution)/shard_map/ppermute | solution.py:498
  164.0 2.1 %collective-permute-start.42 = (bf16[9,64,128]{2,1,0:T(8,128)(2,1)S(1)}, bf16[9,64,128]{2,1,0:T(8,128)(2,1)S(1)}, u32[]{:S(2)}, u32[]{:S(2)}) collective-permute-start(bf16[9,64,128]{2,1,0:T(8,128)(2,1)S(1)} %get-tuple-element.255), channel_id=1, source_target_pairs={{0,16},{1,17},{2,18},{3,19},{4,20},{5,21},{6,22},{7,23},{8,24},{9,... | collective-permute-start | bytes 442376 | tf_op jit(solution)/shard_map/ppermute | solution.py:498
  166.1 2.5 %collective-permute-start.43 = (bf16[9,64,128]{2,1,0:T(8,128)(2,1)S(1)}, bf16[9,64,128]{2,1,0:T(8,128)(2,1)S(1)}, u32[]{:S(2)}, u32[]{:S(2)}) collective-permute-start(bf16[9,64,128]{2,1,0:T(8,128)(2,1)S(1)} %get-tuple-element.254), channel_id=1, source_target_pairs={{0,24},{1,25},{2,26},{3,27},{4,28},{5,29},{6,30},{7,31},{8,16},{9,... | collective-permute-start | bytes 442376 | tf_op jit(solution)/shard_map/ppermute | solution.py:498
  168.6 9.2 %collective-permute-done.42.refs_2_ = bf16[9,64,128]{2,1,0:T(8,128)(2,1)S(1)} collective-permute-done((bf16[9,64,128]{2,1,0:T(8,128)(2,1)S(1)}, bf16[9,64,128]{2,1,0:T(8,128)(2,1)S(1)}, u32[]{:S(2)}, u32[]{:S(2)}) %collective-permute-start.42) | collective-permute-done | bytes 147488 | tf_op jit(solution)/shard_map/ppermute | solution.py:498
  181.6 3.2 %collective-permute-start.48 = (f32[11,512]{1,0:T(8,128)S(1)}, f32[11,512]{1,0:T(8,128)S(1)}, u32[]{:S(2)}, u32[]{:S(2)}) collective-permute-start(f32[11,512]{1,0:T(8,128)S(1)} %add.207), channel_id=1, source_target_pairs={{0,8},{1,9},{2,10},{3,11},{4,12},{5,13},{6,14},{7,15},{8,0},{9,1},... | collective-permute-start | bytes 67592 | tf_op jit(solution)/shard_map/ppermute | solution.py:498
  186.7 3.5 %collective-permute-start.49 = (f32[11,512]{1,0:T(8,128)S(1)}, f32[11,512]{1,0:T(8,128)S(1)}, u32[]{:S(2)}, u32[]{:S(2)}) collective-permute-start(f32[11,512]{1,0:T(8,128)S(1)} %add.208), channel_id=1, source_target_pairs={{0,16},{1,17},{2,18},{3,19},{4,20},{5,21},{6,22},{7,23},{8,24},{9,... | collective-permute-start | bytes 67592 | tf_op jit(solution)/shard_map/ppermute | solution.py:498
  192.9 3.1 %collective-permute-done.50 = f32[11,512]{1,0:T(8,128)S(1)} collective-permute-done((f32[11,512]{1,0:T(8,128)S(1)}, f32[11,512]{1,0:T(8,128)S(1)}, u32[]{:S(2)}, u32[]{:S(2)}) %collective-permute-start.50) | collective-permute-done | bytes 22560 | tf_op jit(solution)/shard_map/ppermute | solution.py:498
  200.1 2.3 %shard_map.320 = (f32[9,64,128]{2,1,0:T(8,128)}, f32[9,64,128]{2,1,0:T(8,128)}, f32[9,64,128]{2,1,0:T(8,128)}, f32[64,512]{1,0:T(8,128)}, f32[64,512]{1,0:T(8,12...) custom-call(s32[4]{0:T(128)S(1)} %copy-done.12, ...), custom_call_target="tpu_custom_call" | custom-call | flops 1 | bytes 4030468 | tf_op jit(solution)/shard_map/pallas_call | solution.py:388
  (157 shorter events, 53.0 us)
Async XLA Ops:
  3.4 11.2 %collective-permute-start.3 = (bf16[9,64,128]{2,1,0:T(8,128)(2,1)S(1)}, bf16[9,64,128]{2,1,0:T(8,128)(2,1)S(1)}, u32[]{:S(2)}, u32[]{:S(2)}) collective-permute-start(bf16[9,64,128]{2,1,0:T(8,128)(2,1)S(1)} %convert_element_type.262), channel_id=1, source_target_pairs={{0,8},{1,9},{2,10},{3,11},{4,12},{5,13},{6,14},{7,15},{8,0},{9,1},... | collective-permute-start | bytes 442376 | tf_op jit(solution)/shard_map/ppermute | solution.py:498
  8.1 16.3 %collective-permute-start = (bf16[1040,128]{1,0:T(8,128)(2,1)S(1)}, bf16[1040,128]{1,0:T(8,128)(2,1)S(1)}, u32[]{:S(2)}, u32[]{:S(2)}) collective-permute-start(bf16[1040,128]{1,0:T(8,128)(2,1)S(1)} %concatenate.29), channel_id=1, source_target_pairs={{0,1},{1,0},{2,3},{3,2},{4,5},{5,4},{6,7},{7,6},{8,9},{9,8},{10,11... | collective-permute-start | bytes 798728 | tf_op jit(solution)/shard_map/ppermute | solution.py:527
  8.1 16.3 %collective-permute-start.1 = (bf16[1040,128]{1,0:T(8,128)(2,1)S(1)}, bf16[1040,128]{1,0:T(8,128)(2,1)S(1)}, u32[]{:S(2)}, u32[]{:S(2)}) collective-permute-start(bf16[1040,128]{1,0:T(8,128)(2,1)S(1)} %concatenate.30), channel_id=1, source_target_pairs={{0,2},{1,3},{2,0},{3,1},{4,6},{5,7},{6,4},{7,5},{8,10},{9,11},{10,... | collective-permute-start | bytes 798728 | tf_op jit(solution)/shard_map/ppermute | solution.py:527
  8.6 15.8 %collective-permute-start.2 = (bf16[1040,128]{1,0:T(8,128)(2,1)S(1)}, bf16[1040,128]{1,0:T(8,128)(2,1)S(1)}, u32[]{:S(2)}, u32[]{:S(2)}) collective-permute-start(bf16[1040,128]{1,0:T(8,128)(2,1)S(1)} %concatenate.31), channel_id=1, source_target_pairs={{0,3},{1,2},{2,1},{3,0},{4,7},{5,6},{6,5},{7,4},{8,11},{9,10},{10,... | collective-permute-start | bytes 798728 | tf_op jit(solution)/shard_map/ppermute | solution.py:527
  12.0 12.4 %collective-permute-start.4 = (bf16[9,64,128]{2,1,0:T(8,128)(2,1)S(1)}, bf16[9,64,128]{2,1,0:T(8,128)(2,1)S(1)}, u32[]{:S(2)}, u32[]{:S(2)}) collective-permute-start(bf16[9,64,128]{2,1,0:T(8,128)(2,1)S(1)} %convert_element_type.262), channel_id=1, source_target_pairs={{0,16},{1,17},{2,18},{3,19},{4,20},{5,21},{6,22},{7,23},{8,24},{9,... | collective-permute-start | bytes 442376 | tf_op jit(solution)/shard_map/ppermute | solution.py:498
  14.6 9.8 %collective-permute-start.5 = (bf16[9,64,128]{2,1,0:T(8,128)(2,1)S(1)}, bf16[9,64,128]{2,1,0:T(8,128)(2,1)S(1)}, u32[]{:S(2)}, u32[]{:S(2)}) collective-permute-start(bf16[9,64,128]{2,1,0:T(8,128)(2,1)S(1)} %convert_element_type.262), channel_id=1, source_target_pairs={{0,24},{1,25},{2,26},{3,27},{4,28},{5,29},{6,30},{7,31},{8,16},{9,... | collective-permute-start | bytes 442376 | tf_op jit(solution)/shard_map/ppermute | solution.py:498
  24.5 15.8 %collective-permute-start.7 = (bf16[4,9,64,128]{3,2,1,0:T(8,128)(2,1)S(1)}, bf16[4,9,64,128]{3,2,1,0:T(8,128)(2,1)S(1)}, u32[]{:S(2)}, u32[]{:S(2)}) collective-permute-start(bf16[4,9,64,128]{3,2,1,0:T(8,128)(2,1)S(1)} %pad_maximum_fusion.1.refs_5_), channel_id=1, source_target_pairs={{0,4},{1,3},{2,6},{3,1},{4,0},{5,7},{6,2},{7,5},{8,12},{9,11},{10,... | collective-permute-start | bytes 1769480 | tf_op jit(solution)/shard_map/ppermute | solution.py:498
  26.1 14.3 %collective-permute-start.8 = (bf16[4,9,64,128]{3,2,1,0:T(8,128)(2,1)S(1)}, bf16[4,9,64,128]{3,2,1,0:T(8,128)(2,1)S(1)}, u32[]{:S(2)}, u32[]{:S(2)}) collective-permute-start(bf16[4,9,64,128]{3,2,1,0:T(8,128)(2,1)S(1)} %pad_maximum_fusion.1.refs_5_), channel_id=1, source_target_pairs={{0,2},{1,5},{2,0},{3,7},{4,6},{5,1},{6,4},{7,3},{8,10},{9,13},{10,... | collective-permute-start | bytes 1769480 | tf_op jit(solution)/shard_map/ppermute | solution.py:498
  28.0 12.0 %collective-permute-start.10 = (bf16[2,64,512]{2,1,0:T(8,128)(2,1)S(1)}, bf16[2,64,512]{2,1,0:T(8,128)(2,1)S(1)}, u32[]{:S(2)}, u32[]{:S(2)}) collective-permute-start(bf16[2,64,512]{2,1,0:T(8,128)(2,1)S(1)} %pad_maximum_fusion.6), channel_id=1, source_target_pairs={{0,16},{1,17},{2,18},{3,19},{4,20},{5,21},{6,22},{7,23},{8,24},{9,... | collective-permute-start | bytes 393224 | tf_op jit(solution)/shard_map/ppermute | solution.py:498
  40.3 16.1 %collective-permute-start.12 = (bf16[4,9,64,128]{3,2,1,0:T(8,128)(2,1)S(1)}, bf16[4,9,64,128]{3,2,1,0:T(8,128)(2,1)S(1)}, u32[]{:S(2)}, u32[]{:S(2)}) collective-permute-start(bf16[4,9,64,128]{3,2,1,0:T(8,128)(2,1)S(1)} %collective-permute-done.7.refs_6_), channel_id=1, source_target_pairs={{0,2},{1,5},{2,0},{3,7},{4,6},{5,1},{6,4},{7,3},{8,10},{9,13},{10,... | collective-permute-start | bytes 1769480 | tf_op jit(solution)/shard_map/ppermute | solution.py:498
  40.9 15.5 %collective-permute-start.13 = (bf16[4,2,64,512]{3,2,1,0:T(8,128)(2,1)S(1)}, bf16[4,2,64,512]{3,2,1,0:T(8,128)(2,1)S(1)}, u32[]{:S(2)}, u32[]{:S(2)}) collective-permute-start(bf16[4,2,64,512]{3,2,1,0:T(8,128)(2,1)S(1)} %pad_maximum_fusion.2.refs_8_), channel_id=1, source_target_pairs={{0,4},{1,5},{2,6},{3,7},{4,0},{5,1},{6,2},{7,3},{8,12},{9,13},{10,... | collective-permute-start | bytes 1572872 | tf_op jit(solution)/shard_map/ppermute | solution.py:498
  44.5 11.9 %collective-permute-start.15 = (bf16[2,64,512]{2,1,0:T(8,128)(2,1)S(1)}, bf16[2,64,512]{2,1,0:T(8,128)(2,1)S(1)}, u32[]{:S(2)}, u32[]{:S(2)}) collective-permute-start(bf16[2,64,512]{2,1,0:T(8,128)(2,1)S(1)} %pad_maximum_fusion.5), channel_id=1, source_target_pairs={{0,16},{1,17},{2,18},{3,19},{4,20},{5,21},{6,22},{7,23},{8,24},{9,... | collective-permute-start | bytes 393224 | tf_op jit(solution)/shard_map/ppermute | solution.py:498
  45.7 10.7 %collective-permute-start.16 = (bf16[2,64,512]{2,1,0:T(8,128)(2,1)S(1)}, bf16[2,64,512]{2,1,0:T(8,128)(2,1)S(1)}, u32[]{:S(2)}, u32[]{:S(2)}) collective-permute-start(bf16[2,64,512]{2,1,0:T(8,128)(2,1)S(1)} %pad_maximum_fusion.5), channel_id=1, source_target_pairs={{0,24},{1,25},{2,26},{3,27},{4,28},{5,29},{6,30},{7,31},{8,16},{9,... | collective-permute-start | bytes 393224 | tf_op jit(solution)/shard_map/ppermute | solution.py:498
  59.3 16.4 %collective-permute-start.22 = (bf16[4,2,64,512]{3,2,1,0:T(8,128)(2,1)S(1)}, bf16[4,2,64,512]{3,2,1,0:T(8,128)(2,1)S(1)}, u32[]{:S(2)}, u32[]{:S(2)}) collective-permute-start(bf16[4,2,64,512]{3,2,1,0:T(8,128)(2,1)S(1)} %pad_maximum_fusion.3.refs_12_), channel_id=1, source_target_pairs={{0,4},{1,5},{2,6},{3,7},{4,0},{5,1},{6,2},{7,3},{8,12},{9,13},{10,... | collective-permute-start | bytes 1572872 | tf_op jit(solution)/shard_map/ppermute | solution.py:498
  60.9 14.8 %collective-permute-start.23 = (bf16[4,2,64,512]{3,2,1,0:T(8,128)(2,1)S(1)}, bf16[4,2,64,512]{3,2,1,0:T(8,128)(2,1)S(1)}, u32[]{:S(2)}, u32[]{:S(2)}) collective-permute-start(bf16[4,2,64,512]{3,2,1,0:T(8,128)(2,1)S(1)} %pad_maximum_fusion.3.refs_12_), channel_id=1, source_target_pairs={{0,1},{1,0},{2,3},{3,2},{4,5},{5,4},{6,7},{7,6},{8,9},{9,8},{10,11... | collective-permute-start | bytes 1572872 | tf_op jit(solution)/shard_map/ppermute | solution.py:498
  61.2 14.5 %collective-permute-start.21 = (bf16[4,2,64,512]{3,2,1,0:T(8,128)(2,1)S(1)}, bf16[4,2,64,512]{3,2,1,0:T(8,128)(2,1)S(1)}, u32[]{:S(2)}, u32[]{:S(2)}) collective-permute-start(bf16[4,2,64,512]{3,2,1,0:T(8,128)(2,1)S(1)} %pad_maximum_fusion.2.refs_8_), channel_id=1, source_target_pairs={{0,1},{1,0},{2,3},{3,2},{4,5},{5,4},{6,7},{7,6},{8,9},{9,8},{10,11... | collective-permute-start | bytes 1572872 | tf_op jit(solution)/shard_map/ppermute | solution.py:498
  62.1 9.1 %collective-permute-start.24 = (bf16[1024,128]{1,0:T(8,128)(2,1)S(1)}, bf16[1024,128]{1,0:T(8,128)(2,1)S(1)}, u32[]{:S(2)}, u32[]{:S(2)}) collective-permute-start(bf16[1024,128]{1,0:T(8,128)(2,1)S(1)} %get-tuple-element.277), channel_id=1, source_target_pairs={{0,2},{1,3},{2,0},{3,1},{4,6},{5,7},{6,4},{7,5},{8,10},{9,11},{10,... | collective-permute-start | bytes 786440 | tf_op jit(solution)/shard_map/ppermute | solution.py:575
  62.9 12.8 %collective-permute-start.25 = (bf16[1024,128]{1,0:T(8,128)(2,1)S(1)}, bf16[1024,128]{1,0:T(8,128)(2,1)S(1)}, u32[]{:S(2)}, u32[]{:S(2)}) collective-permute-start(bf16[1024,128]{1,0:T(8,128)(2,1)S(1)} %get-tuple-element.276), channel_id=1, source_target_pairs={{0,3},{1,2},{2,1},{3,0},{4,7},{5,6},{6,5},{7,4},{8,11},{9,10},{10,... | collective-permute-start | bytes 786440 | tf_op jit(solution)/shard_map/ppermute | solution.py:575
  84.6 10.0 %collective-permute-start.29 = (bf16[1024,128]{1,0:T(8,128)(2,1)S(1)}, bf16[1024,128]{1,0:T(8,128)(2,1)S(1)}, u32[]{:S(2)}, u32[]{:S(2)}) collective-permute-start(bf16[1024,128]{1,0:T(8,128)(2,1)S(1)} %get-tuple-element.275), channel_id=1, source_target_pairs={{0,1},{1,0},{2,3},{3,2},{4,5},{5,4},{6,7},{7,6},{8,9},{9,8},{10,11... | collective-permute-start | bytes 786440 | tf_op jit(solution)/shard_map/ppermute | solution.py:633
  85.1 9.6 %collective-permute-start.30 = (bf16[1024,128]{1,0:T(8,128)(2,1)S(1)}, bf16[1024,128]{1,0:T(8,128)(2,1)S(1)}, u32[]{:S(2)}, u32[]{:S(2)}) collective-permute-start(bf16[1024,128]{1,0:T(8,128)(2,1)S(1)} %get-tuple-element.274), channel_id=1, source_target_pairs={{0,2},{1,3},{2,0},{3,1},{4,6},{5,7},{6,4},{7,5},{8,10},{9,11},{10,... | collective-permute-start | bytes 786440 | tf_op jit(solution)/shard_map/ppermute | solution.py:633
  102.8 14.8 %collective-permute-start.33 = (bf16[2,4,2,64,512]{4,3,2,1,0:T(8,128)(2,1)S(1)}, bf16[2,4,2,64,512]{4,3,2,1,0:T(8,128)(2,1)S(1)}, u32[]{:S(2)}, u32[]{:S(2)}) collective-permute-start(bf16[2,4,2,64,512]{4,3,2,1,0:T(8,128)(2,1)S(1)} %fusion.2), channel_id=1, source_target_pairs={{0,2},{1,5},{2,0},{3,7},{4,6},{5,1},{6,4},{7,3},{8,10},{9,13},{10,... | collective-permute-start | bytes 3145736 | tf_op jit(solution)/shard_map/ppermute | solution.py:498
  118.0 9.6 %collective-permute-start.35 = (bf16[4,2,64,512]{3,2,1,0:T(8,128)(2,1)S(1)}, bf16[4,2,64,512]{3,2,1,0:T(8,128)(2,1)S(1)}, u32[]{:S(2)}, u32[]{:S(2)}) collective-permute-start(bf16[4,2,64,512]{3,2,1,0:T(8,128)(2,1)S(1)} %fusion.3), channel_id=1, source_target_pairs={{0,4},{1,3},{2,6},{3,1},{4,0},{5,7},{6,2},{7,5},{8,12},{9,11},{10,... | collective-permute-start | bytes 1572872 | tf_op jit(solution)/shard_map/ppermute | solution.py:498
  127.5 21.8 %collective-permute-start.36 = (bf16[2,4,9,64,128]{4,3,2,1,0:T(8,128)(2,1)S(1)}, bf16[2,4,9,64,128]{4,3,2,1,0:T(8,128)(2,1)S(1)}, u32[]{:S(2)}, u32[]{:S(2)}) collective-permute-start(bf16[2,4,9,64,128]{4,3,2,1,0:T(8,128)(2,1)S(1)} %fusion), channel_id=1, source_target_pairs={{0,2},{1,5},{2,0},{3,7},{4,6},{5,1},{6,4},{7,3},{8,10},{9,13},{10,... | collective-permute-start | bytes 3538952 | tf_op jit(solution)/shard_map/ppermute | solution.py:498
  128.6 12.2 %collective-permute-start.37 = (bf16[2,64,512]{2,1,0:T(8,128)(2,1)S(1)}, bf16[2,64,512]{2,1,0:T(8,128)(2,1)S(1)}, u32[]{:S(2)}, u32[]{:S(2)}) collective-permute-start(bf16[2,64,512]{2,1,0:T(8,128)(2,1)S(1)} %get-tuple-element.258), channel_id=1, source_target_pairs={{0,8},{1,9},{2,10},{3,11},{4,12},{5,13},{6,14},{7,15},{8,0},{9,1},... | collective-permute-start | bytes 393224 | tf_op jit(solution)/shard_map/ppermute | solution.py:498
  136.4 12.8 %collective-permute-start.38 = (bf16[2,64,512]{2,1,0:T(8,128)(2,1)S(1)}, bf16[2,64,512]{2,1,0:T(8,128)(2,1)S(1)}, u32[]{:S(2)}, u32[]{:S(2)}) collective-permute-start(bf16[2,64,512]{2,1,0:T(8,128)(2,1)S(1)} %get-tuple-element.260), channel_id=1, source_target_pairs={{0,16},{1,17},{2,18},{3,19},{4,20},{5,21},{6,22},{7,23},{8,24},{9,... | collective-permute-start | bytes 393224 | tf_op jit(solution)/shard_map/ppermute | solution.py:498
  138.3 10.9 %collective-permute-start.39 = (bf16[2,64,512]{2,1,0:T(8,128)(2,1)S(1)}, bf16[2,64,512]{2,1,0:T(8,128)(2,1)S(1)}, u32[]{:S(2)}, u32[]{:S(2)}) collective-permute-start(bf16[2,64,512]{2,1,0:T(8,128)(2,1)S(1)} %get-tuple-element.259), channel_id=1, source_target_pairs={{0,24},{1,25},{2,26},{3,27},{4,28},{5,29},{6,30},{7,31},{8,16},{9,... | collective-permute-start | bytes 393224 | tf_op jit(solution)/shard_map/ppermute | solution.py:498
  149.6 9.9 %collective-permute-start.40 = (bf16[4,9,64,128]{3,2,1,0:T(8,128)(2,1)S(1)}, bf16[4,9,64,128]{3,2,1,0:T(8,128)(2,1)S(1)}, u32[]{:S(2)}, u32[]{:S(2)}) collective-permute-start(bf16[4,9,64,128]{3,2,1,0:T(8,128)(2,1)S(1)} %fusion.1), channel_id=1, source_target_pairs={{0,4},{1,3},{2,6},{3,1},{4,0},{5,7},{6,2},{7,5},{8,12},{9,11},{10,... | collective-permute-start | bytes 1769480 | tf_op jit(solution)/shard_map/ppermute | solution.py:498
  162.1 15.8 %collective-permute-start.44 = (bf16[1024,128]{1,0:T(8,128)(2,1)S(1)}, bf16[1024,128]{1,0:T(8,128)(2,1)S(1)}, u32[]{:S(2)}, u32[]{:S(2)}) collective-permute-start(bf16[1024,128]{1,0:T(8,128)(2,1)S(1)} %get-tuple-element.271), channel_id=1, source_target_pairs={{0,1},{1,0},{2,3},{3,2},{4,5},{5,4},{6,7},{7,6},{8,9},{9,8},{10,11... | collective-permute-start | bytes 786440 | tf_op jit(solution)/shard_map/ppermute | solution.py:527
  162.1 15.8 %collective-permute-start.45 = (bf16[1024,128]{1,0:T(8,128)(2,1)S(1)}, bf16[1024,128]{1,0:T(8,128)(2,1)S(1)}, u32[]{:S(2)}, u32[]{:S(2)}) collective-permute-start(bf16[1024,128]{1,0:T(8,128)(2,1)S(1)} %get-tuple-element.270), channel_id=1, source_target_pairs={{0,2},{1,3},{2,0},{3,1},{4,6},{5,7},{6,4},{7,5},{8,10},{9,11},{10,... | collective-permute-start | bytes 786440 | tf_op jit(solution)/shard_map/ppermute | solution.py:527
  163.3 14.7 %collective-permute-start.46 = (bf16[1024,128]{1,0:T(8,128)(2,1)S(1)}, bf16[1024,128]{1,0:T(8,128)(2,1)S(1)}, u32[]{:S(2)}, u32[]{:S(2)}) collective-permute-start(bf16[1024,128]{1,0:T(8,128)(2,1)S(1)} %get-tuple-element.269), channel_id=1, source_target_pairs={{0,3},{1,2},{2,1},{3,0},{4,7},{5,6},{6,5},{7,4},{8,11},{9,10},{10,... | collective-permute-start | bytes 786440 | tf_op jit(solution)/shard_map/ppermute | solution.py:527
  164.0 13.9 %collective-permute-start.42 = (bf16[9,64,128]{2,1,0:T(8,128)(2,1)S(1)}, bf16[9,64,128]{2,1,0:T(8,128)(2,1)S(1)}, u32[]{:S(2)}, u32[]{:S(2)}) collective-permute-start(bf16[9,64,128]{2,1,0:T(8,128)(2,1)S(1)} %get-tuple-element.255), channel_id=1, source_target_pairs={{0,16},{1,17},{2,18},{3,19},{4,20},{5,21},{6,22},{7,23},{8,24},{9,... | collective-permute-start | bytes 442376 | tf_op jit(solution)/shard_map/ppermute | solution.py:498
  166.1 11.8 %collective-permute-start.43 = (bf16[9,64,128]{2,1,0:T(8,128)(2,1)S(1)}, bf16[9,64,128]{2,1,0:T(8,128)(2,1)S(1)}, u32[]{:S(2)}, u32[]{:S(2)}) collective-permute-start(bf16[9,64,128]{2,1,0:T(8,128)(2,1)S(1)} %get-tuple-element.254), channel_id=1, source_target_pairs={{0,24},{1,25},{2,26},{3,27},{4,28},{5,29},{6,30},{7,31},{8,16},{9,... | collective-permute-start | bytes 442376 | tf_op jit(solution)/shard_map/ppermute | solution.py:498
  (41 other events, 293.2 us)
